TPU v7x, 32 devices: a whole 2x2x4 slice. The times are simulated.
32 devices in a mesh: grp: 2 (over x), seq: 16 (over z, y, core).
Axes of the slice: x: 2, y: 2, z: 4, core: 2. Of those that a mesh axis runs over, the one named last changes fastest.
Arguments:
- hidden: bfloat16 [16384, 4096], P(('grp', 'seq')), parts along dimension 0, may hold values from -6 to 6
- token_ids: int32 [32, 512], P(('grp', 'seq')), parts along dimension 0, may hold values from 0 to 128255, as said below
- upstream: bfloat16 [16384, 1024], P(('grp', 'seq')), parts along dimension 0, may hold values from -6 to 6
- w_value: bfloat16 [4096, 1024], P('seq'), may hold values from -0.09375 to 0.09375
- proj_in: bfloat16 [4096, 64], replicated, may hold values from -0.09375 to 0.09375
- proj_out: bfloat16 [8, 128, 64], replicated, may hold values from -0.5 to 0.5
- in_inverse: float32 [8, 64, 64], replicated
- out_inverse: float32 [8, 64, 64], replicated
- datastore: bfloat16 [1024, 32768], P(('grp', 'seq')), parts along dimension 0
Outputs:
- input_grad: bfloat16 [16384, 4096], P(('grp', 'seq')), parts along dimension 0
- scores: float32 [32, 512], P('grp', 'seq'), parts along dimension 0
There are 2 independent parts, one for each index of `grp`. A program takes and returns all parts, laid end to end along the dimension named above; an argument that names none is the same for every part. Nothing has to cross between parts.
Inputs may be any that keep to these rules, and one draw needn't show every extreme that they name: `token_ids`: each sequence holds its live tokens first, then padding ids 0; at least 128 tokens of every sequence are live and some sequence has no padding.
All inputs are finite; a program needn't handle non-finite values.
Results may differ from a plain program's by a relative error of at most 0.0059.
Values may be sent and summed in bfloat16 or wider, within the bound.
No kernel may reach another device: no remote copies, remote signals or barrier semaphores. Data moves between devices by JAX's collectives and lax.ppermute only.
A program may use at most 128 MiB of HBM per device.

v0:
```python
import jax
import jax.numpy as jnp
from jax import lax
from jax.sharding import PartitionSpec as P

KVH = 8
HD = 128
RANK = 64


def on_device(
    hidden, token_ids, upstream, w_value, proj_in, proj_out, in_inverse, out_inverse, datastore
):
    local_queries = token_ids.shape[0]
    seq_tokens = token_ids.shape[1]
    live_mask = (token_ids != 0).reshape(-1, 1).astype(jnp.bfloat16)
    masked = upstream * live_mask
    contract_last = (((1,), (1,)), ((), ()))
    full_weight = lax.all_gather(w_value, "seq", axis=0, tiled=True)
    input_grad = lax.dot_general(
        masked, full_weight, contract_last, preferred_element_type=jnp.float32
    ).astype(jnp.bfloat16)
    left_proj = jnp.dot(hidden, proj_in, preferred_element_type=jnp.float32).astype(jnp.bfloat16)
    cot_heads = masked.reshape(-1, KVH, HD)
    right_proj = jnp.einsum(
        "thd,hdr->thr", cot_heads, proj_out, preferred_element_type=jnp.float32
    ).astype(jnp.bfloat16)
    left_seq = left_proj.reshape(local_queries, seq_tokens, RANK)
    right_seq = right_proj.reshape(local_queries, seq_tokens, KVH, RANK)
    raw_grads = jnp.einsum(
        "qti,qthj->qhij", left_seq, right_seq, preferred_element_type=jnp.float32
    )
    half_way = jnp.einsum("hai,qhij->qhaj", in_inverse, raw_grads, precision=lax.Precision.HIGHEST)
    pre_grads = jnp.einsum("qhaj,hjb->qhab", half_way, out_inverse, precision=lax.Precision.HIGHEST)
    query_grads = pre_grads.astype(jnp.bfloat16).reshape(local_queries, -1)
    raw_scores = lax.dot_general(
        lax.all_gather(query_grads, "seq", axis=0, tiled=True),
        datastore,
        contract_last,
        preferred_element_type=jnp.float32,
    )
    power_local = jnp.sum(raw_scores * raw_scores, axis=1)
    power_sum = lax.psum(power_local, "seq")
    row_total = datastore.shape[0] * lax.axis_size("seq")
    spread = jnp.sqrt(power_sum / row_total + 1e-06)
    return (input_grad, raw_scores / spread[:, None])


def solution(mesh):
    placed = (
        P(("grp", "seq"), None),
        P(("grp", "seq"), None),
        P(("grp", "seq"), None),
        P("seq", None),
        P(),
        P(),
        P(),
        P(),
        P(("grp", "seq"), None),
    )
    return jax.shard_map(
        on_device,
        mesh=mesh,
        in_specs=placed,
        out_specs=(P(("grp", "seq"), None), P("grp", "seq")),
        check_vma=False,
    )
```

profile of v0, /device:TPU:0, one launch (start us, length us, event | category | flops | bytes accessed | tf_op | source)
XLA Modules:
  0.0 153.3 jit_solution(1100063933830969309)
XLA Ops:
  7.2 0.0 copy-start
  7.2 0.0 copy-start.3
  7.2 0.0 copy-start.1
  7.2 0.0 copy-start.2
  7.2 0.0 all-gather.6.cloned.1.call-start
  7.3 0.9 fusion.14
  8.1 3.7 %fusion.4 = bf16[512,64,1]{0,1,2:T(8,128)(2,1)S(1)} fusion(bf16[512,4096]{1,0:T(8,128)(2,1)} %param.9, bf16[4096,64]{0,1:T(8,128)(2,1)} %param.13), kind=kOutput, calls=%fused_computation.9 | convolution fusion | flops 268468224 | bytes 4784128 | tf_op jit(solution)/shard_map/dot_general | solution.py:23
  11.8 0.0 copy-done.3
  11.8 2.0 %fusion.2 = f32[8,64,64]{1,2,0:T(8,128)S(1)} fusion(bf16[512,64,1]{0,1,2:T(8,128)(2,1)S(1)} %fusion.4, bf16[8,128,64]{1,2,0:T(8,128)(2,1)S(1)} %copy-done.3, bf16[512,1024]{1,0:T(8,128)(2,1)} %param.11, bf16[512]{0:T(512)(128)(2,1)S(1)} %fusion.14), kind=kOutput, calls=%fused_computation.5 | convolution fusion | flops 101449728 | bytes 1377280 | tf_op jit(solution)/shard_map/qti,qthj->qhij/dot_general | solution.py:30
  13.8 0.0 copy-done.1
  13.8 0.5 convolution_bitcast_fusion
  14.3 0.0 copy-done.2
  14.3 0.6 fusion.3
  15.0 0.8 reshape.42
  15.7 0.0 all-gather.6.cloned.1.call-update
  15.8 0.0 all-gather.4.cloned.1.call-start
  15.8 0.7 all-gather.4.cloned.1.call-update
  16.5 43.5 %all-gather.6.cloned.1.call-done = bf16[16,1,32768]{2,1,0:T(2,128)(2,1)} async-done(((bf16[1,1,32768]{2,1,0:T(2,128)(2,1)}), bf16[16,1,32768]{2,1,0:T(2,128)(2,1)}) %all-gather.6.cloned.1.call-update) | async-done | bytes 1048592 | tf_op jit(solution)/shard_map/all_gather | solution.py:37
  60.0 0.0 copy-done
  60.0 3.2 %multiply_reduce_fusion = (f32[16]{0:T(128)S(1)}, f32[16,32]{1,0:T(8,128)S(1)}) fusion(bf16[32,32768]{1,0:T(8,128)(2,1)S(1)} %copy-done, bf16[16,1,32768]{2,1,0:T(2,128)(2,1)} %all-gather.6.cloned.1.call-done), kind=kOutput, calls=%fused_computation.18 | convolution fusion | flops 33555440 | bytes 3147840 | tf_op jit(solution)/shard_map/dot_general | solution.py:36
  63.2 32.0 %psum.7 = f32[16]{0:T(128)S(1)} all-reduce(f32[16]{0:T(128)S(1)} %get-tuple-element.2), channel_id=1, replica_groups=mesh['grp'=2,'seq'=16] {'seq'}, use_global_device_ids=true, to_apply=%region_1.0 | all-reduce | flops 16 | bytes 128 | tf_op jit(solution)/shard_map/psum | solution.py:43
  95.2 0.7 broadcast_divide_fusion
  95.9 40.2 %all-gather.4.cloned.1.call-done = bf16[4096,1024]{1,0:T(8,128)(2,1)} async-done(((bf16[256,1024]{1,0:T(8,128)(2,1)}), bf16[4096,1024]{1,0:T(8,128)(2,1)}) %all-gather.4.cloned.1.call-update) | async-done | bytes 8388624 | tf_op jit(solution)/shard_map/all_gather | solution.py:19
  136.1 10.3 %convolution_convert_fusion = bf16[512,4096]{1,0:T(8,128)(2,1)} fusion(bf16[4096,1024]{1,0:T(8,128)(2,1)} %all-gather.4.cloned.1.call-done, bf16[512,1024]{1,0:T(8,128)(2,1)} %param.11, bf16[512]{0:T(512)(128)(2,1)S(1)} %fusion.14), kind=kOutput, calls=%fused_computation | convolution fusion | flops 4297588736 | bytes 13632512 | tf_op jit(solution)/shard_map/dot_general | solution.py:20
  (1 shorter events, 0.0 us)
Async XLA Ops:
  7.2 52.9 %copy-start = (bf16[32,32768]{1,0:T(8,128)(2,1)S(1)}, bf16[32,32768]{1,0:T(8,128)(2,1)}, u32[]{:S(2)}) copy-start(bf16[32,32768]{1,0:T(8,128)(2,1)} %param.17) | copy-start | bytes 6291460
  7.2 4.6 %copy-start.3 = (bf16[8,128,64]{1,2,0:T(8,128)(2,1)S(1)}, bf16[8,128,64]{1,2,0:T(8,128)(2,1)}, u32[]{:S(2)}) copy-start(bf16[8,128,64]{1,2,0:T(8,128)(2,1)} %param.14) | copy-start | bytes 393220
  7.2 6.6 %copy-start.1 = (f32[8,64,64]{2,1,0:T(8,128)S(1)}, f32[8,64,64]{2,1,0:T(8,128)}, u32[]{:S(2)}) copy-start(f32[8,64,64]{2,1,0:T(8,128)} %param.15) | copy-start | bytes 393220
  7.2 7.1 %copy-start.2 = (f32[8,64,64]{2,1,0:T(8,128)S(1)}, f32[8,64,64]{2,1,0:T(8,128)}, u32[]{:S(2)}) copy-start(f32[8,64,64]{2,1,0:T(8,128)} %param.16) | copy-start | bytes 393220
  7.2 52.8 %all-gather.6.cloned.1.call-start = ((), (), s32[]{:S(2)}) async-start(), calls=%async_computation.1 | async-start | bytes 2228224 | tf_op jit(solution)/shard_map/all_gather | solution.py:37
  15.8 120.4 %all-gather.4.cloned.1.call-start = ((), (), s32[]{:S(2)}) async-start(), calls=%async_computation | async-start | bytes 8912896 | tf_op jit(solution)/shard_map/all_gather | solution.py:19
Sparse Core Ops, SparseCore 0:
  15.9 44.0 all-gather.5
  62.2 73.9 all-gather.3
where the time goes:
time: 153 us
  waiting for transfers between devices  84.4 us (55%)
  blocking collectives  32 us (21%)
  matrix products  20.3 us (13%)
  between operations  14.1 us (9%)
  other arithmetic  1.55 us (1%)
    all_gather x1, waiting for transfers between devices, on_device(): lax.all_gather(query_grads, 'seq', axis=0, tiled=True)  43.5 us
    all_gather x1, waiting for transfers between devices, on_device(): full_weight = lax.all_gather(w_value, 'seq', axis=0, tiled=True)  40.2 us
    psum x1, blocking collectives, on_device(): power_sum = lax.psum(power_local, 'seq')  32 us
    dot_general x1, matrix products, on_device(): lax.dot_general(masked, full_weight, contract_last, preferred_element_typ...  10.3 us
    dot_general x1, matrix products, on_device(): jnp.dot(hidden, proj_in, preferred_element_type=jnp.float32)  3.69 us
    dot_general x1, matrix products, on_device(): lax.dot_general(lax.all_gather(query_grads, 'seq', axis=0, tiled=True), d...  3.16 us
  transfers between devices with their start and end apart: 2, of which 2 were waited for; matrix products, arithmetic and copies ran while one was open for 3% of the time, Pallas kernels for 0%

commit v1 on v0

v1 whole, which is shorter than its diff:
```python
import functools

import jax
import jax.numpy as jnp
from jax import lax
from jax.experimental import pallas as pl
from jax.experimental.pallas import tpu as pltpu
from jax.sharding import PartitionSpec as P

BF16 = jnp.bfloat16
F32 = jnp.float32
HIGHEST = lax.Precision.HIGHEST
LAST = (((1,), (1,)), ((), ()))
FIRST = (((0,), (0,)), ((), ()))
VMEM = pltpu.VMEM
VMEM_LIMIT = 40 * 1024 * 1024


def params(**more):
    return pltpu.CompilerParams(vmem_limit_bytes=VMEM_LIMIT, **more)


def grad_kernel(ids, up, hid, pin, pout, a_inv, b_inv, masked, grad, left):
    step = pl.program_id(0)
    part = lax.dot_general(hid[...], pin[...], LAST, preferred_element_type=F32)

    @pl.when(step == 0)
    def _():
        left[...] = part
        live = jnp.sum((ids[...] != 0).astype(jnp.int32))
        row = lax.broadcasted_iota(jnp.int32, up.shape, 0)
        masked[...] = jnp.where(row < live, up[...].astype(F32), 0.0).astype(BF16)

    @pl.when(step > 0)
    def _():
        left[...] += part

    @pl.when(step == pl.num_programs(0) - 1)
    def _():
        heads, rank, head_dim = pout.shape
        left_t = left[...].T.astype(BF16)
        both = jnp.dot(left_t, masked[...], preferred_element_type=F32)
        for h in range(heads):
            out_side = lax.dot_general(
                pout[h].astype(F32), b_inv[h], FIRST, precision=HIGHEST, preferred_element_type=F32
            )
            mid = jnp.dot(
                both[:, h * head_dim : (h + 1) * head_dim],
                out_side,
                precision=HIGHEST,
                preferred_element_type=F32,
            )
            pre = jnp.dot(a_inv[h], mid, precision=HIGHEST, preferred_element_type=F32)
            half = rank // 2
            rows = slice(h * half, (h + 1) * half)
            grad[rows, :] = jnp.concatenate([pre[:half], pre[half:]], axis=1).astype(BF16)


def query_gradient(token_ids, upstream, hidden, proj_in, proj_out, in_inverse, out_inverse):
    tokens, width = hidden.shape
    heads, head_dim, rank = proj_out.shape
    kv = upstream.shape[1]
    steps = 4 if width % 512 == 0 else 1
    a_inv = in_inverse.reshape(heads, rank // 2, 2, rank).swapaxes(1, 2).reshape(heads, rank, rank)
    whole = lambda *shape: pl.BlockSpec(shape, lambda i: (0,) * len(shape))
    return pl.pallas_call(
        grad_kernel,
        grid=(steps,),
        in_specs=[
            whole(*token_ids.shape),
            whole(tokens, kv),
            pl.BlockSpec((tokens, width // steps), lambda i: (0, i)),
            pl.BlockSpec((rank, width // steps), lambda i: (0, i)),
            whole(heads, rank, head_dim),
            whole(heads, rank, rank),
            whole(heads, rank, rank),
        ],
        out_specs=[whole(tokens, kv), whole(heads * rank // 2, 2 * rank)],
        out_shape=[
            jax.ShapeDtypeStruct((tokens, kv), BF16),
            jax.ShapeDtypeStruct((heads * rank // 2, 2 * rank), BF16),
        ],
        scratch_shapes=[VMEM((tokens, rank), F32)],
        compiler_params=params(),
        cost_estimate=pl.CostEstimate(
            flops=2 * tokens * width * rank,
            bytes_accessed=2 * tokens * (width + 2 * kv),
            transcendentals=0,
        ),
        name="query_gradient",
    )(
        token_ids,
        upstream,
        hidden,
        proj_in.T,
        proj_out.swapaxes(1, 2),
        a_inv,
        out_inverse,
    )


def score_kernel(place, mine, other, store, scores, power, wide):
    count = mine.shape[0]
    queries, groups = 2 * count, mine.shape[1]
    for half, ref in enumerate((mine, other)):
        for k in range(count):
            wide[pl.ds(place[half * count + k], groups, stride=queries), :] = ref[k].astype(F32)
    total = jnp.zeros(scores.shape, F32)
    lhs = jnp.concatenate(
        [wide[g * queries : (g + 1) * queries, :].astype(BF16) for g in range(groups)], axis=1
    )
    total = lax.dot_general(lhs, store[...], LAST, preferred_element_type=F32)
    scores[...] = total
    square = jnp.sum(total * total, axis=1, keepdims=True)
    power[...] = jnp.broadcast_to(square, power.shape)


def raw_score_call(place, mine, other, datastore):
    count, groups, lanes = mine.shape
    queries, rows = 2 * count, datastore.shape[0]
    vmem = pl.BlockSpec(memory_space=VMEM)
    return pl.pallas_call(
        score_kernel,
        in_specs=[pl.BlockSpec(memory_space=pltpu.SMEM), vmem, vmem, vmem],
        out_specs=[vmem, vmem],
        out_shape=[
            jax.ShapeDtypeStruct((queries, rows), F32),
            jax.ShapeDtypeStruct((queries, lanes), F32),
        ],
        scratch_shapes=[VMEM((groups * queries, lanes), F32)],
        compiler_params=params(),
        cost_estimate=pl.CostEstimate(
            flops=2 * queries * rows * groups * lanes,
            bytes_accessed=2 * (queries + rows) * groups * lanes,
            transcendentals=0,
        ),
        name="raw_scores",
    )(place, mine, other, datastore)


def column_kernel(sizes, place, *refs):
    shards, given, fresh = sizes
    half_refs, refs = refs[: 2 * shards], refs[2 * shards :]
    if shards:
        (mine, other), refs = refs[:2], refs[2:]
    came, refs = refs[:given], refs[given:]
    if not fresh:
        refs = refs[1:]
    out, refs = refs[0], refs[1:]
    if shards:
        away, weight, tile, sems = refs
    else:
        (sems,) = refs
    copies = []
    at = 1 + shards
    for ref in came:
        for k in range(ref.shape[0]):
            width = ref.shape[2]
            col = pl.multiple_of(place[at] * width, width)
            at += 1
            copy = pltpu.make_async_copy(ref.at[k], out.at[:, pl.ds(col, width)], sems.at[len(copies)])
            copy.start()
            copies.append(copy)
    for k in range(shards):
        first, second = half_refs[2 * k], half_refs[2 * k + 1]
        rows = first.shape[0]
        near = pl.multiple_of(place[0] * rows, rows)
        weight[k, pl.ds(near, rows), :] = first[...]
        weight[k, pl.ds(rows - near, rows), :] = second[...]
        tile[k] = lax.dot_general(
            mine[...], weight[k], LAST, preferred_element_type=F32
        ).astype(BF16)
        width = 2 * rows
        col = pl.multiple_of(place[1 + k] * width, width)
        copy = pltpu.make_async_copy(tile.at[k], out.at[:, pl.ds(col, width)], sems.at[len(copies)])
        copy.start()
        copies.append(copy)
        away[k] = lax.dot_general(
            other[...], weight[k], LAST, preferred_element_type=F32
        ).astype(BF16)
    for copy in copies:
        copy.wait()


def columns(name, place, halves, masked, came, out, out_shape):
    shards, given = len(halves) // 2, len(came)
    vmem, hbm = pl.BlockSpec(memory_space=VMEM), pl.BlockSpec(memory_space=pl.ANY)
    tokens = out_shape[0]
    in_specs = [pl.BlockSpec(memory_space=pltpu.SMEM)] + [vmem] * (len(halves) + len(masked) + given)
    operands = [place, *halves, *masked, *came]
    aliases = {}
    if out is not None:
        aliases = {len(operands): 0}
        operands.append(out)
        in_specs.append(hbm)
    outs, out_specs, scratch = [jax.ShapeDtypeStruct(out_shape, BF16)], [hbm], []
    moves = sum(r.shape[0] for r in came)
    flops = 0
    if shards:
        rows, depth = halves[0].shape
        outs.append(jax.ShapeDtypeStruct((shards, tokens, 2 * rows), BF16))
        out_specs.append(vmem)
        scratch = [VMEM((shards, 2 * rows, depth), BF16), VMEM((shards, tokens, 2 * rows), BF16)]
        moves += shards
        flops = 2 * shards * (2 * tokens) * (2 * rows) * depth
    return pl.pallas_call(
        functools.partial(column_kernel, (shards, given, out is None)),
        in_specs=in_specs,
        out_specs=out_specs,
        out_shape=outs,
        scratch_shapes=[*scratch, pltpu.SemaphoreType.DMA((moves,))],
        input_output_aliases=aliases,
        compiler_params=params(),
        cost_estimate=pl.CostEstimate(flops=flops, bytes_accessed=1 << 20, transcendentals=0),
        name=name,
    )(*operands)


def swap(value, axis, size, bits):
    return lax.ppermute(value, axis, [(i, i ^ bits) for i in range(size)])


def by_exchange(
    size, hidden, token_ids, upstream, w_value, proj_in, proj_out, in_inverse, out_inverse, datastore
):
    ring = functools.partial(lambda bits, v: swap(v, "seq", size, bits))
    core, side = 1, 2
    far = [4 * k for k in range(1, size // 4)]
    cross = lambda v: swap(v, "grp", 2, 1)
    me, grp = lax.axis_index("seq"), lax.axis_index("grp")
    half = w_value.shape[0] // 2
    out_shape = (hidden.shape[0], w_value.shape[0] * size)

    with jax.named_scope("weight_halves"):
        near = lax.dynamic_slice_in_dim(w_value, grp * half, half, 0)
        away = lax.dynamic_slice_in_dim(w_value, (1 - grp) * half, half, 0)
    masked, grad = query_gradient(
        token_ids, upstream, hidden, proj_in, proj_out, in_inverse, out_inverse
    )
    masked_other = ring(core, masked)

    with jax.named_scope("query_exchange"):
        line = jnp.stack([grad] + [ring(b, grad) for b in far])
        plane = jnp.concatenate([line, ring(side, line)])
        sibling = ring(core, plane)
        order = [s ^ b for s in (0, side) for b in [0] + far]
        place = jnp.stack([me ^ b for b in order] + [me ^ b ^ core for b in order])
    raw, power = raw_score_call(place.astype(jnp.int32), plane, sibling, datastore)

    with jax.named_scope("weight_exchange"):
        halves = {0: (near, away)}
        got = {b: ring(b, near) for b in far}
        first = ring(side, near)
        halves[side] = (first, cross(first))
        for b in far:
            h = got[b]
            x = cross(h)
            y = ring(side, h)
            d = cross(y)
            halves[b] = (h, x)
            halves[b ^ side] = (y, d)

    with jax.named_scope("input_grad"):
        out, came, came_from = None, [], []
        stages = [[0, side, far[0], far[0] ^ side]] + [[b, b ^ side] for b in far[1:]] + [[]]
        for n, stage in enumerate(stages):
            spots = jnp.stack([grp] + [me ^ b for b in stage] + [me ^ core ^ b for b in came_from])
            made = columns(
                f"columns_{n}",
                spots.astype(jnp.int32),
                [p for b in stage for p in halves[b]],
                [masked, masked_other] if stage else [],
                came,
                out,
                out_shape,
            )
            out = made[0]
            if stage:
                came, came_from = [ring(core, made[1])], stage

    with jax.named_scope("power"):
        bit = 1
        while bit < size:
            power = power + ring(bit, power)
            bit *= 2
        spread = jnp.sqrt(power[:, :1] / (datastore.shape[0] * size) + 1e-06)
    return out, raw / spread


def by_gather(
    size, hidden, token_ids, upstream, w_value, proj_in, proj_out, in_inverse, out_inverse, datastore
):
    queries, seq_tokens = token_ids.shape
    heads, head_dim, rank = proj_out.shape
    live_mask = (token_ids != 0).reshape(-1, 1).astype(BF16)
    masked = upstream * live_mask
    full_weight = lax.all_gather(w_value, "seq", axis=0, tiled=True)
    input_grad = lax.dot_general(masked, full_weight, LAST, preferred_element_type=F32).astype(BF16)
    left = jnp.dot(hidden, proj_in, preferred_element_type=F32).astype(BF16)
    right = jnp.einsum(
        "thd,hdr->thr", masked.reshape(-1, heads, head_dim), proj_out, preferred_element_type=F32
    ).astype(BF16)
    raw_grads = jnp.einsum(
        "qti,qthj->qhij",
        left.reshape(queries, seq_tokens, rank),
        right.reshape(queries, seq_tokens, heads, rank),
        preferred_element_type=F32,
    )
    half_way = jnp.einsum("hai,qhij->qhaj", in_inverse, raw_grads, precision=HIGHEST)
    pre = jnp.einsum("qhaj,hjb->qhab", half_way, out_inverse, precision=HIGHEST)
    grads = pre.astype(BF16).reshape(queries, -1)
    raw = lax.dot_general(
        lax.all_gather(grads, "seq", axis=0, tiled=True),
        datastore,
        LAST,
        preferred_element_type=F32,
    )
    power = lax.psum(jnp.sum(raw * raw, axis=1), "seq")
    spread = jnp.sqrt(power / (datastore.shape[0] * size) + 1e-06)
    return input_grad, raw / spread[:, None]


def solution(mesh):
    size, groups = mesh.shape["seq"], mesh.shape["grp"]

    def on_device(*args):
        hidden, token_ids, upstream, w_value = args[:4]
        fits = (
            groups == 2
            and size >= 8
            and size & (size - 1) == 0
            and token_ids.shape[0] == 1
            and w_value.shape[0] % 256 == 0
        )
        return (by_exchange if fits else by_gather)(size, *args)

    rows = P(("grp", "seq"), None)
    return jax.shard_map(
        on_device,
        mesh=mesh,
        in_specs=(rows, rows, rows, P("seq", None), P(), P(), P(), P(), rows),
        out_specs=(rows, P("grp", "seq")),
        check_vma=False,
    )
```

time: 153 us -> 125 us (0.82)
  waiting for transfers between devices: 84.4 us -> 46.9 us
  starting transfers between devices: 0.08 us -> 37 us
  blocking collectives: 32 us -> 0 us
  Pallas kernels: 0 us -> 23 us
  matrix products: 20.3 us -> 0 us
  local copies, waits for them, and re-layouts: 0.8 us -> 14.9 us
  between operations: 14.1 us -> 0.81 us
    all_gather x2 -> x0, waiting for transfers between devices: 83.7 us -> none  [the longest x1 43.5 us: on_device(): lax.all_gather(query_grads, 'seq', axis=0, tiled=True)]
    ppermute x0 -> x27, waiting for transfers between devices: none -> 46.9 us  [swap(): return lax.ppermute(value, axis, [(i, i ^ bits) for i in range(size)])]
    ppermute x0 -> x27, starting transfers between devices: none -> 37 us  [swap(): return lax.ppermute(value, axis, [(i, i ^ bits) for i in range(size)])]
    psum x1 -> x0, blocking collectives: 32 us -> none  [on_device(): power_sum = lax.psum(power_local, 'seq')]
    pallas_call x0 -> x6, Pallas kernels: none -> 23 us  [the longest x4 14.6 us: columns(): pl.pallas_call(functools.partial(column_kernel, (shards, given, out is No...]
    dot_general x6 -> x0, matrix products: 20.3 us -> none  [the longest x1 10.3 us: on_device(): lax.dot_general(masked, full_weight, contract_last, preferred_element_typ...]
    unnamed x9 -> x20, local copies, waits for them, and re-layouts: 0.8 us -> 12.8 us
  transfers between devices with their start and end apart: 2 -> 27, of which waited for: 2 -> 14; matrix products, arithmetic and copies ran while one was open for 3% -> 6% of each run, Pallas kernels for 0% -> 13%
where the time goes in v1:
time: 125 us; the launch traced here: 124 us
  waiting for transfers between devices  46.9 us (38%)
  starting transfers between devices  37 us (30%)
  Pallas kernels  23 us (18%)
  local copies, waits for them, and re-layouts  14.9 us (12%)
  other arithmetic  1.8 us (1%)
    ppermute x27, waiting for transfers between devices, swap(): return lax.ppermute(value, axis, [(i, i ^ bits) for i in range(size)])  46.9 us
    ppermute x27, starting transfers between devices, swap(): return lax.ppermute(value, axis, [(i, i ^ bits) for i in range(size)])  37 us
    pallas_call x4, Pallas kernels, columns(): pl.pallas_call(functools.partial(column_kernel, (shards, given, out is No...  14.6 us
    unnamed x20, local copies, waits for them, and re-layouts  12.8 us
    pallas_call x1, Pallas kernels, query_gradient(): pl.pallas_call(grad_kernel, grid=(steps,), in_specs=[whole(*token_ids.sha...  5.56 us
    pallas_call x1, Pallas kernels, raw_score_call(): pl.pallas_call(score_kernel, in_specs=[pl.BlockSpec(memory_space=pltpu.SM...  2.85 us
  transfers between devices with their start and end apart: 27, of which 14 were waited for; matrix products, arithmetic and copies ran while one was open for 6% of the time, Pallas kernels for 13%

profile of v1, /device:TPU:0, one launch (start us, length us, event | category | flops | bytes accessed | tf_op | source)
XLA Modules:
  0.0 124.4 jit_solution(6040462963080166511)
XLA Ops:
  1.7 2.2 %copy-done = bf16[512,4096]{1,0:T(8,128)(2,1)S(1)} copy-done((bf16[512,4096]{1,0:T(8,128)(2,1)S(1)}, bf16[512,4096]{1,0:T(8,128)(2,1)}, u32[]{:S(2)}) %copy-start) | copy-done | bytes 4194328
  8.7 5.6 %query_gradient.1 = (bf16[512,1024]{1,0:T(8,128)(2,1)S(1)}, bf16[256,128]{1,0:T(8,128)(2,1)S(1)}) custom-call(s32[1,512]{1,0:T(1,128)S(1)} %copy-done.6, bf16[512,1024]{1,0:T(8,128)(2,1)S(1)} %copy-done.2, bf16[512,4096]{1,0:T(8,128)(2,1)S(1)} %copy-done, bf16[64,4096]{1,0:T(8,128)(2,1)S(1)} %bitcast.39, bf16[8,64,128]{2,1,0:T(8,128)(2,1)S(1)} %bitcast.41, ...), custom_call_target="tpu_custom_call" | custom-call | flops 268435456 | bytes 6291456 | tf_op jit(solution)/shard_map/query_gradient/pallas_call | solution.py:66
  14.8 2.7 %collective-permute-start.11 = (bf16[128,1024]{1,0:T(8,128)(2,1)S(1)}, bf16[128,1024]{1,0:T(8,128)(2,1)S(1)}, u32[]{:S(2)}, u32[]{:S(2)}) collective-permute-start(bf16[128,1024]{1,0:T(8,128)(2,1)S(1)} %get-tuple-element.23.refs_0_), channel_id=1, source_target_pairs={{0,4},{1,5},{2,6},{3,7},{4,0},{5,1},{6,2},{7,3},{8,12},{9,13},{10,... | collective-permute-start | bytes 786440 | tf_op jit(solution)/shard_map/weight_exchange/ppermute | solution.py:220
  17.5 1.5 %collective-permute-start.9 = (bf16[128,1024]{1,0:T(8,128)(2,1)S(1)}, bf16[128,1024]{1,0:T(8,128)(2,1)S(1)}, u32[]{:S(2)}, u32[]{:S(2)}) collective-permute-start(bf16[128,1024]{1,0:T(8,128)(2,1)S(1)} %get-tuple-element.23.refs_0_), channel_id=1, source_target_pairs={{0,2},{1,3},{2,0},{3,1},{4,6},{5,7},{6,4},{7,5},{8,10},{9,11},{10,... | collective-permute-start | bytes 786440 | tf_op jit(solution)/shard_map/weight_exchange/ppermute | solution.py:220
  19.0 5.4 %collective-permute-done.11.refs_4_ = bf16[128,1024]{1,0:T(8,128)(2,1)S(1)} collective-permute-done((bf16[128,1024]{1,0:T(8,128)(2,1)S(1)}, bf16[128,1024]{1,0:T(8,128)(2,1)S(1)}, u32[]{:S(2)}, u32[]{:S(2)}) %collective-permute-start.11) | collective-permute-done | bytes 262176 | tf_op jit(solution)/shard_map/weight_exchange/ppermute | solution.py:220
  24.4 1.7 %collective-permute-start.13 = (bf16[128,1024]{1,0:T(8,128)(2,1)S(1)}, bf16[128,1024]{1,0:T(8,128)(2,1)}, u32[]{:S(2)}, u32[]{:S(2)}) collective-permute-start(bf16[128,1024]{1,0:T(8,128)(2,1)S(1)} %collective-permute-done.11.refs_4_), channel_id=1, source_target_pairs={{0,2},{1,3},{2,0},{3,1},{4,6},{5,7},{6,4},{7,5},{8,10},{9,11},{10,... | collective-permute-start | bytes 786440 | tf_op jit(solution)/shard_map/weight_exchange/ppermute | solution.py:220
  26.1 1.5 %collective-permute-start.12 = (bf16[128,1024]{1,0:T(8,128)(2,1)S(1)}, bf16[128,1024]{1,0:T(8,128)(2,1)}, u32[]{:S(2)}, u32[]{:S(2)}) collective-permute-start(bf16[128,1024]{1,0:T(8,128)(2,1)S(1)} %collective-permute-done.11.refs_4_), channel_id=1, source_target_pairs={{0,16},{16,0},{1,17},{17,1},{2,18},{18,2},{3,19},{19,3},{4,20},{20... | collective-permute-start | bytes 786440 | tf_op jit(solution)/shard_map/weight_exchange/ppermute | solution.py:220
  28.1 4.5 %collective-permute-done.13.refs_6_ = bf16[128,1024]{1,0:T(8,128)(2,1)} collective-permute-done((bf16[128,1024]{1,0:T(8,128)(2,1)S(1)}, bf16[128,1024]{1,0:T(8,128)(2,1)}, u32[]{:S(2)}, u32[]{:S(2)}) %collective-permute-start.13) | collective-permute-done | bytes 262176 | tf_op jit(solution)/shard_map/weight_exchange/ppermute | solution.py:220
  34.1 2.6 %collective-permute-start.5 = (bf16[128,1024]{1,0:T(8,128)(2,1)S(1)}, bf16[128,1024]{1,0:T(8,128)(2,1)}, u32[]{:S(2)}, u32[]{:S(2)}) collective-permute-start(bf16[128,1024]{1,0:T(8,128)(2,1)S(1)} %get-tuple-element.23.refs_0_), channel_id=1, source_target_pairs={{0,8},{1,9},{2,10},{3,11},{4,12},{5,13},{6,14},{7,15},{8,0},{9,1},... | collective-permute-start | bytes 786440 | tf_op jit(solution)/shard_map/weight_exchange/ppermute | solution.py:220
  36.7 4.3 %collective-permute-done.10.refs_3_ = bf16[128,1024]{1,0:T(8,128)(2,1)} collective-permute-done((bf16[128,1024]{1,0:T(8,128)(2,1)S(1)}, bf16[128,1024]{1,0:T(8,128)(2,1)}, u32[]{:S(2)}, u32[]{:S(2)}) %collective-permute-start.10) | collective-permute-done | bytes 262176 | tf_op jit(solution)/shard_map/weight_exchange/ppermute | solution.py:220
  41.1 4.0 %collective-permute-done.14.refs_7_ = bf16[128,1024]{1,0:T(8,128)(2,1)} collective-permute-done((bf16[128,1024]{1,0:T(8,128)(2,1)}, bf16[128,1024]{1,0:T(8,128)(2,1)}, u32[]{:S(2)}, u32[]{:S(2)}) %collective-permute-start.14) | collective-permute-done | bytes 262176 | tf_op jit(solution)/shard_map/weight_exchange/ppermute | solution.py:220
  45.1 5.3 %columns_0.1 = (bf16[512,4096]{1,0:T(8,128)(2,1)}, bf16[4,512,256]{2,1,0:T(8,128)(2,1)}) custom-call(s32[5]{0:T(128)S(1)} %stack.134.place, bf16[128,1024]{1,0:T(8,128)(2,1)S(1)} %get-tuple-element.23.refs_0_, bf16[128,1024]{1,0:T(8,128)(2,1)S(1)} %get-tuple-element.22.refs_1_, bf16[128,1024]{1,0:T(8,128)(2,1)S(1)} %collective-permute-done.9.refs_2_, ...), custom_call_target="tpu_custom_call" | custom-call | flops 2147483648 | bytes 1048576 | tf_op jit(solution)/shard_map/input_grad/columns_0/pallas_call | solution.py:206
  50.5 1.6 %collective-permute-start.18 = (bf16[256,128]{1,0:T(8,128)(2,1)S(1)}, bf16[256,128]{1,0:T(8,128)(2,1)}, u32[]{:S(2)}, u32[]{:S(2)}) collective-permute-start(bf16[256,128]{1,0:T(8,128)(2,1)S(1)} %get-tuple-element.19), channel_id=1, source_target_pairs={{0,4},{1,5},{2,6},{3,7},{4,0},{5,1},{6,2},{7,3},{8,12},{9,13},{10,... | collective-permute-start | bytes 196616 | tf_op jit(solution)/shard_map/query_exchange/ppermute | solution.py:220
  52.1 2.6 %collective-permute-start.19 = (bf16[256,128]{1,0:T(8,128)(2,1)S(1)}, bf16[256,128]{1,0:T(8,128)(2,1)}, u32[]{:S(2)}, u32[]{:S(2)}) collective-permute-start(bf16[256,128]{1,0:T(8,128)(2,1)S(1)} %get-tuple-element.19), channel_id=1, source_target_pairs={{0,8},{1,9},{2,10},{3,11},{4,12},{5,13},{6,14},{7,15},{8,0},{9,1},... | collective-permute-start | bytes 196616 | tf_op jit(solution)/shard_map/query_exchange/ppermute | solution.py:220
  56.2 3.6 %collective-permute-start = (bf16[128,1024]{1,0:T(8,128)(2,1)S(1)}, bf16[128,1024]{1,0:T(8,128)(2,1)}, u32[]{:S(2)}, u32[]{:S(2)}) collective-permute-start(bf16[128,1024]{1,0:T(8,128)(2,1)S(1)} %get-tuple-element.23.refs_0_), channel_id=1, source_target_pairs={{0,12},{1,13},{2,14},{3,15},{4,8},{5,9},{6,10},{7,11},{8,4},{9,5},... | collective-permute-start | bytes 786440 | tf_op jit(solution)/shard_map/weight_exchange/ppermute | solution.py:220
  59.9 1.6 %collective-permute-done.20 = bf16[256,128]{1,0:T(8,128)(2,1)S(1)} collective-permute-done((bf16[256,128]{1,0:T(8,128)(2,1)S(1)}, bf16[256,128]{1,0:T(8,128)(2,1)S(1)}, u32[]{:S(2)}, u32[]{:S(2)}) %collective-permute-start.20) | collective-permute-done | bytes 65568 | tf_op jit(solution)/shard_map/query_exchange/ppermute | solution.py:220
  62.5 1.6 %collective-permute-start.6 = (bf16[128,1024]{1,0:T(8,128)(2,1)}, bf16[128,1024]{1,0:T(8,128)(2,1)S(1)}, u32[]{:S(2)}, u32[]{:S(2)}) collective-permute-start(bf16[128,1024]{1,0:T(8,128)(2,1)} %collective-permute-done.5.refs_0_), channel_id=1, source_target_pairs={{0,16},{16,0},{1,17},{17,1},{2,18},{18,2},{3,19},{19,3},{4,20},{20... | collective-permute-start | bytes 786440 | tf_op jit(solution)/shard_map/weight_exchange/ppermute | solution.py:220
  66.1 1.5 %constant_dynamic-update-slice_fusion.2 = bf16[8,256,128]{2,1,0:T(8,128)(2,1)} fusion(bf16[8,256,128]{2,1,0:T(8,128)(2,1)} %constant_dynamic-update-slice_fusion.3, bf16[256,128]{1,0:T(8,128)(2,1)} %collective-permute-done.19), kind=kLoop, calls=%fused_computation.3 | loop fusion | bytes 131072
  67.5 1.9 %collective-permute-start.2 = (bf16[128,1024]{1,0:T(8,128)(2,1)}, bf16[128,1024]{1,0:T(8,128)(2,1)S(1)}, u32[]{:S(2)}, u32[]{:S(2)}) collective-permute-start(bf16[128,1024]{1,0:T(8,128)(2,1)} %collective-permute-done.refs_0_), channel_id=1, source_target_pairs={{0,2},{1,3},{2,0},{3,1},{4,6},{5,7},{6,4},{7,5},{8,10},{9,11},{10,... | collective-permute-start | bytes 786440 | tf_op jit(solution)/shard_map/weight_exchange/ppermute | solution.py:220
  69.5 2.5 %collective-permute-done.6.refs_1_ = bf16[128,1024]{1,0:T(8,128)(2,1)S(1)} collective-permute-done((bf16[128,1024]{1,0:T(8,128)(2,1)}, bf16[128,1024]{1,0:T(8,128)(2,1)S(1)}, u32[]{:S(2)}, u32[]{:S(2)}) %collective-permute-start.6) | collective-permute-done | bytes 262176 | tf_op jit(solution)/shard_map/weight_exchange/ppermute | solution.py:220
  72.0 3.1 %collective-permute-done.8.refs_3_ = bf16[128,1024]{1,0:T(8,128)(2,1)S(1)} collective-permute-done((bf16[128,1024]{1,0:T(8,128)(2,1)}, bf16[128,1024]{1,0:T(8,128)(2,1)S(1)}, u32[]{:S(2)}, u32[]{:S(2)}) %collective-permute-start.8) | collective-permute-done | bytes 262176 | tf_op jit(solution)/shard_map/weight_exchange/ppermute | solution.py:220
  75.1 3.9 %columns_1.1 = (bf16[512,4096]{1,0:T(8,128)(2,1)}, bf16[2,512,256]{2,1,0:T(8,128)(2,1)}) custom-call(s32[7]{0:T(128)S(1)} %stack.129.place, bf16[128,1024]{1,0:T(8,128)(2,1)} %collective-permute-done.5.refs_0_, bf16[128,1024]{1,0:T(8,128)(2,1)S(1)} %collective-permute-done.6.refs_1_, ...), custom_call_target="tpu_custom_call", output_to_operand_aliasing={{0}: (8, {})} | custom-call | flops 1073741824 | bytes 1048576 | tf_op jit(solution)/shard_map/input_grad/columns_1/pallas_call | solution.py:206
  81.0 1.5 %collective-permute-start.1 = (bf16[128,1024]{1,0:T(8,128)(2,1)}, bf16[128,1024]{1,0:T(8,128)(2,1)}, u32[]{:S(2)}, u32[]{:S(2)}) collective-permute-start(bf16[128,1024]{1,0:T(8,128)(2,1)} %collective-permute-done.refs_0_), channel_id=1, source_target_pairs={{0,16},{16,0},{1,17},{17,1},{2,18},{18,2},{3,19},{19,3},{4,20},{20... | collective-permute-start | bytes 786440 | tf_op jit(solution)/shard_map/weight_exchange/ppermute | solution.py:220
  83.1 7.4 %collective-permute-done.1.refs_1_ = bf16[128,1024]{1,0:T(8,128)(2,1)} collective-permute-done((bf16[128,1024]{1,0:T(8,128)(2,1)}, bf16[128,1024]{1,0:T(8,128)(2,1)}, u32[]{:S(2)}, u32[]{:S(2)}) %collective-permute-start.1) | collective-permute-done | bytes 262176 | tf_op jit(solution)/shard_map/weight_exchange/ppermute | solution.py:220
  90.4 4.7 %collective-permute-done.3.refs_3_ = bf16[128,1024]{1,0:T(8,128)(2,1)} collective-permute-done((bf16[128,1024]{1,0:T(8,128)(2,1)S(1)}, bf16[128,1024]{1,0:T(8,128)(2,1)}, u32[]{:S(2)}, u32[]{:S(2)}) %collective-permute-start.3) | collective-permute-done | bytes 262176 | tf_op jit(solution)/shard_map/weight_exchange/ppermute | solution.py:220
  95.1 4.0 %columns_2.1 = (bf16[512,4096]{1,0:T(8,128)(2,1)}, bf16[2,512,256]{2,1,0:T(8,128)(2,1)}) custom-call(s32[5]{0:T(128)S(1)} %stack.122.place, bf16[128,1024]{1,0:T(8,128)(2,1)} %collective-permute-done.refs_0_, bf16[128,1024]{1,0:T(8,128)(2,1)} %collective-permute-done.1.refs_1_, ...), custom_call_target="tpu_custom_call", output_to_operand_aliasing={{0}: (8, {})} | custom-call | flops 1073741824 | bytes 1048576 | tf_op jit(solution)/shard_map/input_grad/columns_2/pallas_call | solution.py:206
  99.3 1.6 %copy-done.1 = bf16[32,32768]{1,0:T(8,128)(2,1)S(1)} copy-done((bf16[32,32768]{1,0:T(8,128)(2,1)S(1)}, bf16[32,32768]{1,0:T(8,128)(2,1)}, u32[]{:S(2)}) %copy-start.1) | copy-done | bytes 2097176
  100.9 2.9 %raw_scores.1 = (f32[16,32]{1,0:T(8,128)S(1)}, f32[16,128]{1,0:T(8,128)S(1)}) custom-call(s32[16]{0:T(128)S(1)} %stack.142.place, bf16[8,256,128]{2,1,0:T(8,128)(2,1)} %constant_dynamic-update-slice_fusion.mine, bf16[8,256,128]{2,1,0:T(8,128)(2,1)S(1)} %collective-permute-done.22.other, bf16[32,32768]{1,0:T(8,128)(2,1)S(1)} %copy-done.1), custom_call_target="tpu_custom_call" | custom-call | flops 33554432 | bytes 3145728 | tf_op jit(solution)/shard_map/raw_scores/pallas_call | solution.py:122
  106.3 2.4 %collective-permute-done.24 = f32[16,128]{1,0:T(8,128)S(1)} collective-permute-done((f32[16,128]{1,0:T(8,128)S(1)}, f32[16,128]{1,0:T(8,128)S(1)}, u32[]{:S(2)}, u32[]{:S(2)}) %collective-permute-start.24) | collective-permute-done | bytes 8224 | tf_op jit(solution)/shard_map/power/ppermute | solution.py:220
  108.7 7.3 %collective-permute-start.25 = (f32[16,128]{1,0:T(8,128)S(1)}, f32[16,128]{1,0:T(8,128)S(1)}, u32[]{:S(2)}, u32[]{:S(2)}) collective-permute-start(f32[16,128]{1,0:T(8,128)S(1)} %add.24), channel_id=1, source_target_pairs={{0,4},{1,5},{2,6},{3,7},{4,0},{5,1},{6,2},{7,3},{8,12},{9,13},{10,... | collective-permute-start | bytes 24584 | tf_op jit(solution)/shard_map/power/ppermute | solution.py:220
  116.0 1.6 %collective-permute-done.25 = f32[16,128]{1,0:T(8,128)S(1)} collective-permute-done((f32[16,128]{1,0:T(8,128)S(1)}, f32[16,128]{1,0:T(8,128)S(1)}, u32[]{:S(2)}, u32[]{:S(2)}) %collective-permute-start.25) | collective-permute-done | bytes 8224 | tf_op jit(solution)/shard_map/power/ppermute | solution.py:220
  117.7 4.5 %collective-permute-done.26 = f32[16,128]{1,0:T(8,128)S(1)} collective-permute-done((f32[16,128]{1,0:T(8,128)S(1)}, f32[16,128]{1,0:T(8,128)S(1)}, u32[]{:S(2)}, u32[]{:S(2)}) %collective-permute-start.26) | collective-permute-done | bytes 8224 | tf_op jit(solution)/shard_map/power/ppermute | solution.py:220
  (62 shorter events, 20.7 us)
Async XLA Ops:
  0.6 14.1 %copy-start.7 = (bf16[256,1024]{1,0:T(8,128)(2,1)S(1)}, bf16[256,1024]{1,0:T(8,128)(2,1)}, u32[]{:S(2)}) copy-start(bf16[256,1024]{1,0:T(8,128)(2,1)} %param.12) | copy-start | bytes 1572868
  1.7 2.2 %copy-start = (bf16[512,4096]{1,0:T(8,128)(2,1)S(1)}, bf16[512,4096]{1,0:T(8,128)(2,1)}, u32[]{:S(2)}) copy-start(bf16[512,4096]{1,0:T(8,128)(2,1)} %hid.1) | copy-start | bytes 12582916
  3.9 1.2 copy-start.2
  5.1 1.0 copy-start.3
  14.2 30.8 %collective-permute-start.4 = (bf16[512,1024]{1,0:T(8,128)(2,1)S(1)}, bf16[512,1024]{1,0:T(8,128)(2,1)S(1)}, u32[]{:S(2)}, u32[]{:S(2)}) collective-permute-start(bf16[512,1024]{1,0:T(8,128)(2,1)S(1)} %get-tuple-element.12.refs_8_.refs_4_), channel_id=1, source_target_pairs={{0,1},{1,0},{2,3},{3,2},{4,5},{5,4},{6,7},{7,6},{8,9},{9,8},{10,11... | collective-permute-start | bytes 3145736 | tf_op jit(solution)/shard_map/ppermute | solution.py:220
  14.8 9.6 %collective-permute-start.11 = (bf16[128,1024]{1,0:T(8,128)(2,1)S(1)}, bf16[128,1024]{1,0:T(8,128)(2,1)S(1)}, u32[]{:S(2)}, u32[]{:S(2)}) collective-permute-start(bf16[128,1024]{1,0:T(8,128)(2,1)S(1)} %get-tuple-element.23.refs_0_), channel_id=1, source_target_pairs={{0,4},{1,5},{2,6},{3,7},{4,0},{5,1},{6,2},{7,3},{8,12},{9,13},{10,... | collective-permute-start | bytes 786440 | tf_op jit(solution)/shard_map/weight_exchange/ppermute | solution.py:220
  17.5 10.1 %collective-permute-start.9 = (bf16[128,1024]{1,0:T(8,128)(2,1)S(1)}, bf16[128,1024]{1,0:T(8,128)(2,1)S(1)}, u32[]{:S(2)}, u32[]{:S(2)}) collective-permute-start(bf16[128,1024]{1,0:T(8,128)(2,1)S(1)} %get-tuple-element.23.refs_0_), channel_id=1, source_target_pairs={{0,2},{1,3},{2,0},{3,1},{4,6},{5,7},{6,4},{7,5},{8,10},{9,11},{10,... | collective-permute-start | bytes 786440 | tf_op jit(solution)/shard_map/weight_exchange/ppermute | solution.py:220
  24.4 8.2 %collective-permute-start.13 = (bf16[128,1024]{1,0:T(8,128)(2,1)S(1)}, bf16[128,1024]{1,0:T(8,128)(2,1)}, u32[]{:S(2)}, u32[]{:S(2)}) collective-permute-start(bf16[128,1024]{1,0:T(8,128)(2,1)S(1)} %collective-permute-done.11.refs_4_), channel_id=1, source_target_pairs={{0,2},{1,3},{2,0},{3,1},{4,6},{5,7},{6,4},{7,5},{8,10},{9,11},{10,... | collective-permute-start | bytes 786440 | tf_op jit(solution)/shard_map/weight_exchange/ppermute | solution.py:220
  26.1 10.6 %collective-permute-start.12 = (bf16[128,1024]{1,0:T(8,128)(2,1)S(1)}, bf16[128,1024]{1,0:T(8,128)(2,1)}, u32[]{:S(2)}, u32[]{:S(2)}) collective-permute-start(bf16[128,1024]{1,0:T(8,128)(2,1)S(1)} %collective-permute-done.11.refs_4_), channel_id=1, source_target_pairs={{0,16},{16,0},{1,17},{17,1},{2,18},{18,2},{3,19},{19,3},{4,20},{20... | collective-permute-start | bytes 786440 | tf_op jit(solution)/shard_map/weight_exchange/ppermute | solution.py:220
  27.6 13.5 %collective-permute-start.10 = (bf16[128,1024]{1,0:T(8,128)(2,1)S(1)}, bf16[128,1024]{1,0:T(8,128)(2,1)}, u32[]{:S(2)}, u32[]{:S(2)}) collective-permute-start(bf16[128,1024]{1,0:T(8,128)(2,1)S(1)} %collective-permute-done.9.refs_2_), channel_id=1, source_target_pairs={{0,16},{16,0},{1,17},{17,1},{2,18},{18,2},{3,19},{19,3},{4,20},{20... | collective-permute-start | bytes 786440 | tf_op jit(solution)/shard_map/weight_exchange/ppermute | solution.py:220
  32.6 12.4 %collective-permute-start.14 = (bf16[128,1024]{1,0:T(8,128)(2,1)}, bf16[128,1024]{1,0:T(8,128)(2,1)}, u32[]{:S(2)}, u32[]{:S(2)}) collective-permute-start(bf16[128,1024]{1,0:T(8,128)(2,1)} %collective-permute-done.13.refs_6_), channel_id=1, source_target_pairs={{0,16},{16,0},{1,17},{17,1},{2,18},{18,2},{3,19},{19,3},{4,20},{20... | collective-permute-start | bytes 786440 | tf_op jit(solution)/shard_map/weight_exchange/ppermute | solution.py:220
  34.1 20.9 %collective-permute-start.5 = (bf16[128,1024]{1,0:T(8,128)(2,1)S(1)}, bf16[128,1024]{1,0:T(8,128)(2,1)}, u32[]{:S(2)}, u32[]{:S(2)}) collective-permute-start(bf16[128,1024]{1,0:T(8,128)(2,1)S(1)} %get-tuple-element.23.refs_0_), channel_id=1, source_target_pairs={{0,8},{1,9},{2,10},{3,11},{4,12},{5,13},{6,14},{7,15},{8,0},{9,1},... | collective-permute-start | bytes 786440 | tf_op jit(solution)/shard_map/weight_exchange/ppermute | solution.py:220
  50.4 24.7 %collective-permute-start.15 = (bf16[4,512,256]{2,1,0:T(8,128)(2,1)}, bf16[4,512,256]{2,1,0:T(8,128)(2,1)S(1)}, u32[]{:S(2)}, u32[]{:S(2)}) collective-permute-start(bf16[4,512,256]{2,1,0:T(8,128)(2,1)} %get-tuple-element.13), channel_id=1, source_target_pairs={{0,1},{1,0},{2,3},{3,2},{4,5},{5,4},{6,7},{7,6},{8,9},{9,8},{10,11... | collective-permute-start | bytes 3145736 | tf_op jit(solution)/shard_map/input_grad/ppermute | solution.py:220
  50.5 5.7 %collective-permute-start.18 = (bf16[256,128]{1,0:T(8,128)(2,1)S(1)}, bf16[256,128]{1,0:T(8,128)(2,1)}, u32[]{:S(2)}, u32[]{:S(2)}) collective-permute-start(bf16[256,128]{1,0:T(8,128)(2,1)S(1)} %get-tuple-element.19), channel_id=1, source_target_pairs={{0,4},{1,5},{2,6},{3,7},{4,0},{5,1},{6,2},{7,3},{8,12},{9,13},{10,... | collective-permute-start | bytes 196616 | tf_op jit(solution)/shard_map/query_exchange/ppermute | solution.py:220
  52.1 7.8 %collective-permute-start.19 = (bf16[256,128]{1,0:T(8,128)(2,1)S(1)}, bf16[256,128]{1,0:T(8,128)(2,1)}, u32[]{:S(2)}, u32[]{:S(2)}) collective-permute-start(bf16[256,128]{1,0:T(8,128)(2,1)S(1)} %get-tuple-element.19), channel_id=1, source_target_pairs={{0,8},{1,9},{2,10},{3,11},{4,12},{5,13},{6,14},{7,15},{8,0},{9,1},... | collective-permute-start | bytes 196616 | tf_op jit(solution)/shard_map/query_exchange/ppermute | solution.py:220
  54.7 6.8 %collective-permute-start.20 = (bf16[256,128]{1,0:T(8,128)(2,1)S(1)}, bf16[256,128]{1,0:T(8,128)(2,1)S(1)}, u32[]{:S(2)}, u32[]{:S(2)}) collective-permute-start(bf16[256,128]{1,0:T(8,128)(2,1)S(1)} %get-tuple-element.19), channel_id=1, source_target_pairs={{0,12},{1,13},{2,14},{3,15},{4,8},{5,9},{6,10},{7,11},{8,4},{9,5},... | collective-permute-start | bytes 196616 | tf_op jit(solution)/shard_map/query_exchange/ppermute | solution.py:220
  54.9 9.1 %collective-permute-start.7 = (bf16[128,1024]{1,0:T(8,128)(2,1)}, bf16[128,1024]{1,0:T(8,128)(2,1)}, u32[]{:S(2)}, u32[]{:S(2)}) collective-permute-start(bf16[128,1024]{1,0:T(8,128)(2,1)} %collective-permute-done.5.refs_0_), channel_id=1, source_target_pairs={{0,2},{1,3},{2,0},{3,1},{4,6},{5,7},{6,4},{7,5},{8,10},{9,11},{10,... | collective-permute-start | bytes 786440 | tf_op jit(solution)/shard_map/weight_exchange/ppermute | solution.py:220
  56.2 11.4 %collective-permute-start = (bf16[128,1024]{1,0:T(8,128)(2,1)S(1)}, bf16[128,1024]{1,0:T(8,128)(2,1)}, u32[]{:S(2)}, u32[]{:S(2)}) collective-permute-start(bf16[128,1024]{1,0:T(8,128)(2,1)S(1)} %get-tuple-element.23.refs_0_), channel_id=1, source_target_pairs={{0,12},{1,13},{2,14},{3,15},{4,8},{5,9},{6,10},{7,11},{8,4},{9,5},... | collective-permute-start | bytes 786440 | tf_op jit(solution)/shard_map/weight_exchange/ppermute | solution.py:220
  62.4 17.3 %collective-permute-start.21 = (bf16[4,256,128]{2,1,0:T(8,128)(2,1)S(1)}, bf16[4,256,128]{2,1,0:T(8,128)(2,1)S(1)}, u32[]{:S(2)}, u32[]{:S(2)}) collective-permute-start(bf16[4,256,128]{2,1,0:T(8,128)(2,1)S(1)} %pad_maximum_fusion), channel_id=1, source_target_pairs={{0,2},{1,3},{2,0},{3,1},{4,6},{5,7},{6,4},{7,5},{8,10},{9,11},{10,... | collective-permute-start | bytes 786440 | tf_op jit(solution)/shard_map/query_exchange/ppermute | solution.py:220
  62.5 9.5 %collective-permute-start.6 = (bf16[128,1024]{1,0:T(8,128)(2,1)}, bf16[128,1024]{1,0:T(8,128)(2,1)S(1)}, u32[]{:S(2)}, u32[]{:S(2)}) collective-permute-start(bf16[128,1024]{1,0:T(8,128)(2,1)} %collective-permute-done.5.refs_0_), channel_id=1, source_target_pairs={{0,16},{16,0},{1,17},{17,1},{2,18},{18,2},{3,19},{19,3},{4,20},{20... | collective-permute-start | bytes 786440 | tf_op jit(solution)/shard_map/weight_exchange/ppermute | solution.py:220
  64.1 11.0 %collective-permute-start.8 = (bf16[128,1024]{1,0:T(8,128)(2,1)}, bf16[128,1024]{1,0:T(8,128)(2,1)S(1)}, u32[]{:S(2)}, u32[]{:S(2)}) collective-permute-start(bf16[128,1024]{1,0:T(8,128)(2,1)} %collective-permute-done.7.refs_2_), channel_id=1, source_target_pairs={{0,16},{16,0},{1,17},{17,1},{2,18},{18,2},{3,19},{19,3},{4,20},{20... | collective-permute-start | bytes 786440 | tf_op jit(solution)/shard_map/weight_exchange/ppermute | solution.py:220
  67.5 14.9 %collective-permute-start.2 = (bf16[128,1024]{1,0:T(8,128)(2,1)}, bf16[128,1024]{1,0:T(8,128)(2,1)S(1)}, u32[]{:S(2)}, u32[]{:S(2)}) collective-permute-start(bf16[128,1024]{1,0:T(8,128)(2,1)} %collective-permute-done.refs_0_), channel_id=1, source_target_pairs={{0,2},{1,3},{2,0},{3,1},{4,6},{5,7},{6,4},{7,5},{8,10},{9,11},{10,... | collective-permute-start | bytes 786440 | tf_op jit(solution)/shard_map/weight_exchange/ppermute | solution.py:220
  79.0 16.1 %collective-permute-start.16 = (bf16[2,512,256]{2,1,0:T(8,128)(2,1)}, bf16[2,512,256]{2,1,0:T(8,128)(2,1)S(1)}, u32[]{:S(2)}, u32[]{:S(2)}) collective-permute-start(bf16[2,512,256]{2,1,0:T(8,128)(2,1)} %get-tuple-element.15), channel_id=1, source_target_pairs={{0,1},{1,0},{2,3},{3,2},{4,5},{5,4},{6,7},{7,6},{8,9},{9,8},{10,11... | collective-permute-start | bytes 1572872 | tf_op jit(solution)/shard_map/input_grad/ppermute | solution.py:220
  80.5 18.9 %collective-permute-start.22 = (bf16[8,256,128]{2,1,0:T(8,128)(2,1)}, bf16[8,256,128]{2,1,0:T(8,128)(2,1)S(1)}, u32[]{:S(2)}, u32[]{:S(2)}) collective-permute-start(bf16[8,256,128]{2,1,0:T(8,128)(2,1)} %constant_dynamic-update-slice_fusion.mine), channel_id=1, source_target_pairs={{0,1},{1,0},{2,3},{3,2},{4,5},{5,4},{6,7},{7,6},{8,9},{9,8},{10,11... | collective-permute-start | bytes 1572872 | tf_op jit(solution)/shard_map/query_exchange/ppermute | solution.py:220
  81.0 9.5 %collective-permute-start.1 = (bf16[128,1024]{1,0:T(8,128)(2,1)}, bf16[128,1024]{1,0:T(8,128)(2,1)}, u32[]{:S(2)}, u32[]{:S(2)}) collective-permute-start(bf16[128,1024]{1,0:T(8,128)(2,1)} %collective-permute-done.refs_0_), channel_id=1, source_target_pairs={{0,16},{16,0},{1,17},{17,1},{2,18},{18,2},{3,19},{19,3},{4,20},{20... | collective-permute-start | bytes 786440 | tf_op jit(solution)/shard_map/weight_exchange/ppermute | solution.py:220
  82.4 12.7 %collective-permute-start.3 = (bf16[128,1024]{1,0:T(8,128)(2,1)S(1)}, bf16[128,1024]{1,0:T(8,128)(2,1)}, u32[]{:S(2)}, u32[]{:S(2)}) collective-permute-start(bf16[128,1024]{1,0:T(8,128)(2,1)S(1)} %collective-permute-done.2.refs_2_), channel_id=1, source_target_pairs={{0,16},{16,0},{1,17},{17,1},{2,18},{18,2},{3,19},{19,3},{4,20},{20... | collective-permute-start | bytes 786440 | tf_op jit(solution)/shard_map/weight_exchange/ppermute | solution.py:220
  99.1 23.9 %collective-permute-start.17 = (bf16[2,512,256]{2,1,0:T(8,128)(2,1)}, bf16[2,512,256]{2,1,0:T(8,128)(2,1)S(1)}, u32[]{:S(2)}, u32[]{:S(2)}) collective-permute-start(bf16[2,512,256]{2,1,0:T(8,128)(2,1)} %get-tuple-element.17), channel_id=1, source_target_pairs={{0,1},{1,0},{2,3},{3,2},{4,5},{5,4},{6,7},{7,6},{8,9},{9,8},{10,11... | collective-permute-start | bytes 1572872 | tf_op jit(solution)/shard_map/input_grad/ppermute | solution.py:220
  99.3 1.6 %copy-start.1 = (bf16[32,32768]{1,0:T(8,128)(2,1)S(1)}, bf16[32,32768]{1,0:T(8,128)(2,1)}, u32[]{:S(2)}) copy-start(bf16[32,32768]{1,0:T(8,128)(2,1)} %store.1) | copy-start | bytes 6291460
  103.8 1.3 %collective-permute-start.23 = (f32[16,128]{1,0:T(8,128)S(1)}, f32[16,128]{1,0:T(8,128)S(1)}, u32[]{:S(2)}, u32[]{:S(2)}) collective-permute-start(f32[16,128]{1,0:T(8,128)S(1)} %get-tuple-element.21), channel_id=1, source_target_pairs={{0,1},{1,0},{2,3},{3,2},{4,5},{5,4},{6,7},{7,6},{8,9},{9,8},{10,11... | collective-permute-start | bytes 24584 | tf_op jit(solution)/shard_map/power/ppermute | solution.py:220
  105.1 3.7 %collective-permute-start.24 = (f32[16,128]{1,0:T(8,128)S(1)}, f32[16,128]{1,0:T(8,128)S(1)}, u32[]{:S(2)}, u32[]{:S(2)}) collective-permute-start(f32[16,128]{1,0:T(8,128)S(1)} %add.23), channel_id=1, source_target_pairs={{0,2},{1,3},{2,0},{3,1},{4,6},{5,7},{6,4},{7,5},{8,10},{9,11},{10,... | collective-permute-start | bytes 24584 | tf_op jit(solution)/shard_map/power/ppermute | solution.py:220
  108.7 8.9 %collective-permute-start.25 = (f32[16,128]{1,0:T(8,128)S(1)}, f32[16,128]{1,0:T(8,128)S(1)}, u32[]{:S(2)}, u32[]{:S(2)}) collective-permute-start(f32[16,128]{1,0:T(8,128)S(1)} %add.24), channel_id=1, source_target_pairs={{0,4},{1,5},{2,6},{3,7},{4,0},{5,1},{6,2},{7,3},{8,12},{9,13},{10,... | collective-permute-start | bytes 24584 | tf_op jit(solution)/shard_map/power/ppermute | solution.py:220
  117.7 4.5 %collective-permute-start.26 = (f32[16,128]{1,0:T(8,128)S(1)}, f32[16,128]{1,0:T(8,128)S(1)}, u32[]{:S(2)}, u32[]{:S(2)}) collective-permute-start(f32[16,128]{1,0:T(8,128)S(1)} %add.25), channel_id=1, source_target_pairs={{0,8},{1,9},{2,10},{3,11},{4,12},{5,13},{6,14},{7,15},{8,0},{9,1},... | collective-permute-start | bytes 24584 | tf_op jit(solution)/shard_map/power/ppermute | solution.py:220
  (3 other events, 2.5 us)

commit v2 on v0

v2 whole, which is shorter than its diff:
```python
import functools

import jax
import jax.numpy as jnp
from jax import lax
from jax.experimental import pallas as pl
from jax.experimental.pallas import tpu as pltpu
from jax.sharding import PartitionSpec as P

BF16 = jnp.bfloat16
F32 = jnp.float32
HIGHEST = lax.Precision.HIGHEST
LAST = (((1,), (1,)), ((), ()))
FIRST = (((0,), (0,)), ((), ()))
VMEM = pltpu.VMEM
MIB = 1024 * 1024


SMALL = pl.CostEstimate(flops=1, bytes_accessed=1, transcendentals=0)


def params(mib=24):
    return pltpu.CompilerParams(vmem_limit_bytes=mib * MIB)


def split(x):
    high = x.astype(BF16)
    return high, (x - high.astype(F32)).astype(BF16)


def mask_kernel(ids, up, masked):
    live = jnp.sum((ids[...] != 0).astype(jnp.int32))
    row = lax.broadcasted_iota(jnp.int32, up.shape, 0)
    masked[...] = jnp.where(row < live, up[...].astype(F32), 0.0).astype(BF16)


def mask(token_ids, upstream):
    return pl.pallas_call(
        mask_kernel,
        in_specs=[pl.BlockSpec(memory_space=VMEM)] * 2,
        out_specs=pl.BlockSpec(memory_space=VMEM),
        out_shape=jax.ShapeDtypeStruct(upstream.shape, BF16),
        compiler_params=params(),
        cost_estimate=SMALL,
        name="mask",
    )(token_ids, upstream)


def grad_kernel(ids, pout, a_inv, b_inv, up_hbm, hid_hbm, pin_hbm, masked, grad, up, hid, pin, sems):
    steps, _, chunk = hid.shape
    copies = [pltpu.make_async_copy(pin_hbm, pin, sems.at[0])]
    for k in range(steps):
        copies.append(
            pltpu.make_async_copy(hid_hbm.at[:, pl.ds(k * chunk, chunk)], hid.at[k], sems.at[1 + k])
        )
    copies.append(pltpu.make_async_copy(up_hbm, up, sems.at[1 + steps]))
    for copy in copies:
        copy.start()
    heads, rank, head_dim = pout.shape
    half = rank // 2
    out_sides, in_sides = [], []
    for h in range(heads):
        high, low = split(b_inv[h])
        side = lax.dot_general(pout[h], high, FIRST, preferred_element_type=F32)
        side += lax.dot_general(pout[h], low, FIRST, preferred_element_type=F32)
        high, low = split(side)
        out_sides.append(jnp.concatenate([high, low, high], axis=0))
        rows = [a_inv[h, pl.ds(odd, half, stride=2), :] for odd in range(2)]
        high, low = split(jnp.concatenate(rows, axis=0))
        in_sides.append(jnp.concatenate([high, high, low], axis=1))
    copies[0].wait()
    left = None
    for k in range(steps):
        copies[1 + k].wait()
        part = lax.dot_general(
            hid[k], pin[:, k * chunk : (k + 1) * chunk], LAST, preferred_element_type=F32
        )
        left = part if left is None else left + part
    copies[-1].wait()
    mask_kernel(ids, up, masked)
    both = jnp.dot(left.T.astype(BF16), masked[...], preferred_element_type=F32)
    high, low = split(both)
    for h in range(heads):
        lanes = slice(h * head_dim, (h + 1) * head_dim)
        terms = jnp.concatenate([high[:, lanes], high[:, lanes], low[:, lanes]], axis=1)
        mid = jnp.dot(terms, out_sides[h], preferred_element_type=F32)
        mid_high, mid_low = split(mid)
        terms = jnp.concatenate([mid_high, mid_low, mid_high], axis=0)
        pre = jnp.dot(in_sides[h], terms, preferred_element_type=F32)
        grad[h * half : (h + 1) * half, :] = jnp.concatenate(
            [pre[:half], pre[half:]], axis=1
        ).astype(BF16)


def query_gradient(token_ids, upstream, hidden, proj_in, proj_out, in_inverse, out_inverse):
    tokens, width = hidden.shape
    heads, head_dim, rank = proj_out.shape
    steps = 4 if width % 512 == 0 else 1
    vmem, hbm = pl.BlockSpec(memory_space=VMEM), pl.BlockSpec(memory_space=pltpu.HBM)
    whole = pl.BlockSpec()
    return pl.pallas_call(
        grad_kernel,
        in_specs=[whole] * 4 + [hbm] * 3,
        out_specs=[vmem, vmem],
        out_shape=[
            jax.ShapeDtypeStruct(upstream.shape, BF16),
            jax.ShapeDtypeStruct((heads * rank // 2, 2 * rank), BF16),
        ],
        scratch_shapes=[
            VMEM(upstream.shape, BF16),
            VMEM((steps, tokens, width // steps), BF16),
            VMEM((rank, width), BF16),
            pltpu.SemaphoreType.DMA((steps + 2,)),
        ],
        compiler_params=params(57),
        cost_estimate=SMALL,
        name="query_gradient",
    )(token_ids, proj_out.swapaxes(1, 2), in_inverse, out_inverse, upstream, hidden, proj_in.T)


def join_kernel(first, second, both):
    count = first.shape[0]
    both[:count] = first[...]
    both[count:] = second[...]


def join(first, second):
    vmem = pl.BlockSpec(memory_space=VMEM)
    shape = (first.shape[0] + second.shape[0], *first.shape[1:])
    return pl.pallas_call(
        join_kernel,
        in_specs=[vmem, vmem],
        out_specs=vmem,
        out_shape=jax.ShapeDtypeStruct(shape, first.dtype),
        compiler_params=params(),
        cost_estimate=SMALL,
        name="join",
    )(first, second)


def score_kernel(bits, *refs):
    *held, store_hbm, scores, power, wide, store, sems = refs
    steps, _, chunk = store.shape
    copies = []
    for k in range(steps):
        copies.append(
            pltpu.make_async_copy(store_hbm.at[:, pl.ds(k * chunk, chunk)], store.at[k], sems.at[k])
        )
        copies[-1].start()
    me = lax.axis_index("seq")
    queries = len(bits)
    groups, lanes = held[0].shape[1:]
    rows = [ref.at[k] for ref in held for k in range(ref.shape[0])]
    for bit, row in zip(bits, rows):
        wide[pl.ds(me ^ bit, groups, stride=queries), :] = row[...].astype(F32)
    total = jnp.zeros(scores.shape, F32)
    each = chunk // lanes
    for k in range(steps):
        lhs = jnp.concatenate(
            [
                wide[g * queries : (g + 1) * queries, :].astype(BF16)
                for g in range(k * each, (k + 1) * each)
            ],
            axis=1,
        )
        copies[k].wait()
        total += lax.dot_general(lhs, store[k], LAST, preferred_element_type=F32)
    scores[...] = total
    square = jnp.sum(total * total, axis=1, keepdims=True)
    power[...] = jnp.broadcast_to(square, power.shape)


def raw_score_call(bits, held, datastore):
    groups, lanes = held[0].shape[1:]
    queries, (rows, flat) = len(bits), datastore.shape
    steps = 4 if groups % 4 == 0 else 1
    vmem = pl.BlockSpec(memory_space=VMEM)
    return pl.pallas_call(
        functools.partial(score_kernel, bits),
        in_specs=[vmem] * len(held) + [pl.BlockSpec(memory_space=pltpu.HBM)],
        out_specs=[vmem, vmem],
        out_shape=[
            jax.ShapeDtypeStruct((queries, rows), F32),
            jax.ShapeDtypeStruct((queries, lanes), F32),
        ],
        scratch_shapes=[
            VMEM((groups * queries, lanes), F32),
            VMEM((steps, rows, flat // steps), BF16),
            pltpu.SemaphoreType.DMA((steps,)),
        ],
        compiler_params=params(48),
        cost_estimate=SMALL,
        name="raw_scores",
    )(*held, datastore)


def put(source, out, spot, sem):
    width = source.shape[1]
    col = pl.multiple_of(spot * width, width)
    copy = pltpu.make_async_copy(source, out.at[:, pl.ds(col, width)], sem)
    copy.start()
    return copy


def column_kernel(bits, pieces, fresh, mine, other, *refs):
    me, grp = lax.axis_index("seq"), lax.axis_index("grp")
    shard_refs = []
    for count, _ in pieces:
        shard_refs.append(refs[:count])
        refs = refs[count:]
    out, *away, weight, tile, sems = refs[0 if fresh else 1 :]
    copies = []
    for k, (bit, parts) in enumerate(zip(bits, shard_refs)):
        if len(parts) == 1:
            (whole,) = parts
        else:
            whole = weight.at[k]
            rows = parts[0].shape[0]
            for part, half in zip(parts, (grp, 1 - grp) if pieces[k][1] else (0, 1)):
                whole[pl.ds(pl.multiple_of(half * rows, rows), rows), :] = part[...]
        tile[k] = lax.dot_general(mine[...], whole[...], LAST, preferred_element_type=F32).astype(BF16)
        copies.append(put(tile.at[k], out, me ^ bit, sems.at[k]))
        away[k][...] = lax.dot_general(
            other[...], whole[...], LAST, preferred_element_type=F32
        ).astype(BF16)
    for copy in copies:
        copy.wait()


def columns(name, bits, tokens, shards, out, out_shape):
    vmem, hbm = pl.BlockSpec(memory_space=VMEM), pl.BlockSpec(memory_space=pltpu.HBM)
    shards, own_first = [s[0] for s in shards], [s[1] for s in shards]
    parts = [p for shard in shards for p in shard]
    operands = [*tokens, *parts]
    in_specs = [vmem] * len(operands)
    aliases = {}
    if out is not None:
        aliases = {len(operands): 0}
        operands.append(out)
        in_specs.append(hbm)
    count, height = len(shards), out_shape[0]
    rows, depth = sum(p.shape[0] for p in shards[0]), parts[0].shape[1]
    made = pl.pallas_call(
        functools.partial(
            column_kernel, bits, [(len(p), f) for p, f in zip(shards, own_first)], out is None
        ),
        in_specs=in_specs,
        out_specs=[hbm] + [vmem] * count,
        out_shape=[jax.ShapeDtypeStruct(out_shape, BF16)]
        + [jax.ShapeDtypeStruct((height, rows), BF16)] * count,
        scratch_shapes=[
            VMEM((count, rows, depth), BF16),
            VMEM((count, height, rows), BF16),
            pltpu.SemaphoreType.DMA((count,)),
        ],
        input_output_aliases=aliases,
        compiler_params=params(),
        cost_estimate=SMALL,
        name=name,
    )(*operands)
    return made[0], made[1:]


def put(source, out, spot, sem):
    width = source.shape[1]
    col = pl.multiple_of(spot * width, width)
    copy = pltpu.make_async_copy(source, out.at[:, pl.ds(col, width)], sem)
    copy.start()
    return copy


def place_kernel(bits, *refs):
    (*came, _, out, sems) = refs
    me = lax.axis_index("seq")
    copies = [put(ref, out, me ^ bit, sems.at[n]) for n, (bit, ref) in enumerate(zip(bits, came))]
    for copy in copies:
        copy.wait()


def place_columns(bits, came, out):
    vmem, hbm = pl.BlockSpec(memory_space=VMEM), pl.BlockSpec(memory_space=pltpu.HBM)
    return pl.pallas_call(
        functools.partial(place_kernel, bits),
        in_specs=[vmem] * len(came) + [hbm],
        out_specs=hbm,
        out_shape=jax.ShapeDtypeStruct(out.shape, BF16),
        scratch_shapes=[pltpu.SemaphoreType.DMA((len(came),))],
        input_output_aliases={len(came): 0},
        compiler_params=params(),
        cost_estimate=SMALL,
        name="place_columns",
    )(*came, out)


def swap(value, axis, size, bits):
    return lax.ppermute(value, axis, [(i, i ^ bits) for i in range(size)])


def by_exchange(
    size, hidden, token_ids, upstream, w_value, proj_in, proj_out, in_inverse, out_inverse, datastore
):
    ring = functools.partial(lambda bits, v: swap(v, "seq", size, bits))
    core, side = 1, 2
    far = [4 * k for k in range(1, size // 4)]
    cross = lambda v: swap(v, "grp", 2, 1)
    me, grp = lax.axis_index("seq"), lax.axis_index("grp")
    half = w_value.shape[0] // 2
    out_shape = (hidden.shape[0], w_value.shape[0] * size)
    own_half = lambda v: lax.dynamic_slice_in_dim(v, grp * half, half, 0)
    after = lambda v, *first: lax.optimization_barrier((v, *first))[0]

    with jax.named_scope("weight_first"):
        upstream_other, ids_other = ring(core, upstream), ring(core, token_ids)
        near = own_half(w_value)
        beside = ring(side, w_value)
        got = [ring(b, near if n else w_value) for n, b in enumerate(far)]
    masked, grad = query_gradient(
        token_ids, upstream, hidden, proj_in, proj_out, in_inverse, out_inverse
    )
    with jax.named_scope("weight_second"):
        h1, beside = after((got[0], beside), grad)
        y1 = [ring(side, h1[:half]), ring(side, h1[half:])]

    with jax.named_scope("query_exchange"):
        held, order, bit = after(grad, upstream_other)[None], [0], 4
        while bit < size:
            came = ring(bit, held)
            if bit == size // 2:
                held, came, rest, y1, beside = lax.optimization_barrier(
                    (held, came, got[1:], y1, beside)
                )
            held, order = join(held, came), order + [b ^ bit for b in order]
            bit *= 2
        came = ring(side, held)
        xs, ys = [cross(h) for h in rest], [ring(side, h) for h in rest[:-1]]
        came, xs, ys = lax.optimization_barrier((came, xs, ys))
        groups = [held, came, ring(core, held), ring(core, came)]
        order = [b ^ s for s in (0, side, core, side ^ core) for b in order]
    raw, power = raw_score_call(order, groups, datastore)

    with jax.named_scope("power"):
        for bits in ([core, side, core ^ side], far):
            parts = [ring(b, power) for b in bits]
            power = power + functools.reduce(jnp.add, parts)
        spread = jnp.sqrt(power[:, :1] / (datastore.shape[0] * size) + 1e-06)

    with jax.named_scope("weight_third"):
        ys.append(ring(side, rest[-1]))
        shards = {0: ((w_value,), False), side: ((beside,), False)}
        shards[far[0]], shards[far[0] ^ side] = ((h1,), False), (y1, False)
        for n, (b, h, x, y) in enumerate(zip(far[1:], rest, xs, ys)):
            d = ring(side, x) if n % 2 else cross(y)
            shards[b], shards[b ^ side] = ((h, x), True), ((y, d), True)

    with jax.named_scope("input_grad"):
        masked_other = mask(ids_other, upstream_other)
        out, came = None, []
        stages = [[0, far[0], side, far[0] ^ side], far[1:], [b ^ side for b in far[1:]]]
        for n, stage in enumerate(stages):
            out, away = columns(
                f"columns_{n}",
                stage,
                [masked, masked_other],
                [shards[b] for b in stage],
                out,
                out_shape,
            )
            came += [ring(core, a) for a in away]
        out = place_columns([core ^ b for stage in stages for b in stage], came, out)
    return out, raw / spread


def by_gather(
    size, hidden, token_ids, upstream, w_value, proj_in, proj_out, in_inverse, out_inverse, datastore
):
    queries, seq_tokens = token_ids.shape
    heads, head_dim, rank = proj_out.shape
    live_mask = (token_ids != 0).reshape(-1, 1).astype(BF16)
    masked = upstream * live_mask
    full_weight = lax.all_gather(w_value, "seq", axis=0, tiled=True)
    input_grad = lax.dot_general(masked, full_weight, LAST, preferred_element_type=F32).astype(BF16)
    left = jnp.dot(hidden, proj_in, preferred_element_type=F32).astype(BF16)
    right = jnp.einsum(
        "thd,hdr->thr", masked.reshape(-1, heads, head_dim), proj_out, preferred_element_type=F32
    ).astype(BF16)
    raw_grads = jnp.einsum(
        "qti,qthj->qhij",
        left.reshape(queries, seq_tokens, rank),
        right.reshape(queries, seq_tokens, heads, rank),
        preferred_element_type=F32,
    )
    half_way = jnp.einsum("hai,qhij->qhaj", in_inverse, raw_grads, precision=HIGHEST)
    pre = jnp.einsum("qhaj,hjb->qhab", half_way, out_inverse, precision=HIGHEST)
    grads = pre.astype(BF16).reshape(queries, -1)
    raw = lax.dot_general(
        lax.all_gather(grads, "seq", axis=0, tiled=True),
        datastore,
        LAST,
        preferred_element_type=F32,
    )
    power = lax.psum(jnp.sum(raw * raw, axis=1), "seq")
    spread = jnp.sqrt(power / (datastore.shape[0] * size) + 1e-06)
    return input_grad, raw / spread[:, None]


def solution(mesh):
    size, groups = mesh.shape["seq"], mesh.shape["grp"]

    def on_device(*args):
        hidden, token_ids, upstream, w_value = args[:4]
        fits = (
            groups == 2
            and size >= 8
            and size & (size - 1) == 0
            and token_ids.shape[0] == 1
            and w_value.shape[0] % 256 == 0
        )
        return (by_exchange if fits else by_gather)(size, *args)

    rows = P(("grp", "seq"), None)
    return jax.shard_map(
        on_device,
        mesh=mesh,
        in_specs=(rows, rows, rows, P("seq", None), P(), P(), P(), P(), rows),
        out_specs=(rows, P("grp", "seq")),
        check_vma=False,
    )
```

time: 153 us -> 86.8 us (0.57)
  waiting for transfers between devices: 84.4 us -> 31.1 us
  starting transfers between devices: 0.08 us -> 32.4 us
  blocking collectives: 32 us -> 0 us
  matrix products: 20.3 us -> 0 us
  Pallas kernels: 0 us -> 19.6 us
  between operations: 14.1 us -> 0.79 us
    all_gather x2 -> x0, waiting for transfers between devices: 83.7 us -> none  [the longest x1 43.5 us: on_device(): lax.all_gather(query_grads, 'seq', axis=0, tiled=True)]
    ppermute x0 -> x33, starting transfers between devices: none -> 32.4 us  [swap(): return lax.ppermute(value, axis, [(i, i ^ bits) for i in range(size)])]
    psum x1 -> x0, blocking collectives: 32 us -> none  [on_device(): power_sum = lax.psum(power_local, 'seq')]
    ppermute x0 -> x33, waiting for transfers between devices: none -> 31.1 us  [swap(): return lax.ppermute(value, axis, [(i, i ^ bits) for i in range(size)])]
    dot_general x6 -> x0, matrix products: 20.3 us -> none  [the longest x1 10.3 us: on_device(): lax.dot_general(masked, full_weight, contract_last, preferred_element_typ...]
    pallas_call x0 -> x9, Pallas kernels: none -> 19.6 us  [the longest x1 7.75 us: query_gradient(): pl.pallas_call(grad_kernel, in_specs=[whole] * 4 + [hbm] * 3, out_specs=[...]
  transfers between devices with their start and end apart: 2 -> 33, of which waited for: 2 -> 12; matrix products, arithmetic and copies ran while one was open for 3% -> 2% of each run, Pallas kernels for 0% -> 21%
where the time goes in v2:
time: 86.8 us; the launch traced here: 86.6 us
  starting transfers between devices  32.4 us (37%)
  waiting for transfers between devices  31.1 us (36%)
  Pallas kernels  19.6 us (23%)
  local copies, waits for them, and re-layouts  1.9 us (2%)
    ppermute x33, starting transfers between devices, swap(): return lax.ppermute(value, axis, [(i, i ^ bits) for i in range(size)])  32.4 us
    ppermute x33, waiting for transfers between devices, swap(): return lax.ppermute(value, axis, [(i, i ^ bits) for i in range(size)])  31.1 us
    pallas_call x1, Pallas kernels, query_gradient(): pl.pallas_call(grad_kernel, in_specs=[whole] * 4 + [hbm] * 3, out_specs=[...  7.75 us
    pallas_call x3, Pallas kernels, columns(): pl.pallas_call(functools.partial(column_kernel, bits, [(len(p), f) for p,...  7.25 us
    pallas_call x1, Pallas kernels, raw_score_call(): pl.pallas_call(functools.partial(score_kernel, bits), in_specs=[vmem] * l...  2.79 us
  transfers between devices with their start and end apart: 33, of which 12 were waited for; matrix products, arithmetic and copies ran while one was open for 2% of the time, Pallas kernels for 21%

profile of v2, /device:TPU:0, one launch (start us, length us, event | category | flops | bytes accessed | tf_op | source)
XLA Modules:
  0.0 86.6 jit_solution(11847256998364407918)
XLA Ops:
  1.1 2.7 %collective-permute-start.2 = (bf16[256,1024]{1,0:T(8,128)(2,1)}, bf16[256,1024]{1,0:T(8,128)(2,1)S(1)}, u32[]{:S(2)}, u32[]{:S(2)}) collective-permute-start(bf16[256,1024]{1,0:T(8,128)(2,1)} %refs_0_.1), channel_id=1, source_target_pairs={{0,4},{1,5},{2,6},{3,7},{4,0},{5,1},{6,2},{7,3},{8,12},{9,13},{10,... | collective-permute-start | bytes 1572872 | tf_op jit(solution)/shard_map/weight_first/ppermute | solution.py:296
  3.8 1.5 %collective-permute-start.3 = (bf16[256,1024]{1,0:T(8,128)(2,1)}, bf16[256,1024]{1,0:T(8,128)(2,1)S(1)}, u32[]{:S(2)}, u32[]{:S(2)}) collective-permute-start(bf16[256,1024]{1,0:T(8,128)(2,1)} %refs_0_.1), channel_id=1, source_target_pairs={{0,2},{1,3},{2,0},{3,1},{4,6},{5,7},{6,4},{7,5},{8,10},{9,11},{10,... | collective-permute-start | bytes 1572872 | tf_op jit(solution)/shard_map/weight_first/ppermute | solution.py:296
  5.3 1.0 %constant_dynamic-slice_fusion = bf16[128,1024]{1,0:T(8,128)(2,1)S(1)} fusion(bf16[256,1024]{1,0:T(8,128)(2,1)} %refs_0_.1, s32[]{:T(128)S(6)} %select_n.3), kind=kLoop, calls=%fused_computation.9 | loop fusion | bytes 524292 | tf_op jit(solution)/shard_map/weight_first/dynamic_slice | solution.py:309
  6.3 2.7 %collective-permute-start.6 = (bf16[128,1024]{1,0:T(8,128)(2,1)S(1)}, bf16[128,1024]{1,0:T(8,128)(2,1)S(1)}, u32[]{:S(2)}, u32[]{:S(2)}) collective-permute-start(bf16[128,1024]{1,0:T(8,128)(2,1)S(1)} %constant_dynamic-slice_fusion), channel_id=1, source_target_pairs={{0,8},{1,9},{2,10},{3,11},{4,12},{5,13},{6,14},{7,15},{8,0},{9,1},... | collective-permute-start | bytes 786440 | tf_op jit(solution)/shard_map/weight_first/ppermute | solution.py:296
  9.2 7.8 %query_gradient.1 = (bf16[512,1024]{1,0:T(8,128)(2,1)}, bf16[256,128]{1,0:T(8,128)(2,1)}) custom-call(s32[1,512]{1,0:T(1,128)} %ids.1, bf16[8,64,128]{2,1,0:T(8,128)(2,1)} %bitcast.6, f32[8,64,64]{2,1,0:T(8,128)} %a_inv.1, f32[8,64,64]{2,1,0:T(8,128)} %b_inv.1, bf16[512,1024]{1,0:T(8,128)(2,1)} %up_hbm.1, bf16[512,4096]{1,0:T(8,128)(2,1)} %hid_hbm.1, ...), custom_call_target="tpu_custom_call" | custom-call | flops 1 | bytes 1 | tf_op jit(solution)/shard_map/query_gradient/pallas_call | solution.py:101
  17.0 5.1 %collective-permute-done.2.refs_1_ = bf16[256,1024]{1,0:T(8,128)(2,1)S(1)} collective-permute-done((bf16[256,1024]{1,0:T(8,128)(2,1)}, bf16[256,1024]{1,0:T(8,128)(2,1)S(1)}, u32[]{:S(2)}, u32[]{:S(2)}) %collective-permute-start.2) | collective-permute-done | bytes 524320 | tf_op jit(solution)/shard_map/weight_first/ppermute | solution.py:296
  22.2 1.8 %collective-permute-start.8 = (bf16[128,1024]{1,0:T(8,128)(2,1)S(1)}, bf16[128,1024]{1,0:T(8,128)(2,1)S(1)}, u32[]{:S(2)}, u32[]{:S(2)}) collective-permute-start(bf16[128,1024]{1,0:T(8,128)(2,1)S(1)} %get-tuple-element.61), channel_id=1, source_target_pairs={{0,2},{1,3},{2,0},{3,1},{4,6},{5,7},{6,4},{7,5},{8,10},{9,11},{10,... | collective-permute-start | bytes 786440 | tf_op jit(solution)/shard_map/weight_second/ppermute | solution.py:296
  24.3 7.2 %collective-permute-done.4.second = bf16[1,256,128]{2,1,0:T(8,128)(2,1)S(1)} collective-permute-done((bf16[1,256,128]{2,1,0:T(8,128)(2,1)}, bf16[1,256,128]{2,1,0:T(8,128)(2,1)S(1)}, u32[]{:S(2)}, u32[]{:S(2)}) %collective-permute-start.4) | collective-permute-done | bytes 65568 | tf_op jit(solution)/shard_map/query_exchange/ppermute | solution.py:296
  31.5 0.8 copy-done.3
  32.3 5.7 %collective-permute-start.5 = (bf16[2,256,128]{2,1,0:T(8,128)(2,1)S(1)}, bf16[2,256,128]{2,1,0:T(8,128)(2,1)S(1)}, u32[]{:S(2)}, u32[]{:S(2)}) collective-permute-start(bf16[2,256,128]{2,1,0:T(8,128)(2,1)S(1)} %join.2.first), channel_id=1, source_target_pairs={{0,8},{1,9},{2,10},{3,11},{4,12},{5,13},{6,14},{7,15},{8,0},{9,1},... | collective-permute-start | bytes 393224 | tf_op jit(solution)/shard_map/query_exchange/ppermute | solution.py:296
  38.0 4.3 %collective-permute-done.5.second = bf16[2,256,128]{2,1,0:T(8,128)(2,1)S(1)} collective-permute-done((bf16[2,256,128]{2,1,0:T(8,128)(2,1)S(1)}, bf16[2,256,128]{2,1,0:T(8,128)(2,1)S(1)}, u32[]{:S(2)}, u32[]{:S(2)}) %collective-permute-start.5) | collective-permute-done | bytes 131104 | tf_op jit(solution)/shard_map/query_exchange/ppermute | solution.py:296
  42.4 1.6 %collective-permute-start.14 = (bf16[4,256,128]{2,1,0:T(8,128)(2,1)S(1)}, bf16[4,256,128]{2,1,0:T(8,128)(2,1)S(1)}, u32[]{:S(2)}, u32[]{:S(2)}) collective-permute-start(bf16[4,256,128]{2,1,0:T(8,128)(2,1)S(1)} %join.3.refs_0_), channel_id=1, source_target_pairs={{0,2},{1,3},{2,0},{3,1},{4,6},{5,7},{6,4},{7,5},{8,10},{9,11},{10,... | collective-permute-start | bytes 786440 | tf_op jit(solution)/shard_map/query_exchange/ppermute | solution.py:296
  44.0 1.5 %collective-permute-start.15 = (bf16[128,1024]{1,0:T(8,128)(2,1)S(1)}, bf16[128,1024]{1,0:T(8,128)(2,1)S(1)}, u32[]{:S(2)}, u32[]{:S(2)}) collective-permute-start(bf16[128,1024]{1,0:T(8,128)(2,1)S(1)} %collective-permute-done.6.refs_0_), channel_id=1, source_target_pairs={{0,16},{16,0},{1,17},{17,1},{2,18},{18,2},{3,19},{19,3},{4,20},{20... | collective-permute-start | bytes 786440 | tf_op jit(solution)/shard_map/query_exchange/ppermute | solution.py:296
  46.5 2.6 %collective-permute-done.14.refs_1_ = bf16[4,256,128]{2,1,0:T(8,128)(2,1)S(1)} collective-permute-done((bf16[4,256,128]{2,1,0:T(8,128)(2,1)S(1)}, bf16[4,256,128]{2,1,0:T(8,128)(2,1)S(1)}, u32[]{:S(2)}, u32[]{:S(2)}) %collective-permute-start.14) | collective-permute-done | bytes 262176 | tf_op jit(solution)/shard_map/query_exchange/ppermute | solution.py:296
  49.1 1.2 %collective-permute-done.15.refs_1_ = bf16[128,1024]{1,0:T(8,128)(2,1)S(1)} collective-permute-done((bf16[128,1024]{1,0:T(8,128)(2,1)S(1)}, bf16[128,1024]{1,0:T(8,128)(2,1)S(1)}, u32[]{:S(2)}, u32[]{:S(2)}) %collective-permute-start.15) | collective-permute-done | bytes 262176 | tf_op jit(solution)/shard_map/query_exchange/ppermute | solution.py:296
  50.4 2.8 %collective-permute-done.16.refs_3_ = bf16[128,1024]{1,0:T(8,128)(2,1)S(1)} collective-permute-done((bf16[128,1024]{1,0:T(8,128)(2,1)S(1)}, bf16[128,1024]{1,0:T(8,128)(2,1)S(1)}, u32[]{:S(2)}, u32[]{:S(2)}) %collective-permute-start.16) | collective-permute-done | bytes 262176 | tf_op jit(solution)/shard_map/query_exchange/ppermute | solution.py:296
  53.7 1.0 %collective-permute-done.26.refs_3_ = bf16[4,256,128]{2,1,0:T(8,128)(2,1)S(1)} collective-permute-done((bf16[4,256,128]{2,1,0:T(8,128)(2,1)S(1)}, bf16[4,256,128]{2,1,0:T(8,128)(2,1)S(1)}, u32[]{:S(2)}, u32[]{:S(2)}) %collective-permute-start.26) | collective-permute-done | bytes 262176 | tf_op jit(solution)/shard_map/query_exchange/ppermute | solution.py:296
  54.7 2.8 %raw_scores.1 = (f32[16,32]{1,0:T(8,128)S(1)}, f32[16,128]{1,0:T(8,128)S(1)}) custom-call(bf16[4,256,128]{2,1,0:T(8,128)(2,1)S(1)} %join.3.refs_0_, bf16[4,256,128]{2,1,0:T(8,128)(2,1)S(1)} %collective-permute-done.14.refs_1_, bf16[4,256,128]{2,1,0:T(8,128)(2,1)S(1)} %collective-permute-done.25.refs_2_, ...), custom_call_target="tpu_custom_call" | custom-call | flops 1 | bytes 1 | tf_op jit(solution)/shard_map/raw_scores/pallas_call | solution.py:178
  58.1 0.8 collective-permute-done.ids
  59.4 0.6 collective-permute-start.28
  60.0 1.1 %collective-permute-start.29 = (f32[16,128]{1,0:T(8,128)S(1)}, f32[16,128]{1,0:T(8,128)S(1)}, u32[]{:S(2)}, u32[]{:S(2)}) collective-permute-start(f32[16,128]{1,0:T(8,128)S(1)} %get-tuple-element.59), channel_id=1, source_target_pairs={{0,3},{1,2},{2,1},{3,0},{4,7},{5,6},{6,5},{7,4},{8,11},{9,10},{10,... | collective-permute-start | bytes 24584 | tf_op jit(solution)/shard_map/power/ppermute | solution.py:296
  61.1 3.1 %columns_0.1 = (bf16[512,4096]{1,0:T(8,128)(2,1)}, bf16[512,256]{1,0:T(8,128)(2,1)S(1)}, bf16[512,256]{1,0:T(8,128)(2,1)S(1)}, bf16[512,256]{1,0:T(8,128)(2,1)S(1)}, bf16[512,256]{1,0:T(8,128)(2,1)S(1)}) custom-call(bf16[512,1024]{1,0:T(8,128)(2,1)S(1)} %copy-done, bf16[512,1024]{1,0:T(8,128)(2,1)S(1)} %mask.1.other, bf16[256,1024]{1,0:T(8,128)(2,1)S(1)} %copy-done.2, ...), custom_call_target="tpu_custom_call" | custom-call | flops 1 | bytes 1 | tf_op jit(solution)/shard_map/input_grad/columns_0/pallas_call | solution.py:243
  64.8 1.5 %collective-permute-start.20 = (bf16[128,1024]{1,0:T(8,128)(2,1)S(1)}, bf16[128,1024]{1,0:T(8,128)(2,1)S(1)}, u32[]{:S(2)}, u32[]{:S(2)}) collective-permute-start(bf16[128,1024]{1,0:T(8,128)(2,1)S(1)} %collective-permute-done.17.refs_0_), channel_id=1, source_target_pairs={{0,16},{16,0},{1,17},{17,1},{2,18},{18,2},{3,19},{19,3},{4,20},{20... | collective-permute-start | bytes 786440 | tf_op jit(solution)/shard_map/weight_third/ppermute | solution.py:296
  66.3 0.6 collective-permute-start.22
  67.3 1.0 %collective-permute-start.30 = (f32[16,128]{1,0:T(8,128)S(1)}, f32[16,128]{1,0:T(8,128)S(1)}, u32[]{:S(2)}, u32[]{:S(2)}) collective-permute-start(f32[16,128]{1,0:T(8,128)S(1)} %add_add_fusion), channel_id=1, source_target_pairs={{0,4},{1,5},{2,6},{3,7},{4,0},{5,1},{6,2},{7,3},{8,12},{9,13},{10,... | collective-permute-start | bytes 24584 | tf_op jit(solution)/shard_map/power/ppermute | solution.py:296
  68.3 4.8 %collective-permute-done.20.refs_1_ = bf16[128,1024]{1,0:T(8,128)(2,1)S(1)} collective-permute-done((bf16[128,1024]{1,0:T(8,128)(2,1)S(1)}, bf16[128,1024]{1,0:T(8,128)(2,1)S(1)}, u32[]{:S(2)}, u32[]{:S(2)}) %collective-permute-start.20) | collective-permute-done | bytes 262176 | tf_op jit(solution)/shard_map/weight_third/ppermute | solution.py:296
  73.1 1.6 %collective-permute-start.31 = (f32[16,128]{1,0:T(8,128)S(1)}, f32[16,128]{1,0:T(8,128)S(1)}, u32[]{:S(2)}, u32[]{:S(2)}) collective-permute-start(f32[16,128]{1,0:T(8,128)S(1)} %add_add_fusion), channel_id=1, source_target_pairs={{0,8},{1,9},{2,10},{3,11},{4,12},{5,13},{6,14},{7,15},{8,0},{9,1},... | collective-permute-start | bytes 24584 | tf_op jit(solution)/shard_map/power/ppermute | solution.py:296
  74.7 3.3 %collective-permute-start.32 = (f32[16,128]{1,0:T(8,128)S(1)}, f32[16,128]{1,0:T(8,128)S(1)}, u32[]{:S(2)}, u32[]{:S(2)}) collective-permute-start(f32[16,128]{1,0:T(8,128)S(1)} %add_add_fusion), channel_id=1, source_target_pairs={{0,12},{1,13},{2,14},{3,15},{4,8},{5,9},{6,10},{7,11},{8,4},{9,5},... | collective-permute-start | bytes 24584 | tf_op jit(solution)/shard_map/power/ppermute | solution.py:296
  78.0 2.1 %columns_1.1 = (bf16[512,4096]{1,0:T(8,128)(2,1)}, bf16[512,256]{1,0:T(8,128)(2,1)S(1)}, bf16[512,256]{1,0:T(8,128)(2,1)S(1)}) custom-call(bf16[512,1024]{1,0:T(8,128)(2,1)S(1)} %copy-done, bf16[512,1024]{1,0:T(8,128)(2,1)S(1)} %mask.1.other, bf16[128,1024]{1,0:T(8,128)(2,1)S(1)} %collective-permute-done.6.refs_0_, ...), custom_call_target="tpu_custom_call", output_to_operand_aliasing={{0}: (6, {})} | custom-call | flops 1 | bytes 1 | tf_op jit(solution)/shard_map/input_grad/columns_1/pallas_call | solution.py:243
  80.1 2.1 %columns_2.1 = (bf16[512,4096]{1,0:T(8,128)(2,1)}, bf16[512,256]{1,0:T(8,128)(2,1)S(1)}, bf16[512,256]{1,0:T(8,128)(2,1)S(1)}) custom-call(bf16[512,1024]{1,0:T(8,128)(2,1)S(1)} %copy-done, bf16[512,1024]{1,0:T(8,128)(2,1)S(1)} %mask.1.other, bf16[128,1024]{1,0:T(8,128)(2,1)S(1)} %collective-permute-done.17.refs_0_, ...), custom_call_target="tpu_custom_call", output_to_operand_aliasing={{0}: (6, {})} | custom-call | flops 1 | bytes 1 | tf_op jit(solution)/shard_map/input_grad/columns_2/pallas_call | solution.py:243
  83.5 0.7 broadcast_divide_fusion
  85.3 1.4 %place_columns.1 = bf16[512,4096]{1,0:T(8,128)(2,1)} custom-call(bf16[512,256]{1,0:T(8,128)(2,1)S(1)} %collective-permute-done.10.refs_0_, bf16[512,256]{1,0:T(8,128)(2,1)S(1)} %collective-permute-done.11.refs_1_, bf16[512,256]{1,0:T(8,128)(2,1)S(1)} %collective-permute-done.12.refs_2_, ...), custom_call_target="tpu_custom_call", output_to_operand_aliasing={{}: (8, {})} | custom-call | flops 1 | bytes 1 | tf_op jit(solution)/shard_map/input_grad/place_columns/pallas_call | solution.py:282
  (58 shorter events, 7.2 us)
Async XLA Ops:
  0.6 23.7 %collective-permute-start.1 = (bf16[512,1024]{1,0:T(8,128)(2,1)}, bf16[512,1024]{1,0:T(8,128)(2,1)S(1)}, u32[]{:S(2)}, u32[]{:S(2)}) collective-permute-start(bf16[512,1024]{1,0:T(8,128)(2,1)} %up_hbm.1), channel_id=1, source_target_pairs={{0,1},{1,0},{2,3},{3,2},{4,5},{5,4},{6,7},{7,6},{8,9},{9,8},{10,11... | collective-permute-start | bytes 3145736 | tf_op jit(solution)/shard_map/weight_first/ppermute | solution.py:296
  1.1 21.0 %collective-permute-start.2 = (bf16[256,1024]{1,0:T(8,128)(2,1)}, bf16[256,1024]{1,0:T(8,128)(2,1)S(1)}, u32[]{:S(2)}, u32[]{:S(2)}) collective-permute-start(bf16[256,1024]{1,0:T(8,128)(2,1)} %refs_0_.1), channel_id=1, source_target_pairs={{0,4},{1,5},{2,6},{3,7},{4,0},{5,1},{6,2},{7,3},{8,12},{9,13},{10,... | collective-permute-start | bytes 1572872 | tf_op jit(solution)/shard_map/weight_first/ppermute | solution.py:296
  3.8 18.3 %collective-permute-start.3 = (bf16[256,1024]{1,0:T(8,128)(2,1)}, bf16[256,1024]{1,0:T(8,128)(2,1)S(1)}, u32[]{:S(2)}, u32[]{:S(2)}) collective-permute-start(bf16[256,1024]{1,0:T(8,128)(2,1)} %refs_0_.1), channel_id=1, source_target_pairs={{0,2},{1,3},{2,0},{3,1},{4,6},{5,7},{6,4},{7,5},{8,10},{9,11},{10,... | collective-permute-start | bytes 1572872 | tf_op jit(solution)/shard_map/weight_first/ppermute | solution.py:296
  6.3 31.7 %collective-permute-start.6 = (bf16[128,1024]{1,0:T(8,128)(2,1)S(1)}, bf16[128,1024]{1,0:T(8,128)(2,1)S(1)}, u32[]{:S(2)}, u32[]{:S(2)}) collective-permute-start(bf16[128,1024]{1,0:T(8,128)(2,1)S(1)} %constant_dynamic-slice_fusion), channel_id=1, source_target_pairs={{0,8},{1,9},{2,10},{3,11},{4,12},{5,13},{6,14},{7,15},{8,0},{9,1},... | collective-permute-start | bytes 786440 | tf_op jit(solution)/shard_map/weight_first/ppermute | solution.py:296
  9.0 29.0 %collective-permute-start.7 = (bf16[128,1024]{1,0:T(8,128)(2,1)S(1)}, bf16[128,1024]{1,0:T(8,128)(2,1)S(1)}, u32[]{:S(2)}, u32[]{:S(2)}) collective-permute-start(bf16[128,1024]{1,0:T(8,128)(2,1)S(1)} %constant_dynamic-slice_fusion), channel_id=1, source_target_pairs={{0,12},{1,13},{2,14},{3,15},{4,8},{5,9},{6,10},{7,11},{8,4},{9,5},... | collective-permute-start | bytes 786440 | tf_op jit(solution)/shard_map/weight_first/ppermute | solution.py:296
  22.2 15.8 %collective-permute-start.8 = (bf16[128,1024]{1,0:T(8,128)(2,1)S(1)}, bf16[128,1024]{1,0:T(8,128)(2,1)S(1)}, u32[]{:S(2)}, u32[]{:S(2)}) collective-permute-start(bf16[128,1024]{1,0:T(8,128)(2,1)S(1)} %get-tuple-element.61), channel_id=1, source_target_pairs={{0,2},{1,3},{2,0},{3,1},{4,6},{5,7},{6,4},{7,5},{8,10},{9,11},{10,... | collective-permute-start | bytes 786440 | tf_op jit(solution)/shard_map/weight_second/ppermute | solution.py:296
  24.0 14.1 %collective-permute-start.9 = (bf16[128,1024]{1,0:T(8,128)(2,1)S(1)}, bf16[128,1024]{1,0:T(8,128)(2,1)S(1)}, u32[]{:S(2)}, u32[]{:S(2)}) collective-permute-start(bf16[128,1024]{1,0:T(8,128)(2,1)S(1)} %get-tuple-element.60), channel_id=1, source_target_pairs={{0,2},{1,3},{2,0},{3,1},{4,6},{5,7},{6,4},{7,5},{8,10},{9,11},{10,... | collective-permute-start | bytes 786440 | tf_op jit(solution)/shard_map/weight_second/ppermute | solution.py:296
  24.3 7.2 %collective-permute-start.4 = (bf16[1,256,128]{2,1,0:T(8,128)(2,1)}, bf16[1,256,128]{2,1,0:T(8,128)(2,1)S(1)}, u32[]{:S(2)}, u32[]{:S(2)}) collective-permute-start(bf16[1,256,128]{2,1,0:T(8,128)(2,1)} %bitcast.3), channel_id=1, source_target_pairs={{0,4},{1,5},{2,6},{3,7},{4,0},{5,1},{6,2},{7,3},{8,12},{9,13},{10,... | collective-permute-start | bytes 196616 | tf_op jit(solution)/shard_map/query_exchange/ppermute | solution.py:296
  32.3 10.0 %collective-permute-start.5 = (bf16[2,256,128]{2,1,0:T(8,128)(2,1)S(1)}, bf16[2,256,128]{2,1,0:T(8,128)(2,1)S(1)}, u32[]{:S(2)}, u32[]{:S(2)}) collective-permute-start(bf16[2,256,128]{2,1,0:T(8,128)(2,1)S(1)} %join.2.first), channel_id=1, source_target_pairs={{0,8},{1,9},{2,10},{3,11},{4,12},{5,13},{6,14},{7,15},{8,0},{9,1},... | collective-permute-start | bytes 393224 | tf_op jit(solution)/shard_map/query_exchange/ppermute | solution.py:296
  42.4 6.7 %collective-permute-start.14 = (bf16[4,256,128]{2,1,0:T(8,128)(2,1)S(1)}, bf16[4,256,128]{2,1,0:T(8,128)(2,1)S(1)}, u32[]{:S(2)}, u32[]{:S(2)}) collective-permute-start(bf16[4,256,128]{2,1,0:T(8,128)(2,1)S(1)} %join.3.refs_0_), channel_id=1, source_target_pairs={{0,2},{1,3},{2,0},{3,1},{4,6},{5,7},{6,4},{7,5},{8,10},{9,11},{10,... | collective-permute-start | bytes 786440 | tf_op jit(solution)/shard_map/query_exchange/ppermute | solution.py:296
  44.0 6.4 %collective-permute-start.15 = (bf16[128,1024]{1,0:T(8,128)(2,1)S(1)}, bf16[128,1024]{1,0:T(8,128)(2,1)S(1)}, u32[]{:S(2)}, u32[]{:S(2)}) collective-permute-start(bf16[128,1024]{1,0:T(8,128)(2,1)S(1)} %collective-permute-done.6.refs_0_), channel_id=1, source_target_pairs={{0,16},{16,0},{1,17},{17,1},{2,18},{18,2},{3,19},{19,3},{4,20},{20... | collective-permute-start | bytes 786440 | tf_op jit(solution)/shard_map/query_exchange/ppermute | solution.py:296
  45.5 7.7 %collective-permute-start.16 = (bf16[128,1024]{1,0:T(8,128)(2,1)S(1)}, bf16[128,1024]{1,0:T(8,128)(2,1)S(1)}, u32[]{:S(2)}, u32[]{:S(2)}) collective-permute-start(bf16[128,1024]{1,0:T(8,128)(2,1)S(1)} %collective-permute-done.7.refs_2_), channel_id=1, source_target_pairs={{0,16},{16,0},{1,17},{17,1},{2,18},{18,2},{3,19},{19,3},{4,20},{20... | collective-permute-start | bytes 786440 | tf_op jit(solution)/shard_map/query_exchange/ppermute | solution.py:296
  46.0 7.2 %collective-permute-start.17 = (bf16[128,1024]{1,0:T(8,128)(2,1)S(1)}, bf16[128,1024]{1,0:T(8,128)(2,1)S(1)}, u32[]{:S(2)}, u32[]{:S(2)}) collective-permute-start(bf16[128,1024]{1,0:T(8,128)(2,1)S(1)} %collective-permute-done.6.refs_0_), channel_id=1, source_target_pairs={{0,2},{1,3},{2,0},{3,1},{4,6},{5,7},{6,4},{7,5},{8,10},{9,11},{10,... | collective-permute-start | bytes 786440 | tf_op jit(solution)/shard_map/query_exchange/ppermute | solution.py:296
  46.5 7.2 %collective-permute-start.25 = (bf16[4,256,128]{2,1,0:T(8,128)(2,1)S(1)}, bf16[4,256,128]{2,1,0:T(8,128)(2,1)S(1)}, u32[]{:S(2)}, u32[]{:S(2)}) collective-permute-start(bf16[4,256,128]{2,1,0:T(8,128)(2,1)S(1)} %join.3.refs_0_), channel_id=1, source_target_pairs={{0,1},{1,0},{2,3},{3,2},{4,5},{5,4},{6,7},{7,6},{8,9},{9,8},{10,11... | collective-permute-start | bytes 786440 | tf_op jit(solution)/shard_map/query_exchange/ppermute | solution.py:296
  53.2 1.5 %collective-permute-start.26 = (bf16[4,256,128]{2,1,0:T(8,128)(2,1)S(1)}, bf16[4,256,128]{2,1,0:T(8,128)(2,1)S(1)}, u32[]{:S(2)}, u32[]{:S(2)}) collective-permute-start(bf16[4,256,128]{2,1,0:T(8,128)(2,1)S(1)} %collective-permute-done.14.refs_1_), channel_id=1, source_target_pairs={{0,1},{1,0},{2,3},{3,2},{4,5},{5,4},{6,7},{7,6},{8,9},{9,8},{10,11... | collective-permute-start | bytes 786440 | tf_op jit(solution)/shard_map/query_exchange/ppermute | solution.py:296
  53.2 11.6 %collective-permute-start.21 = (bf16[128,1024]{1,0:T(8,128)(2,1)S(1)}, bf16[128,1024]{1,0:T(8,128)(2,1)S(1)}, u32[]{:S(2)}, u32[]{:S(2)}) collective-permute-start(bf16[128,1024]{1,0:T(8,128)(2,1)S(1)} %collective-permute-done.7.refs_2_), channel_id=1, source_target_pairs={{0,2},{1,3},{2,0},{3,1},{4,6},{5,7},{6,4},{7,5},{8,10},{9,11},{10,... | collective-permute-start | bytes 786440 | tf_op jit(solution)/shard_map/weight_third/ppermute | solution.py:296
  57.5 8.7 %collective-permute-start.27 = (f32[16,128]{1,0:T(8,128)S(1)}, f32[16,128]{1,0:T(8,128)S(1)}, u32[]{:S(2)}, u32[]{:S(2)}) collective-permute-start(f32[16,128]{1,0:T(8,128)S(1)} %get-tuple-element.59), channel_id=1, source_target_pairs={{0,1},{1,0},{2,3},{3,2},{4,5},{5,4},{6,7},{7,6},{8,9},{9,8},{10,11... | collective-permute-start | bytes 24584 | tf_op jit(solution)/shard_map/power/ppermute | solution.py:296
  59.4 7.5 %collective-permute-start.28 = (f32[16,128]{1,0:T(8,128)S(1)}, f32[16,128]{1,0:T(8,128)S(1)}, u32[]{:S(2)}, u32[]{:S(2)}) collective-permute-start(f32[16,128]{1,0:T(8,128)S(1)} %get-tuple-element.59), channel_id=1, source_target_pairs={{0,2},{1,3},{2,0},{3,1},{4,6},{5,7},{6,4},{7,5},{8,10},{9,11},{10,... | collective-permute-start | bytes 24584 | tf_op jit(solution)/shard_map/power/ppermute | solution.py:296
  60.0 6.8 %collective-permute-start.29 = (f32[16,128]{1,0:T(8,128)S(1)}, f32[16,128]{1,0:T(8,128)S(1)}, u32[]{:S(2)}, u32[]{:S(2)}) collective-permute-start(f32[16,128]{1,0:T(8,128)S(1)} %get-tuple-element.59), channel_id=1, source_target_pairs={{0,3},{1,2},{2,1},{3,0},{4,7},{5,6},{6,5},{7,4},{8,11},{9,10},{10,... | collective-permute-start | bytes 24584 | tf_op jit(solution)/shard_map/power/ppermute | solution.py:296
  64.2 3.1 %collective-permute-start.10 = (bf16[512,256]{1,0:T(8,128)(2,1)S(1)}, bf16[512,256]{1,0:T(8,128)(2,1)S(1)}, u32[]{:S(2)}, u32[]{:S(2)}) collective-permute-start(bf16[512,256]{1,0:T(8,128)(2,1)S(1)} %get-tuple-element.39), channel_id=1, source_target_pairs={{0,1},{1,0},{2,3},{3,2},{4,5},{5,4},{6,7},{7,6},{8,9},{9,8},{10,11... | collective-permute-start | bytes 786440 | tf_op jit(solution)/shard_map/input_grad/ppermute | solution.py:296
  64.8 8.3 %collective-permute-start.20 = (bf16[128,1024]{1,0:T(8,128)(2,1)S(1)}, bf16[128,1024]{1,0:T(8,128)(2,1)S(1)}, u32[]{:S(2)}, u32[]{:S(2)}) collective-permute-start(bf16[128,1024]{1,0:T(8,128)(2,1)S(1)} %collective-permute-done.17.refs_0_), channel_id=1, source_target_pairs={{0,16},{16,0},{1,17},{17,1},{2,18},{18,2},{3,19},{19,3},{4,20},{20... | collective-permute-start | bytes 786440 | tf_op jit(solution)/shard_map/weight_third/ppermute | solution.py:296
  66.3 8.4 %collective-permute-start.22 = (bf16[128,1024]{1,0:T(8,128)(2,1)S(1)}, bf16[128,1024]{1,0:T(8,128)(2,1)S(1)}, u32[]{:S(2)}, u32[]{:S(2)}) collective-permute-start(bf16[128,1024]{1,0:T(8,128)(2,1)S(1)} %collective-permute-done.16.refs_3_), channel_id=1, source_target_pairs={{0,2},{1,3},{2,0},{3,1},{4,6},{5,7},{6,4},{7,5},{8,10},{9,11},{10,... | collective-permute-start | bytes 786440 | tf_op jit(solution)/shard_map/weight_third/ppermute | solution.py:296
  66.8 15.3 %collective-permute-start.11 = (bf16[512,256]{1,0:T(8,128)(2,1)S(1)}, bf16[512,256]{1,0:T(8,128)(2,1)S(1)}, u32[]{:S(2)}, u32[]{:S(2)}) collective-permute-start(bf16[512,256]{1,0:T(8,128)(2,1)S(1)} %get-tuple-element.40), channel_id=1, source_target_pairs={{0,1},{1,0},{2,3},{3,2},{4,5},{5,4},{6,7},{7,6},{8,9},{9,8},{10,11... | collective-permute-start | bytes 786440 | tf_op jit(solution)/shard_map/input_grad/ppermute | solution.py:296
  66.8 15.4 %collective-permute-start.12 = (bf16[512,256]{1,0:T(8,128)(2,1)S(1)}, bf16[512,256]{1,0:T(8,128)(2,1)S(1)}, u32[]{:S(2)}, u32[]{:S(2)}) collective-permute-start(bf16[512,256]{1,0:T(8,128)(2,1)S(1)} %get-tuple-element.41), channel_id=1, source_target_pairs={{0,1},{1,0},{2,3},{3,2},{4,5},{5,4},{6,7},{7,6},{8,9},{9,8},{10,11... | collective-permute-start | bytes 786440 | tf_op jit(solution)/shard_map/input_grad/ppermute | solution.py:296
  67.3 15.4 %collective-permute-start.30 = (f32[16,128]{1,0:T(8,128)S(1)}, f32[16,128]{1,0:T(8,128)S(1)}, u32[]{:S(2)}, u32[]{:S(2)}) collective-permute-start(f32[16,128]{1,0:T(8,128)S(1)} %add_add_fusion), channel_id=1, source_target_pairs={{0,4},{1,5},{2,6},{3,7},{4,0},{5,1},{6,2},{7,3},{8,12},{9,13},{10,... | collective-permute-start | bytes 24584 | tf_op jit(solution)/shard_map/power/ppermute | solution.py:296
  73.1 9.8 %collective-permute-start.31 = (f32[16,128]{1,0:T(8,128)S(1)}, f32[16,128]{1,0:T(8,128)S(1)}, u32[]{:S(2)}, u32[]{:S(2)}) collective-permute-start(f32[16,128]{1,0:T(8,128)S(1)} %add_add_fusion), channel_id=1, source_target_pairs={{0,8},{1,9},{2,10},{3,11},{4,12},{5,13},{6,14},{7,15},{8,0},{9,1},... | collective-permute-start | bytes 24584 | tf_op jit(solution)/shard_map/power/ppermute | solution.py:296
  74.7 8.6 %collective-permute-start.32 = (f32[16,128]{1,0:T(8,128)S(1)}, f32[16,128]{1,0:T(8,128)S(1)}, u32[]{:S(2)}, u32[]{:S(2)}) collective-permute-start(f32[16,128]{1,0:T(8,128)S(1)} %add_add_fusion), channel_id=1, source_target_pairs={{0,12},{1,13},{2,14},{3,15},{4,8},{5,9},{6,10},{7,11},{8,4},{9,5},... | collective-permute-start | bytes 24584 | tf_op jit(solution)/shard_map/power/ppermute | solution.py:296
  82.2 2.0 %collective-permute-start.13 = (bf16[512,256]{1,0:T(8,128)(2,1)S(1)}, bf16[512,256]{1,0:T(8,128)(2,1)S(1)}, u32[]{:S(2)}, u32[]{:S(2)}) collective-permute-start(bf16[512,256]{1,0:T(8,128)(2,1)S(1)} %get-tuple-element.42), channel_id=1, source_target_pairs={{0,1},{1,0},{2,3},{3,2},{4,5},{5,4},{6,7},{7,6},{8,9},{9,8},{10,11... | collective-permute-start | bytes 786440 | tf_op jit(solution)/shard_map/input_grad/ppermute | solution.py:296
  82.2 1.9 %collective-permute-start.18 = (bf16[512,256]{1,0:T(8,128)(2,1)S(1)}, bf16[512,256]{1,0:T(8,128)(2,1)S(1)}, u32[]{:S(2)}, u32[]{:S(2)}) collective-permute-start(bf16[512,256]{1,0:T(8,128)(2,1)S(1)} %get-tuple-element.50), channel_id=1, source_target_pairs={{0,1},{1,0},{2,3},{3,2},{4,5},{5,4},{6,7},{7,6},{8,9},{9,8},{10,11... | collective-permute-start | bytes 786440 | tf_op jit(solution)/shard_map/input_grad/ppermute | solution.py:296
  82.7 1.8 %collective-permute-start.19 = (bf16[512,256]{1,0:T(8,128)(2,1)S(1)}, bf16[512,256]{1,0:T(8,128)(2,1)S(1)}, u32[]{:S(2)}, u32[]{:S(2)}) collective-permute-start(bf16[512,256]{1,0:T(8,128)(2,1)S(1)} %get-tuple-element.51), channel_id=1, source_target_pairs={{0,1},{1,0},{2,3},{3,2},{4,5},{5,4},{6,7},{7,6},{8,9},{9,8},{10,11... | collective-permute-start | bytes 786440 | tf_op jit(solution)/shard_map/input_grad/ppermute | solution.py:296
  82.8 2.1 %collective-permute-start.23 = (bf16[512,256]{1,0:T(8,128)(2,1)S(1)}, bf16[512,256]{1,0:T(8,128)(2,1)S(1)}, u32[]{:S(2)}, u32[]{:S(2)}) collective-permute-start(bf16[512,256]{1,0:T(8,128)(2,1)S(1)} %get-tuple-element.54), channel_id=1, source_target_pairs={{0,1},{1,0},{2,3},{3,2},{4,5},{5,4},{6,7},{7,6},{8,9},{9,8},{10,11... | collective-permute-start | bytes 786440 | tf_op jit(solution)/shard_map/input_grad/ppermute | solution.py:296
  83.3 2.0 %collective-permute-start.24 = (bf16[512,256]{1,0:T(8,128)(2,1)S(1)}, bf16[512,256]{1,0:T(8,128)(2,1)S(1)}, u32[]{:S(2)}, u32[]{:S(2)}) collective-permute-start(bf16[512,256]{1,0:T(8,128)(2,1)S(1)} %get-tuple-element.55), channel_id=1, source_target_pairs={{0,1},{1,0},{2,3},{3,2},{4,5},{5,4},{6,7},{7,6},{8,9},{9,8},{10,11... | collective-permute-start | bytes 786440 | tf_op jit(solution)/shard_map/input_grad/ppermute | solution.py:296
  (6 other events, 187.2 us)

commit v3 on v2

--- a/solution.py
+++ b/solution.py
@@ -87,7 +87,7 @@
         mid_high, mid_low = split(mid)
         terms = jnp.concatenate([mid_high, mid_low, mid_high], axis=0)
         pre = jnp.dot(in_sides[h], terms, preferred_element_type=F32)
-        grad[h * half : (h + 1) * half, :] = jnp.concatenate(
+        grad[0, h * half : (h + 1) * half, :] = jnp.concatenate(
             [pre[:half], pre[half:]], axis=1
         ).astype(BF16)
 
@@ -104,7 +104,7 @@
         out_specs=[vmem, vmem],
         out_shape=[
             jax.ShapeDtypeStruct(upstream.shape, BF16),
-            jax.ShapeDtypeStruct((heads * rank // 2, 2 * rank), BF16),
+            jax.ShapeDtypeStruct((1, heads * rank // 2, 2 * rank), BF16),
         ],
         scratch_shapes=[
             VMEM(upstream.shape, BF16),
@@ -313,60 +313,63 @@
         upstream_other, ids_other = ring(core, upstream), ring(core, token_ids)
         near = own_half(w_value)
         beside = ring(side, w_value)
-        got = [ring(b, near if n else w_value) for n, b in enumerate(far)]
+        got = [ring(b, near) for b in far]
     masked, grad = query_gradient(
         token_ids, upstream, hidden, proj_in, proj_out, in_inverse, out_inverse
     )
     with jax.named_scope("weight_second"):
         h1, beside = after((got[0], beside), grad)
-        y1 = [ring(side, h1[:half]), ring(side, h1[half:])]
+        x1, y1 = cross(h1), ring(side, h1)
 
     with jax.named_scope("query_exchange"):
-        held, order, bit = after(grad, upstream_other)[None], [0], 4
-        while bit < size:
+        held, order, bit = after(grad, upstream_other), [0], side
+        while bit < size // 2:
             came = ring(bit, held)
-            if bit == size // 2:
-                held, came, rest, y1, beside = lax.optimization_barrier(
-                    (held, came, got[1:], y1, beside)
+            if bit == size // 4:
+                held, came, rest, x1, y1, beside = lax.optimization_barrier(
+                    (held, came, got[1:], x1, y1, beside)
                 )
             held, order = join(held, came), order + [b ^ bit for b in order]
             bit *= 2
-        came = ring(side, held)
-        xs, ys = [cross(h) for h in rest], [ring(side, h) for h in rest[:-1]]
+        came = ring(bit, held)
+        xs, ys = [cross(h) for h in rest], [ring(side, h) for h in rest]
         came, xs, ys = lax.optimization_barrier((came, xs, ys))
         groups = [held, came, ring(core, held), ring(core, came)]
-        order = [b ^ s for s in (0, side, core, side ^ core) for b in order]
+        order = [b ^ s for s in (0, bit, core, bit ^ core) for b in order]
     raw, power = raw_score_call(order, groups, datastore)
 
+    with jax.named_scope("weight_third"):
+        ds = [ring(side, x) if n % 2 else cross(y) for n, (x, y) in enumerate(zip(xs, ys))]
+        d1 = cross(y1)
+
+    shards = {0: ((w_value,), False), side: ((beside,), False), far[0]: ((h1, x1), True)}
+    for b, h, x in zip(far[1:], rest, xs):
+        shards[b] = (h, x), True
+    out, came = None, []
+    tokens = [masked, mask(ids_other, upstream_other)]
+
+    def stage_columns(n, stage, out):
+        out, away = columns(f"columns_{n}", stage, tokens, [shards[b] for b in stage], out, out_shape)
+        return out, [ring(core, a) for a in away]
+
+    stages = [[0, side] + far, [b ^ side for b in far]]
+    with jax.named_scope("input_grad"):
+        out, came = stage_columns(0, stages[0], None)
+
     with jax.named_scope("power"):
-        for bits in ([core, side, core ^ side], far):
+        for n, bits in enumerate(([core, side, core ^ side], far)):
             parts = [ring(b, power) for b in bits]
             power = power + functools.reduce(jnp.add, parts)
+            if n == 0:
+                power, ds, d1, out = lax.optimization_barrier((power, ds, d1, out))
         spread = jnp.sqrt(power[:, :1] / (datastore.shape[0] * size) + 1e-06)
 
-    with jax.named_scope("weight_third"):
-        ys.append(ring(side, rest[-1]))
-        shards = {0: ((w_value,), False), side: ((beside,), False)}
-        shards[far[0]], shards[far[0] ^ side] = ((h1,), False), (y1, False)
-        for n, (b, h, x, y) in enumerate(zip(far[1:], rest, xs, ys)):
-            d = ring(side, x) if n % 2 else cross(y)
-            shards[b], shards[b ^ side] = ((h, x), True), ((y, d), True)
-
+    shards[far[0] ^ side] = (y1, d1), True
+    for b, y, d in zip(far[1:], ys, ds):
+        shards[b ^ side] = (y, d), True
     with jax.named_scope("input_grad"):
-        masked_other = mask(ids_other, upstream_other)
-        out, came = None, []
-        stages = [[0, far[0], side, far[0] ^ side], far[1:], [b ^ side for b in far[1:]]]
-        for n, stage in enumerate(stages):
-            out, away = columns(
-                f"columns_{n}",
-                stage,
-                [masked, masked_other],
-                [shards[b] for b in stage],
-                out,
-                out_shape,
-            )
-            came += [ring(core, a) for a in away]
-        out = place_columns([core ^ b for stage in stages for b in stage], came, out)
+        out, last = stage_columns(1, stages[1], out)
+        out = place_columns([core ^ b for stage in stages for b in stage], [*came, *last], out)
     return out, raw / spread
 
 

time: 86.8 us -> 76.6 us (0.88)
  waiting for transfers between devices: 31.1 us -> 23.6 us
  starting transfers between devices: 32.4 us -> 29.5 us
    ppermute x33 -> x34, waiting for transfers between devices: 31.1 us -> 23.6 us  [swap(): return lax.ppermute(value, axis, [(i, i ^ bits) for i in range(size)])]
    ppermute x33 -> x34, starting transfers between devices: 32.4 us -> 29.5 us  [swap(): return lax.ppermute(value, axis, [(i, i ^ bits) for i in range(size)])]
    pallas_call x3 -> x2, Pallas kernels: 7.25 us -> 7.34 us  [columns(): pl.pallas_call(functools.partial(column_kernel, bits, [(len(p), f) for p,...]
  transfers between devices with their start and end apart: 33 -> 34, of which waited for: 12 -> 11; matrix products, arithmetic and copies ran while one was open for 2% -> 2% of each run, Pallas kernels for 21% -> 24%
where the time goes in v3:
time: 76.6 us; the launch traced here: 76.3 us
  starting transfers between devices  29.5 us (39%)
  waiting for transfers between devices  23.6 us (31%)
  Pallas kernels  19.7 us (26%)
  local copies, waits for them, and re-layouts  1.86 us (2%)
  other arithmetic  0.81 us (1%)
  between operations  0.8 us (1%)
    ppermute x34, starting transfers between devices, swap(): return lax.ppermute(value, axis, [(i, i ^ bits) for i in range(size)])  29.5 us
    ppermute x34, waiting for transfers between devices, swap(): return lax.ppermute(value, axis, [(i, i ^ bits) for i in range(size)])  23.6 us
    pallas_call x1, Pallas kernels, query_gradient(): pl.pallas_call(grad_kernel, in_specs=[whole] * 4 + [hbm] * 3, out_specs=[...  7.75 us
    pallas_call x2, Pallas kernels, columns(): pl.pallas_call(functools.partial(column_kernel, bits, [(len(p), f) for p,...  7.34 us
    pallas_call x1, Pallas kernels, raw_score_call(): pl.pallas_call(functools.partial(score_kernel, bits), in_specs=[vmem] * l...  2.79 us
  transfers between devices with their start and end apart: 34, of which 11 were waited for; matrix products, arithmetic and copies ran while one was open for 2% of the time, Pallas kernels for 24%

profile of v3, /device:TPU:0, one launch (start us, length us, event | category | flops | bytes accessed | tf_op | source)
XLA Modules:
  0.0 76.3 jit_solution(9265736983643639716)
XLA Ops:
  1.2 2.6 %collective-permute-start.7 = (bf16[256,1024]{1,0:T(8,128)(2,1)}, bf16[256,1024]{1,0:T(8,128)(2,1)}, u32[]{:S(2)}, u32[]{:S(2)}) collective-permute-start(bf16[256,1024]{1,0:T(8,128)(2,1)} %refs_0_.1), channel_id=1, source_target_pairs={{0,2},{1,3},{2,0},{3,1},{4,6},{5,7},{6,4},{7,5},{8,10},{9,11},{10,... | collective-permute-start | bytes 1572872 | tf_op jit(solution)/shard_map/weight_first/ppermute | solution.py:296
  3.8 1.0 %constant_dynamic-slice_fusion = bf16[128,1024]{1,0:T(8,128)(2,1)S(1)} fusion(bf16[256,1024]{1,0:T(8,128)(2,1)} %refs_0_.1, s32[]{:T(128)S(6)} %select_n.3), kind=kLoop, calls=%fused_computation.9 | loop fusion | bytes 524292 | tf_op jit(solution)/shard_map/weight_first/dynamic_slice | solution.py:309
  4.8 1.6 %collective-permute-start.6 = (bf16[128,1024]{1,0:T(8,128)(2,1)S(1)}, bf16[128,1024]{1,0:T(8,128)(2,1)S(1)}, u32[]{:S(2)}, u32[]{:S(2)}) collective-permute-start(bf16[128,1024]{1,0:T(8,128)(2,1)S(1)} %constant_dynamic-slice_fusion), channel_id=1, source_target_pairs={{0,4},{1,5},{2,6},{3,7},{4,0},{5,1},{6,2},{7,3},{8,12},{9,13},{10,... | collective-permute-start | bytes 786440 | tf_op jit(solution)/shard_map/weight_first/ppermute | solution.py:296
  6.4 2.6 %collective-permute-start.4 = (bf16[128,1024]{1,0:T(8,128)(2,1)S(1)}, bf16[128,1024]{1,0:T(8,128)(2,1)S(1)}, u32[]{:S(2)}, u32[]{:S(2)}) collective-permute-start(bf16[128,1024]{1,0:T(8,128)(2,1)S(1)} %constant_dynamic-slice_fusion), channel_id=1, source_target_pairs={{0,8},{1,9},{2,10},{3,11},{4,12},{5,13},{6,14},{7,15},{8,0},{9,1},... | collective-permute-start | bytes 786440 | tf_op jit(solution)/shard_map/weight_first/ppermute | solution.py:296
  9.2 7.8 %query_gradient.1 = (bf16[512,1024]{1,0:T(8,128)(2,1)}, bf16[1,256,128]{2,1,0:T(8,128)(2,1)}) custom-call(s32[1,512]{1,0:T(1,128)} %ids.1, bf16[8,64,128]{2,1,0:T(8,128)(2,1)} %bitcast.3, f32[8,64,64]{2,1,0:T(8,128)} %a_inv.1, f32[8,64,64]{2,1,0:T(8,128)} %b_inv.1, bf16[512,1024]{1,0:T(8,128)(2,1)} %up_hbm.1, bf16[512,4096]{1,0:T(8,128)(2,1)} %hid_hbm.1, ...), custom_call_target="tpu_custom_call" | custom-call | flops 1 | bytes 1 | tf_op jit(solution)/shard_map/query_gradient/pallas_call | solution.py:101
  17.0 1.2 %collective-permute-done.6.refs_2_ = bf16[128,1024]{1,0:T(8,128)(2,1)S(1)} collective-permute-done((bf16[128,1024]{1,0:T(8,128)(2,1)S(1)}, bf16[128,1024]{1,0:T(8,128)(2,1)S(1)}, u32[]{:S(2)}, u32[]{:S(2)}) %collective-permute-start.6) | collective-permute-done | bytes 262176 | tf_op jit(solution)/shard_map/weight_first/ppermute | solution.py:296
  18.2 1.5 %collective-permute-start.8 = (bf16[128,1024]{1,0:T(8,128)(2,1)S(1)}, bf16[128,1024]{1,0:T(8,128)(2,1)S(1)}, u32[]{:S(2)}, u32[]{:S(2)}) collective-permute-start(bf16[128,1024]{1,0:T(8,128)(2,1)S(1)} %collective-permute-done.6.refs_2_), channel_id=1, source_target_pairs={{0,16},{16,0},{1,17},{17,1},{2,18},{18,2},{3,19},{19,3},{4,20},{20... | collective-permute-start | bytes 786440 | tf_op jit(solution)/shard_map/weight_second/ppermute | solution.py:296
  20.2 1.5 %collective-permute-start.2 = (bf16[1,256,128]{2,1,0:T(8,128)(2,1)}, bf16[1,256,128]{2,1,0:T(8,128)(2,1)S(1)}, u32[]{:S(2)}, u32[]{:S(2)}) collective-permute-start(bf16[1,256,128]{2,1,0:T(8,128)(2,1)} %get-tuple-element.38.first), channel_id=1, source_target_pairs={{0,2},{1,3},{2,0},{3,1},{4,6},{5,7},{6,4},{7,5},{8,10},{9,11},{10,... | collective-permute-start | bytes 196616 | tf_op jit(solution)/shard_map/query_exchange/ppermute | solution.py:296
  21.8 6.6 %collective-permute-done.2.second = bf16[1,256,128]{2,1,0:T(8,128)(2,1)S(1)} collective-permute-done((bf16[1,256,128]{2,1,0:T(8,128)(2,1)}, bf16[1,256,128]{2,1,0:T(8,128)(2,1)S(1)}, u32[]{:S(2)}, u32[]{:S(2)}) %collective-permute-start.2) | collective-permute-done | bytes 65568 | tf_op jit(solution)/shard_map/query_exchange/ppermute | solution.py:296
  28.4 0.8 %copy-done.3 = bf16[1,256,128]{2,1,0:T(8,128)(2,1)S(1)} copy-done((bf16[1,256,128]{2,1,0:T(8,128)(2,1)S(1)}, bf16[1,256,128]{2,1,0:T(8,128)(2,1)}, u32[]{:S(2)}) %copy-start.3) | copy-done | bytes 65560
  29.3 0.5 collective-permute-start.3
  29.8 4.5 %collective-permute-done.3.second = bf16[2,256,128]{2,1,0:T(8,128)(2,1)S(1)} collective-permute-done((bf16[2,256,128]{2,1,0:T(8,128)(2,1)S(1)}, bf16[2,256,128]{2,1,0:T(8,128)(2,1)S(1)}, u32[]{:S(2)}, u32[]{:S(2)}) %collective-permute-start.3) | collective-permute-done | bytes 131104 | tf_op jit(solution)/shard_map/query_exchange/ppermute | solution.py:296
  34.3 1.6 %collective-permute-start.10 = (bf16[4,256,128]{2,1,0:T(8,128)(2,1)S(1)}, bf16[4,256,128]{2,1,0:T(8,128)(2,1)S(1)}, u32[]{:S(2)}, u32[]{:S(2)}) collective-permute-start(bf16[4,256,128]{2,1,0:T(8,128)(2,1)S(1)} %join.3.refs_0_), channel_id=1, source_target_pairs={{0,8},{1,9},{2,10},{3,11},{4,12},{5,13},{6,14},{7,15},{8,0},{9,1},... | collective-permute-start | bytes 786440 | tf_op jit(solution)/shard_map/query_exchange/ppermute | solution.py:296
  35.9 0.5 collective-permute-start.11
  36.4 1.5 %collective-permute-start.12 = (bf16[128,1024]{1,0:T(8,128)(2,1)S(1)}, bf16[128,1024]{1,0:T(8,128)(2,1)S(1)}, u32[]{:S(2)}, u32[]{:S(2)}) collective-permute-start(bf16[128,1024]{1,0:T(8,128)(2,1)S(1)} %collective-permute-done.5.refs_6_), channel_id=1, source_target_pairs={{0,16},{16,0},{1,17},{17,1},{2,18},{18,2},{3,19},{19,3},{4,20},{20... | collective-permute-start | bytes 786440 | tf_op jit(solution)/shard_map/query_exchange/ppermute | solution.py:296
  37.9 1.6 %collective-permute-start.13 = (bf16[128,1024]{1,0:T(8,128)(2,1)S(1)}, bf16[128,1024]{1,0:T(8,128)(2,1)S(1)}, u32[]{:S(2)}, u32[]{:S(2)}) collective-permute-start(bf16[128,1024]{1,0:T(8,128)(2,1)S(1)} %collective-permute-done.4.refs_4_), channel_id=1, source_target_pairs={{0,2},{1,3},{2,0},{3,1},{4,6},{5,7},{6,4},{7,5},{8,10},{9,11},{10,... | collective-permute-start | bytes 786440 | tf_op jit(solution)/shard_map/query_exchange/ppermute | solution.py:296
  39.9 6.1 %collective-permute-done.10.refs_1_ = bf16[4,256,128]{2,1,0:T(8,128)(2,1)S(1)} collective-permute-done((bf16[4,256,128]{2,1,0:T(8,128)(2,1)S(1)}, bf16[4,256,128]{2,1,0:T(8,128)(2,1)S(1)}, u32[]{:S(2)}, u32[]{:S(2)}) %collective-permute-start.10) | collective-permute-done | bytes 262176 | tf_op jit(solution)/shard_map/query_exchange/ppermute | solution.py:296
  46.1 0.9 %collective-permute-done.12.refs_7_ = bf16[128,1024]{1,0:T(8,128)(2,1)S(1)} collective-permute-done((bf16[128,1024]{1,0:T(8,128)(2,1)S(1)}, bf16[128,1024]{1,0:T(8,128)(2,1)S(1)}, u32[]{:S(2)}, u32[]{:S(2)}) %collective-permute-start.12) | collective-permute-done | bytes 262176 | tf_op jit(solution)/shard_map/query_exchange/ppermute | solution.py:296
  47.0 1.5 %collective-permute-done.14.refs_4_ = bf16[128,1024]{1,0:T(8,128)(2,1)S(1)} collective-permute-done((bf16[128,1024]{1,0:T(8,128)(2,1)S(1)}, bf16[128,1024]{1,0:T(8,128)(2,1)S(1)}, u32[]{:S(2)}, u32[]{:S(2)}) %collective-permute-start.14) | collective-permute-done | bytes 262176 | tf_op jit(solution)/shard_map/query_exchange/ppermute | solution.py:296
  48.5 1.0 %collective-permute-start.27 = (bf16[128,1024]{1,0:T(8,128)(2,1)S(1)}, bf16[128,1024]{1,0:T(8,128)(2,1)S(1)}, u32[]{:S(2)}, u32[]{:S(2)}) collective-permute-start(bf16[128,1024]{1,0:T(8,128)(2,1)S(1)} %collective-permute-done.9.refs_0_), channel_id=1, source_target_pairs={{0,16},{16,0},{1,17},{17,1},{2,18},{18,2},{3,19},{19,3},{4,20},{20... | collective-permute-start | bytes 786440 | tf_op jit(solution)/shard_map/weight_third/ppermute | solution.py:296
  50.0 2.8 %raw_scores.1 = (f32[16,32]{1,0:T(8,128)S(1)}, f32[16,128]{1,0:T(8,128)S(1)}) custom-call(bf16[4,256,128]{2,1,0:T(8,128)(2,1)S(1)} %join.3.refs_0_, bf16[4,256,128]{2,1,0:T(8,128)(2,1)S(1)} %collective-permute-done.10.refs_1_, bf16[4,256,128]{2,1,0:T(8,128)(2,1)S(1)} %collective-permute-done.20.refs_2_, ...), custom_call_target="tpu_custom_call" | custom-call | flops 1 | bytes 1 | tf_op jit(solution)/shard_map/raw_scores/pallas_call | solution.py:178
  53.4 1.0 %collective-permute-start.25 = (bf16[128,1024]{1,0:T(8,128)(2,1)S(1)}, bf16[128,1024]{1,0:T(8,128)(2,1)S(1)}, u32[]{:S(2)}, u32[]{:S(2)}) collective-permute-start(bf16[128,1024]{1,0:T(8,128)(2,1)S(1)} %collective-permute-done.13.refs_2_), channel_id=1, source_target_pairs={{0,16},{16,0},{1,17},{17,1},{2,18},{18,2},{3,19},{19,3},{4,20},{20... | collective-permute-start | bytes 786440 | tf_op jit(solution)/shard_map/weight_third/ppermute | solution.py:296
  54.5 1.0 %collective-permute-start.23 = (f32[16,128]{1,0:T(8,128)S(1)}, f32[16,128]{1,0:T(8,128)S(1)}, u32[]{:S(2)}, u32[]{:S(2)}) collective-permute-start(f32[16,128]{1,0:T(8,128)S(1)} %get-tuple-element.56), channel_id=1, source_target_pairs={{0,2},{1,3},{2,0},{3,1},{4,6},{5,7},{6,4},{7,5},{8,10},{9,11},{10,... | collective-permute-start | bytes 24584 | tf_op jit(solution)/shard_map/power/ppermute | solution.py:296
  55.5 1.0 %collective-permute-start.26 = (bf16[128,1024]{1,0:T(8,128)(2,1)S(1)}, bf16[128,1024]{1,0:T(8,128)(2,1)S(1)}, u32[]{:S(2)}, u32[]{:S(2)}) collective-permute-start(bf16[128,1024]{1,0:T(8,128)(2,1)S(1)} %collective-permute-done.12.refs_7_), channel_id=1, source_target_pairs={{0,2},{1,3},{2,0},{3,1},{4,6},{5,7},{6,4},{7,5},{8,10},{9,11},{10,... | collective-permute-start | bytes 786440 | tf_op jit(solution)/shard_map/weight_third/ppermute | solution.py:296
  56.5 1.1 %collective-permute-done.27.refs_1_ = bf16[128,1024]{1,0:T(8,128)(2,1)S(1)} collective-permute-done((bf16[128,1024]{1,0:T(8,128)(2,1)S(1)}, bf16[128,1024]{1,0:T(8,128)(2,1)S(1)}, u32[]{:S(2)}, u32[]{:S(2)}) %collective-permute-start.27) | collective-permute-done | bytes 262176 | tf_op jit(solution)/shard_map/weight_third/ppermute | solution.py:296
  58.2 4.7 %columns_0.1 = (bf16[512,4096]{1,0:T(8,128)(2,1)}, bf16[512,256]{1,0:T(8,128)(2,1)S(1)}, bf16[512,256]{1,0:T(8,128)(2,1)S(1)}, bf16[512,256]{1,0:T(8,128)(2,1)S(...) custom-call(bf16[512,1024]{1,0:T(8,128)(2,1)S(1)} %copy-done, bf16[512,1024]{1,0:T(8,128)(2,1)S(1)} %mask.1.other, ...), custom_call_target="tpu_custom_call" | custom-call | flops 1 | bytes 1 | tf_op jit(solution)/shard_map/input_grad/columns_0/pallas_call | solution.py:243
  63.0 1.2 %collective-permute-start.15 = (bf16[512,256]{1,0:T(8,128)(2,1)S(1)}, bf16[512,256]{1,0:T(8,128)(2,1)S(1)}, u32[]{:S(2)}, u32[]{:S(2)}) collective-permute-start(bf16[512,256]{1,0:T(8,128)(2,1)S(1)} %get-tuple-element.49), channel_id=1, source_target_pairs={{0,1},{1,0},{2,3},{3,2},{4,5},{5,4},{6,7},{7,6},{8,9},{9,8},{10,11... | collective-permute-start | bytes 786440 | tf_op jit(solution)/shard_map/input_grad/ppermute | solution.py:296
  64.7 1.6 %collective-permute-start.31 = (f32[16,128]{1,0:T(8,128)S(1)}, f32[16,128]{1,0:T(8,128)S(1)}, u32[]{:S(2)}, u32[]{:S(2)}) collective-permute-start(f32[16,128]{1,0:T(8,128)S(1)} %add_add_fusion), channel_id=1, source_target_pairs={{0,4},{1,5},{2,6},{3,7},{4,0},{5,1},{6,2},{7,3},{8,12},{9,13},{10,... | collective-permute-start | bytes 24584 | tf_op jit(solution)/shard_map/power/ppermute | solution.py:296
  66.7 2.5 %collective-permute-start.33 = (f32[16,128]{1,0:T(8,128)S(1)}, f32[16,128]{1,0:T(8,128)S(1)}, u32[]{:S(2)}, u32[]{:S(2)}) collective-permute-start(f32[16,128]{1,0:T(8,128)S(1)} %add_add_fusion), channel_id=1, source_target_pairs={{0,12},{1,13},{2,14},{3,15},{4,8},{5,9},{6,10},{7,11},{8,4},{9,5},... | collective-permute-start | bytes 24584 | tf_op jit(solution)/shard_map/power/ppermute | solution.py:296
  69.2 2.6 %columns_1.1 = (bf16[512,4096]{1,0:T(8,128)(2,1)}, bf16[512,256]{1,0:T(8,128)(2,1)S(1)}, bf16[512,256]{1,0:T(8,128)(2,1)S(1)}, bf16[512,256]{1,0:T(8,128)(2,1)S(1)}) custom-call(bf16[512,1024]{1,0:T(8,128)(2,1)S(1)} %copy-done, bf16[512,1024]{1,0:T(8,128)(2,1)S(1)} %mask.1.other, ...), custom_call_target="tpu_custom_call", output_to_operand_aliasing={{0}: (8, {})} | custom-call | flops 1 | bytes 1 | tf_op jit(solution)/shard_map/input_grad/columns_1/pallas_call | solution.py:243
  73.1 0.7 broadcast_divide_fusion
  74.9 1.4 %place_columns.1 = bf16[512,4096]{1,0:T(8,128)(2,1)} custom-call(bf16[512,256]{1,0:T(8,128)(2,1)S(1)} %collective-permute-done.15.refs_0_, bf16[512,256]{1,0:T(8,128)(2,1)S(1)} %collective-permute-done.16.refs_1_, bf16[512,256]{1,0:T(8,128)(2,1)S(1)} %collective-permute-done.17.refs_2_, ...), custom_call_target="tpu_custom_call", output_to_operand_aliasing={{}: (8, {})} | custom-call | flops 1 | bytes 1 | tf_op jit(solution)/shard_map/input_grad/place_columns/pallas_call | solution.py:282
  (58 shorter events, 6.7 us)
Async XLA Ops:
  0.6 19.6 %collective-permute-start.1 = (bf16[512,1024]{1,0:T(8,128)(2,1)}, bf16[512,1024]{1,0:T(8,128)(2,1)S(1)}, u32[]{:S(2)}, u32[]{:S(2)}) collective-permute-start(bf16[512,1024]{1,0:T(8,128)(2,1)} %up_hbm.1), channel_id=1, source_target_pairs={{0,1},{1,0},{2,3},{3,2},{4,5},{5,4},{6,7},{7,6},{8,9},{9,8},{10,11... | collective-permute-start | bytes 3145736 | tf_op jit(solution)/shard_map/weight_first/ppermute | solution.py:296
  1.2 17.1 %collective-permute-start.7 = (bf16[256,1024]{1,0:T(8,128)(2,1)}, bf16[256,1024]{1,0:T(8,128)(2,1)}, u32[]{:S(2)}, u32[]{:S(2)}) collective-permute-start(bf16[256,1024]{1,0:T(8,128)(2,1)} %refs_0_.1), channel_id=1, source_target_pairs={{0,2},{1,3},{2,0},{3,1},{4,6},{5,7},{6,4},{7,5},{8,10},{9,11},{10,... | collective-permute-start | bytes 1572872 | tf_op jit(solution)/shard_map/weight_first/ppermute | solution.py:296
  4.8 13.5 %collective-permute-start.6 = (bf16[128,1024]{1,0:T(8,128)(2,1)S(1)}, bf16[128,1024]{1,0:T(8,128)(2,1)S(1)}, u32[]{:S(2)}, u32[]{:S(2)}) collective-permute-start(bf16[128,1024]{1,0:T(8,128)(2,1)S(1)} %constant_dynamic-slice_fusion), channel_id=1, source_target_pairs={{0,4},{1,5},{2,6},{3,7},{4,0},{5,1},{6,2},{7,3},{8,12},{9,13},{10,... | collective-permute-start | bytes 786440 | tf_op jit(solution)/shard_map/weight_first/ppermute | solution.py:296
  6.4 23.4 %collective-permute-start.4 = (bf16[128,1024]{1,0:T(8,128)(2,1)S(1)}, bf16[128,1024]{1,0:T(8,128)(2,1)S(1)}, u32[]{:S(2)}, u32[]{:S(2)}) collective-permute-start(bf16[128,1024]{1,0:T(8,128)(2,1)S(1)} %constant_dynamic-slice_fusion), channel_id=1, source_target_pairs={{0,8},{1,9},{2,10},{3,11},{4,12},{5,13},{6,14},{7,15},{8,0},{9,1},... | collective-permute-start | bytes 786440 | tf_op jit(solution)/shard_map/weight_first/ppermute | solution.py:296
  9.0 20.8 %collective-permute-start.5 = (bf16[128,1024]{1,0:T(8,128)(2,1)S(1)}, bf16[128,1024]{1,0:T(8,128)(2,1)S(1)}, u32[]{:S(2)}, u32[]{:S(2)}) collective-permute-start(bf16[128,1024]{1,0:T(8,128)(2,1)S(1)} %constant_dynamic-slice_fusion), channel_id=1, source_target_pairs={{0,12},{1,13},{2,14},{3,15},{4,8},{5,9},{6,10},{7,11},{8,4},{9,5},... | collective-permute-start | bytes 786440 | tf_op jit(solution)/shard_map/weight_first/ppermute | solution.py:296
  18.2 11.6 %collective-permute-start.8 = (bf16[128,1024]{1,0:T(8,128)(2,1)S(1)}, bf16[128,1024]{1,0:T(8,128)(2,1)S(1)}, u32[]{:S(2)}, u32[]{:S(2)}) collective-permute-start(bf16[128,1024]{1,0:T(8,128)(2,1)S(1)} %collective-permute-done.6.refs_2_), channel_id=1, source_target_pairs={{0,16},{16,0},{1,17},{17,1},{2,18},{18,2},{3,19},{19,3},{4,20},{20... | collective-permute-start | bytes 786440 | tf_op jit(solution)/shard_map/weight_second/ppermute | solution.py:296
  19.7 10.1 %collective-permute-start.9 = (bf16[128,1024]{1,0:T(8,128)(2,1)S(1)}, bf16[128,1024]{1,0:T(8,128)(2,1)S(1)}, u32[]{:S(2)}, u32[]{:S(2)}) collective-permute-start(bf16[128,1024]{1,0:T(8,128)(2,1)S(1)} %collective-permute-done.6.refs_2_), channel_id=1, source_target_pairs={{0,2},{1,3},{2,0},{3,1},{4,6},{5,7},{6,4},{7,5},{8,10},{9,11},{10,... | collective-permute-start | bytes 786440 | tf_op jit(solution)/shard_map/weight_second/ppermute | solution.py:296
  20.2 8.2 %collective-permute-start.2 = (bf16[1,256,128]{2,1,0:T(8,128)(2,1)}, bf16[1,256,128]{2,1,0:T(8,128)(2,1)S(1)}, u32[]{:S(2)}, u32[]{:S(2)}) collective-permute-start(bf16[1,256,128]{2,1,0:T(8,128)(2,1)} %get-tuple-element.38.first), channel_id=1, source_target_pairs={{0,2},{1,3},{2,0},{3,1},{4,6},{5,7},{6,4},{7,5},{8,10},{9,11},{10,... | collective-permute-start | bytes 196616 | tf_op jit(solution)/shard_map/query_exchange/ppermute | solution.py:296
  29.3 5.0 %collective-permute-start.3 = (bf16[2,256,128]{2,1,0:T(8,128)(2,1)S(1)}, bf16[2,256,128]{2,1,0:T(8,128)(2,1)S(1)}, u32[]{:S(2)}, u32[]{:S(2)}) collective-permute-start(bf16[2,256,128]{2,1,0:T(8,128)(2,1)S(1)} %join.2.first), channel_id=1, source_target_pairs={{0,4},{1,5},{2,6},{3,7},{4,0},{5,1},{6,2},{7,3},{8,12},{9,13},{10,... | collective-permute-start | bytes 393224 | tf_op jit(solution)/shard_map/query_exchange/ppermute | solution.py:296
  34.3 11.8 %collective-permute-start.10 = (bf16[4,256,128]{2,1,0:T(8,128)(2,1)S(1)}, bf16[4,256,128]{2,1,0:T(8,128)(2,1)S(1)}, u32[]{:S(2)}, u32[]{:S(2)}) collective-permute-start(bf16[4,256,128]{2,1,0:T(8,128)(2,1)S(1)} %join.3.refs_0_), channel_id=1, source_target_pairs={{0,8},{1,9},{2,10},{3,11},{4,12},{5,13},{6,14},{7,15},{8,0},{9,1},... | collective-permute-start | bytes 786440 | tf_op jit(solution)/shard_map/query_exchange/ppermute | solution.py:296
  35.9 10.2 %collective-permute-start.11 = (bf16[128,1024]{1,0:T(8,128)(2,1)S(1)}, bf16[128,1024]{1,0:T(8,128)(2,1)S(1)}, u32[]{:S(2)}, u32[]{:S(2)}) collective-permute-start(bf16[128,1024]{1,0:T(8,128)(2,1)S(1)} %collective-permute-done.4.refs_4_), channel_id=1, source_target_pairs={{0,16},{16,0},{1,17},{17,1},{2,18},{18,2},{3,19},{19,3},{4,20},{20... | collective-permute-start | bytes 786440 | tf_op jit(solution)/shard_map/query_exchange/ppermute | solution.py:296
  36.4 10.6 %collective-permute-start.12 = (bf16[128,1024]{1,0:T(8,128)(2,1)S(1)}, bf16[128,1024]{1,0:T(8,128)(2,1)S(1)}, u32[]{:S(2)}, u32[]{:S(2)}) collective-permute-start(bf16[128,1024]{1,0:T(8,128)(2,1)S(1)} %collective-permute-done.5.refs_6_), channel_id=1, source_target_pairs={{0,16},{16,0},{1,17},{17,1},{2,18},{18,2},{3,19},{19,3},{4,20},{20... | collective-permute-start | bytes 786440 | tf_op jit(solution)/shard_map/query_exchange/ppermute | solution.py:296
  37.9 9.1 %collective-permute-start.13 = (bf16[128,1024]{1,0:T(8,128)(2,1)S(1)}, bf16[128,1024]{1,0:T(8,128)(2,1)S(1)}, u32[]{:S(2)}, u32[]{:S(2)}) collective-permute-start(bf16[128,1024]{1,0:T(8,128)(2,1)S(1)} %collective-permute-done.4.refs_4_), channel_id=1, source_target_pairs={{0,2},{1,3},{2,0},{3,1},{4,6},{5,7},{6,4},{7,5},{8,10},{9,11},{10,... | collective-permute-start | bytes 786440 | tf_op jit(solution)/shard_map/query_exchange/ppermute | solution.py:296
  39.5 9.0 %collective-permute-start.14 = (bf16[128,1024]{1,0:T(8,128)(2,1)S(1)}, bf16[128,1024]{1,0:T(8,128)(2,1)S(1)}, u32[]{:S(2)}, u32[]{:S(2)}) collective-permute-start(bf16[128,1024]{1,0:T(8,128)(2,1)S(1)} %collective-permute-done.5.refs_6_), channel_id=1, source_target_pairs={{0,2},{1,3},{2,0},{3,1},{4,6},{5,7},{6,4},{7,5},{8,10},{9,11},{10,... | collective-permute-start | bytes 786440 | tf_op jit(solution)/shard_map/query_exchange/ppermute | solution.py:296
  46.1 3.5 %collective-permute-start.20 = (bf16[4,256,128]{2,1,0:T(8,128)(2,1)S(1)}, bf16[4,256,128]{2,1,0:T(8,128)(2,1)S(1)}, u32[]{:S(2)}, u32[]{:S(2)}) collective-permute-start(bf16[4,256,128]{2,1,0:T(8,128)(2,1)S(1)} %join.3.refs_0_), channel_id=1, source_target_pairs={{0,1},{1,0},{2,3},{3,2},{4,5},{5,4},{6,7},{7,6},{8,9},{9,8},{10,11... | collective-permute-start | bytes 786440 | tf_op jit(solution)/shard_map/query_exchange/ppermute | solution.py:296
  48.5 9.1 %collective-permute-start.27 = (bf16[128,1024]{1,0:T(8,128)(2,1)S(1)}, bf16[128,1024]{1,0:T(8,128)(2,1)S(1)}, u32[]{:S(2)}, u32[]{:S(2)}) collective-permute-start(bf16[128,1024]{1,0:T(8,128)(2,1)S(1)} %collective-permute-done.9.refs_0_), channel_id=1, source_target_pairs={{0,16},{16,0},{1,17},{17,1},{2,18},{18,2},{3,19},{19,3},{4,20},{20... | collective-permute-start | bytes 786440 | tf_op jit(solution)/shard_map/weight_third/ppermute | solution.py:296
  52.8 10.1 %collective-permute-start.22 = (f32[16,128]{1,0:T(8,128)S(1)}, f32[16,128]{1,0:T(8,128)S(1)}, u32[]{:S(2)}, u32[]{:S(2)}) collective-permute-start(f32[16,128]{1,0:T(8,128)S(1)} %get-tuple-element.56), channel_id=1, source_target_pairs={{0,1},{1,0},{2,3},{3,2},{4,5},{5,4},{6,7},{7,6},{8,9},{9,8},{10,11... | collective-permute-start | bytes 24584 | tf_op jit(solution)/shard_map/power/ppermute | solution.py:296
  53.0 2.4 %collective-permute-start = (s32[1,512]{1,0:T(1,128)S(1)}, s32[1,512]{1,0:T(1,128)S(1)}, u32[]{:S(2)}, u32[]{:S(2)}) collective-permute-start(s32[1,512]{1,0:T(1,128)S(1)} %copy-done.4), channel_id=1, source_target_pairs={{0,1},{1,0},{2,3},{3,2},{4,5},{5,4},{6,7},{7,6},{8,9},{9,8},{10,11... | collective-permute-start | bytes 6152 | tf_op jit(solution)/shard_map/weight_first/ppermute | solution.py:296
  53.4 11.3 %collective-permute-start.25 = (bf16[128,1024]{1,0:T(8,128)(2,1)S(1)}, bf16[128,1024]{1,0:T(8,128)(2,1)S(1)}, u32[]{:S(2)}, u32[]{:S(2)}) collective-permute-start(bf16[128,1024]{1,0:T(8,128)(2,1)S(1)} %collective-permute-done.13.refs_2_), channel_id=1, source_target_pairs={{0,16},{16,0},{1,17},{17,1},{2,18},{18,2},{3,19},{19,3},{4,20},{20... | collective-permute-start | bytes 786440 | tf_op jit(solution)/shard_map/weight_third/ppermute | solution.py:296
  54.5 9.8 %collective-permute-start.23 = (f32[16,128]{1,0:T(8,128)S(1)}, f32[16,128]{1,0:T(8,128)S(1)}, u32[]{:S(2)}, u32[]{:S(2)}) collective-permute-start(f32[16,128]{1,0:T(8,128)S(1)} %get-tuple-element.56), channel_id=1, source_target_pairs={{0,2},{1,3},{2,0},{3,1},{4,6},{5,7},{6,4},{7,5},{8,10},{9,11},{10,... | collective-permute-start | bytes 24584 | tf_op jit(solution)/shard_map/power/ppermute | solution.py:296
  55.5 9.3 %collective-permute-start.26 = (bf16[128,1024]{1,0:T(8,128)(2,1)S(1)}, bf16[128,1024]{1,0:T(8,128)(2,1)S(1)}, u32[]{:S(2)}, u32[]{:S(2)}) collective-permute-start(bf16[128,1024]{1,0:T(8,128)(2,1)S(1)} %collective-permute-done.12.refs_7_), channel_id=1, source_target_pairs={{0,2},{1,3},{2,0},{3,1},{4,6},{5,7},{6,4},{7,5},{8,10},{9,11},{10,... | collective-permute-start | bytes 786440 | tf_op jit(solution)/shard_map/weight_third/ppermute | solution.py:296
  57.6 6.7 %collective-permute-start.24 = (f32[16,128]{1,0:T(8,128)S(1)}, f32[16,128]{1,0:T(8,128)S(1)}, u32[]{:S(2)}, u32[]{:S(2)}) collective-permute-start(f32[16,128]{1,0:T(8,128)S(1)} %get-tuple-element.56), channel_id=1, source_target_pairs={{0,3},{1,2},{2,1},{3,0},{4,7},{5,6},{6,5},{7,4},{8,11},{9,10},{10,... | collective-permute-start | bytes 24584 | tf_op jit(solution)/shard_map/power/ppermute | solution.py:296
  63.0 3.8 %collective-permute-start.15 = (bf16[512,256]{1,0:T(8,128)(2,1)S(1)}, bf16[512,256]{1,0:T(8,128)(2,1)S(1)}, u32[]{:S(2)}, u32[]{:S(2)}) collective-permute-start(bf16[512,256]{1,0:T(8,128)(2,1)S(1)} %get-tuple-element.49), channel_id=1, source_target_pairs={{0,1},{1,0},{2,3},{3,2},{4,5},{5,4},{6,7},{7,6},{8,9},{9,8},{10,11... | collective-permute-start | bytes 786440 | tf_op jit(solution)/shard_map/input_grad/ppermute | solution.py:296
  64.2 7.6 %collective-permute-start.16 = (bf16[512,256]{1,0:T(8,128)(2,1)S(1)}, bf16[512,256]{1,0:T(8,128)(2,1)S(1)}, u32[]{:S(2)}, u32[]{:S(2)}) collective-permute-start(bf16[512,256]{1,0:T(8,128)(2,1)S(1)} %get-tuple-element.50), channel_id=1, source_target_pairs={{0,1},{1,0},{2,3},{3,2},{4,5},{5,4},{6,7},{7,6},{8,9},{9,8},{10,11... | collective-permute-start | bytes 786440 | tf_op jit(solution)/shard_map/input_grad/ppermute | solution.py:296
  64.3 7.6 %collective-permute-start.17 = (bf16[512,256]{1,0:T(8,128)(2,1)S(1)}, bf16[512,256]{1,0:T(8,128)(2,1)S(1)}, u32[]{:S(2)}, u32[]{:S(2)}) collective-permute-start(bf16[512,256]{1,0:T(8,128)(2,1)S(1)} %get-tuple-element.51), channel_id=1, source_target_pairs={{0,1},{1,0},{2,3},{3,2},{4,5},{5,4},{6,7},{7,6},{8,9},{9,8},{10,11... | collective-permute-start | bytes 786440 | tf_op jit(solution)/shard_map/input_grad/ppermute | solution.py:296
  64.7 7.7 %collective-permute-start.31 = (f32[16,128]{1,0:T(8,128)S(1)}, f32[16,128]{1,0:T(8,128)S(1)}, u32[]{:S(2)}, u32[]{:S(2)}) collective-permute-start(f32[16,128]{1,0:T(8,128)S(1)} %add_add_fusion), channel_id=1, source_target_pairs={{0,4},{1,5},{2,6},{3,7},{4,0},{5,1},{6,2},{7,3},{8,12},{9,13},{10,... | collective-permute-start | bytes 24584 | tf_op jit(solution)/shard_map/power/ppermute | solution.py:296
  66.4 6.1 %collective-permute-start.32 = (f32[16,128]{1,0:T(8,128)S(1)}, f32[16,128]{1,0:T(8,128)S(1)}, u32[]{:S(2)}, u32[]{:S(2)}) collective-permute-start(f32[16,128]{1,0:T(8,128)S(1)} %add_add_fusion), channel_id=1, source_target_pairs={{0,8},{1,9},{2,10},{3,11},{4,12},{5,13},{6,14},{7,15},{8,0},{9,1},... | collective-permute-start | bytes 24584 | tf_op jit(solution)/shard_map/power/ppermute | solution.py:296
  66.7 6.2 %collective-permute-start.33 = (f32[16,128]{1,0:T(8,128)S(1)}, f32[16,128]{1,0:T(8,128)S(1)}, u32[]{:S(2)}, u32[]{:S(2)}) collective-permute-start(f32[16,128]{1,0:T(8,128)S(1)} %add_add_fusion), channel_id=1, source_target_pairs={{0,12},{1,13},{2,14},{3,15},{4,8},{5,9},{6,10},{7,11},{8,4},{9,5},... | collective-permute-start | bytes 24584 | tf_op jit(solution)/shard_map/power/ppermute | solution.py:296
  71.8 2.0 %collective-permute-start.18 = (bf16[512,256]{1,0:T(8,128)(2,1)S(1)}, bf16[512,256]{1,0:T(8,128)(2,1)S(1)}, u32[]{:S(2)}, u32[]{:S(2)}) collective-permute-start(bf16[512,256]{1,0:T(8,128)(2,1)S(1)} %get-tuple-element.52), channel_id=1, source_target_pairs={{0,1},{1,0},{2,3},{3,2},{4,5},{5,4},{6,7},{7,6},{8,9},{9,8},{10,11... | collective-permute-start | bytes 786440 | tf_op jit(solution)/shard_map/input_grad/ppermute | solution.py:296
  71.9 1.9 %collective-permute-start.19 = (bf16[512,256]{1,0:T(8,128)(2,1)S(1)}, bf16[512,256]{1,0:T(8,128)(2,1)S(1)}, u32[]{:S(2)}, u32[]{:S(2)}) collective-permute-start(bf16[512,256]{1,0:T(8,128)(2,1)S(1)} %get-tuple-element.53), channel_id=1, source_target_pairs={{0,1},{1,0},{2,3},{3,2},{4,5},{5,4},{6,7},{7,6},{8,9},{9,8},{10,11... | collective-permute-start | bytes 786440 | tf_op jit(solution)/shard_map/input_grad/ppermute | solution.py:296
  72.5 2.1 %collective-permute-start.29 = (bf16[512,256]{1,0:T(8,128)(2,1)S(1)}, bf16[512,256]{1,0:T(8,128)(2,1)S(1)}, u32[]{:S(2)}, u32[]{:S(2)}) collective-permute-start(bf16[512,256]{1,0:T(8,128)(2,1)S(1)} %get-tuple-element.65), channel_id=1, source_target_pairs={{0,1},{1,0},{2,3},{3,2},{4,5},{5,4},{6,7},{7,6},{8,9},{9,8},{10,11... | collective-permute-start | bytes 786440 | tf_op jit(solution)/shard_map/input_grad/ppermute | solution.py:296
  72.9 2.0 %collective-permute-start.30 = (bf16[512,256]{1,0:T(8,128)(2,1)S(1)}, bf16[512,256]{1,0:T(8,128)(2,1)S(1)}, u32[]{:S(2)}, u32[]{:S(2)}) collective-permute-start(bf16[512,256]{1,0:T(8,128)(2,1)S(1)} %get-tuple-element.66), channel_id=1, source_target_pairs={{0,1},{1,0},{2,3},{3,2},{4,5},{5,4},{6,7},{7,6},{8,9},{9,8},{10,11... | collective-permute-start | bytes 786440 | tf_op jit(solution)/shard_map/input_grad/ppermute | solution.py:296
  (7 other events, 179.9 us)

commit v4 on v3

--- a/solution.py
+++ b/solution.py
@@ -32,18 +32,6 @@
     live = jnp.sum((ids[...] != 0).astype(jnp.int32))
     row = lax.broadcasted_iota(jnp.int32, up.shape, 0)
     masked[...] = jnp.where(row < live, up[...].astype(F32), 0.0).astype(BF16)
-
-
-def mask(token_ids, upstream):
-    return pl.pallas_call(
-        mask_kernel,
-        in_specs=[pl.BlockSpec(memory_space=VMEM)] * 2,
-        out_specs=pl.BlockSpec(memory_space=VMEM),
-        out_shape=jax.ShapeDtypeStruct(upstream.shape, BF16),
-        compiler_params=params(),
-        cost_estimate=SMALL,
-        name="mask",
-    )(token_ids, upstream)
 
 
 def grad_kernel(ids, pout, a_inv, b_inv, up_hbm, hid_hbm, pin_hbm, masked, grad, up, hid, pin, sems):
@@ -205,10 +193,10 @@
 def column_kernel(bits, pieces, fresh, mine, other, *refs):
     me, grp = lax.axis_index("seq"), lax.axis_index("grp")
     shard_refs = []
-    for count, _ in pieces:
-        shard_refs.append(refs[:count])
-        refs = refs[count:]
-    out, *away, weight, tile, sems = refs[0 if fresh else 1 :]
+    for spots, _ in pieces:
+        shard_refs.append([ref if at is None else ref.at[at] for at, ref in zip(spots, refs)])
+        refs = refs[len(spots) :]
+    out, away, weight, tile, sems = refs[0 if fresh else 1 :]
     copies = []
     for k, (bit, parts) in enumerate(zip(bits, shard_refs)):
         if len(parts) == 1:
@@ -220,7 +208,7 @@
                 whole[pl.ds(pl.multiple_of(half * rows, rows), rows), :] = part[...]
         tile[k] = lax.dot_general(mine[...], whole[...], LAST, preferred_element_type=F32).astype(BF16)
         copies.append(put(tile.at[k], out, me ^ bit, sems.at[k]))
-        away[k][...] = lax.dot_general(
+        away[k] = lax.dot_general(
             other[...], whole[...], LAST, preferred_element_type=F32
         ).astype(BF16)
     for copy in copies:
@@ -229,9 +217,9 @@
 
 def columns(name, bits, tokens, shards, out, out_shape):
     vmem, hbm = pl.BlockSpec(memory_space=VMEM), pl.BlockSpec(memory_space=pltpu.HBM)
-    shards, own_first = [s[0] for s in shards], [s[1] for s in shards]
-    parts = [p for shard in shards for p in shard]
-    operands = [*tokens, *parts]
+    split_parts = [[p if isinstance(p, tuple) else (p, None) for p in shard[0]] for shard in shards]
+    pieces = [([at for _, at in parts], shard[1]) for parts, shard in zip(split_parts, shards)]
+    operands = [*tokens, *(array for parts in split_parts for array, _ in parts)]
     in_specs = [vmem] * len(operands)
     aliases = {}
     if out is not None:
@@ -239,15 +227,15 @@
         operands.append(out)
         in_specs.append(hbm)
     count, height = len(shards), out_shape[0]
-    rows, depth = sum(p.shape[0] for p in shards[0]), parts[0].shape[1]
-    made = pl.pallas_call(
-        functools.partial(
-            column_kernel, bits, [(len(p), f) for p, f in zip(shards, own_first)], out is None
-        ),
+    rows, depth = sum(array.shape[-2] for array, _ in split_parts[0]), tokens[0].shape[1]
+    return pl.pallas_call(
+        functools.partial(column_kernel, bits, pieces, out is None),
         in_specs=in_specs,
-        out_specs=[hbm] + [vmem] * count,
-        out_shape=[jax.ShapeDtypeStruct(out_shape, BF16)]
-        + [jax.ShapeDtypeStruct((height, rows), BF16)] * count,
+        out_specs=[hbm, vmem],
+        out_shape=[
+            jax.ShapeDtypeStruct(out_shape, BF16),
+            jax.ShapeDtypeStruct((count, height, rows), BF16),
+        ],
         scratch_shapes=[
             VMEM((count, rows, depth), BF16),
             VMEM((count, height, rows), BF16),
@@ -258,7 +246,6 @@
         cost_estimate=SMALL,
         name=name,
     )(*operands)
-    return made[0], made[1:]
 
 
 def put(source, out, spot, sem):
@@ -269,27 +256,36 @@
     return copy
 
 
-def place_kernel(bits, *refs):
-    (*came, _, out, sems) = refs
+def place_kernel(bits, ids, *refs):
+    (*came, _, out, tiles, sems) = refs
     me = lax.axis_index("seq")
-    copies = [put(ref, out, me ^ bit, sems.at[n]) for n, (bit, ref) in enumerate(zip(bits, came))]
+    live = jnp.sum((ids[...] != 0).astype(jnp.int32))
+    row = lax.broadcasted_iota(jnp.int32, tiles.shape[1:], 0)
+    copies = []
+    given = [ref.at[k] for ref in came for k in range(ref.shape[0])]
+    for n, (bit, ref) in enumerate(zip(bits, given)):
+        tiles[n] = jnp.where(row < live, ref[...].astype(F32), 0.0).astype(BF16)
+        copies.append(put(tiles.at[n], out, me ^ bit, sems.at[n]))
     for copy in copies:
         copy.wait()
 
 
-def place_columns(bits, came, out):
+def place_columns(bits, token_ids, came, out):
     vmem, hbm = pl.BlockSpec(memory_space=VMEM), pl.BlockSpec(memory_space=pltpu.HBM)
     return pl.pallas_call(
         functools.partial(place_kernel, bits),
-        in_specs=[vmem] * len(came) + [hbm],
+        in_specs=[vmem] * (1 + len(came)) + [hbm],
         out_specs=hbm,
         out_shape=jax.ShapeDtypeStruct(out.shape, BF16),
-        scratch_shapes=[pltpu.SemaphoreType.DMA((len(came),))],
-        input_output_aliases={len(came): 0},
+        scratch_shapes=[
+            VMEM((len(bits), *came[0].shape[1:]), BF16),
+            pltpu.SemaphoreType.DMA((len(bits),)),
+        ],
+        input_output_aliases={1 + len(came): 0},
         compiler_params=params(),
         cost_estimate=SMALL,
         name="place_columns",
-    )(*came, out)
+    )(token_ids, *came, out)
 
 
 def swap(value, axis, size, bits):
@@ -310,13 +306,21 @@
     after = lambda v, *first: lax.optimization_barrier((v, *first))[0]
 
     with jax.named_scope("weight_first"):
-        upstream_other, ids_other = ring(core, upstream), ring(core, token_ids)
+        upstream_other = ring(core, upstream)
         near = own_half(w_value)
         beside = ring(side, w_value)
         got = [ring(b, near) for b in far]
     masked, grad = query_gradient(
         token_ids, upstream, hidden, proj_in, proj_out, in_inverse, out_inverse
     )
+    stages = [[0, side, far[0]], far[1:], [b ^ side for b in far]]
+
+    def stage_columns(n, out):
+        with jax.named_scope("input_grad"):
+            tokens, each = [masked, upstream_other], [shards[b] for b in stages[n]]
+            out, away = columns(f"columns_{n}", stages[n], tokens, each, out, out_shape)
+            return out, ring(core, away)
+
     with jax.named_scope("weight_second"):
         h1, beside = after((got[0], beside), grad)
         x1, y1 = cross(h1), ring(side, h1)
@@ -331,45 +335,40 @@
                 )
             held, order = join(held, came), order + [b ^ bit for b in order]
             bit *= 2
+        shards = {0: ((w_value,), False), side: ((beside,), False), far[0]: ((h1, x1), True)}
+        out, back = stage_columns(0, None)
+        came_back = [back]
         came = ring(bit, held)
         xs, ys = [cross(h) for h in rest], [ring(side, h) for h in rest]
-        came, xs, ys = lax.optimization_barrier((came, xs, ys))
+        came, xs, ys, out = lax.optimization_barrier((came, xs, ys, out))
         groups = [held, came, ring(core, held), ring(core, came)]
         order = [b ^ s for s in (0, bit, core, bit ^ core) for b in order]
     raw, power = raw_score_call(order, groups, datastore)
 
     with jax.named_scope("weight_third"):
-        ds = [ring(side, x) if n % 2 else cross(y) for n, (x, y) in enumerate(zip(xs, ys))]
-        d1 = cross(y1)
-
-    shards = {0: ((w_value,), False), side: ((beside,), False), far[0]: ((h1, x1), True)}
-    for b, h, x in zip(far[1:], rest, xs):
-        shards[b] = (h, x), True
-    out, came = None, []
-    tokens = [masked, mask(ids_other, upstream_other)]
-
-    def stage_columns(n, stage, out):
-        out, away = columns(f"columns_{n}", stage, tokens, [shards[b] for b in stage], out, out_shape)
-        return out, [ring(core, a) for a in away]
-
-    stages = [[0, side] + far, [b ^ side for b in far]]
-    with jax.named_scope("input_grad"):
-        out, came = stage_columns(0, stages[0], None)
+        d3 = ring(side, xs[-1])
+        pair = cross(join(y1[None], ys[0][None]))
+        for b, h, x in zip(far[1:], rest, xs):
+            shards[b] = (h, x), True
+        out, back = stage_columns(1, after(out, power))
+        came_back.append(back)
 
     with jax.named_scope("power"):
-        for n, bits in enumerate(([core, side, core ^ side], far)):
+        for bits in ([core], [side], far):
             parts = [ring(b, power) for b in bits]
+            if bits == [side]:
+                power, parts, out = lax.optimization_barrier((power, parts, out))
+            if bits is far:
+                power, parts, d3, pair, out = lax.optimization_barrier((power, parts, d3, pair, out))
             power = power + functools.reduce(jnp.add, parts)
-            if n == 0:
-                power, ds, d1, out = lax.optimization_barrier((power, ds, d1, out))
         spread = jnp.sqrt(power[:, :1] / (datastore.shape[0] * size) + 1e-06)
 
-    shards[far[0] ^ side] = (y1, d1), True
-    for b, y, d in zip(far[1:], ys, ds):
-        shards[b ^ side] = (y, d), True
-    with jax.named_scope("input_grad"):
-        out, last = stage_columns(1, stages[1], out)
-        out = place_columns([core ^ b for stage in stages for b in stage], [*came, *last], out)
+    shards[far[0] ^ side] = (y1, (pair, 0)), True
+    shards[far[1] ^ side] = (ys[0], (pair, 1)), True
+    shards[far[2] ^ side] = (ys[1], d3), True
+    out, back = stage_columns(2, out)
+    came_back.append(back)
+    out = place_columns([core ^ b for stage in stages for b in stage], token_ids, came_back, out)
     return out, raw / spread
 
 
@@ -413,8 +412,7 @@
         hidden, token_ids, upstream, w_value = args[:4]
         fits = (
             groups == 2
-            and size >= 8
-            and size & (size - 1) == 0
+            and size == 16
             and token_ids.shape[0] == 1
             and w_value.shape[0] % 256 == 0
         )

time: 76.6 us -> 74.2 us (0.969)
  starting transfers between devices: 29.5 us -> 25.8 us
  local copies, waits for them, and re-layouts: 1.86 us -> 3.08 us
    ppermute x34 -> x26, starting transfers between devices: 29.5 us -> 25.8 us  [swap(): return lax.ppermute(value, axis, [(i, i ^ bits) for i in range(size)])]
    unnamed x10 -> x12, local copies, waits for them, and re-layouts: 0.86 us -> 2.08 us
    ppermute x34 -> x26, waiting for transfers between devices: 23.6 us -> 23.9 us  [swap(): return lax.ppermute(value, axis, [(i, i ^ bits) for i in range(size)])]
  transfers between devices with their start and end apart: 34 -> 26, of which waited for: 11 -> 13; matrix products, arithmetic and copies ran while one was open for 2% -> 2% of each run, Pallas kernels for 24% -> 24%
where the time goes in v4:
time: 74.2 us; the launch traced here: 74 us
  starting transfers between devices  25.8 us (35%)
  waiting for transfers between devices  23.9 us (32%)
  Pallas kernels  19.6 us (26%)
  local copies, waits for them, and re-layouts  3.08 us (4%)
  other arithmetic  0.81 us (1%)
  between operations  0.75 us (1%)
    ppermute x26, starting transfers between devices, swap(): return lax.ppermute(value, axis, [(i, i ^ bits) for i in range(size)])  25.8 us
    ppermute x26, waiting for transfers between devices, swap(): return lax.ppermute(value, axis, [(i, i ^ bits) for i in range(size)])  23.9 us
    pallas_call x1, Pallas kernels, query_gradient(): pl.pallas_call(grad_kernel, in_specs=[whole] * 4 + [hbm] * 3, out_specs=[...  7.89 us
    pallas_call x3, Pallas kernels, columns(): pl.pallas_call(functools.partial(column_kernel, bits, pieces, out is None...  7.25 us
    pallas_call x1, Pallas kernels, raw_score_call(): pl.pallas_call(functools.partial(score_kernel, bits), in_specs=[vmem] * l...  2.79 us
    unnamed x12, local copies, waits for them, and re-layouts  2.08 us
    pallas_call x1, Pallas kernels, place_columns(): pl.pallas_call(functools.partial(place_kernel, bits), in_specs=[vmem] * (...  1.59 us
  transfers between devices with their start and end apart: 26, of which 13 were waited for; matrix products, arithmetic and copies ran while one was open for 2% of the time, Pallas kernels for 24%

profile of v4, /device:TPU:0, one launch (start us, length us, event | category | flops | bytes accessed | tf_op | source)
XLA Modules:
  0.0 74.0 jit_solution(14572258481343257998)
XLA Ops:
  1.2 2.6 %collective-permute-start.6 = (bf16[256,1024]{1,0:T(8,128)(2,1)}, bf16[256,1024]{1,0:T(8,128)(2,1)S(1)}, u32[]{:S(2)}, u32[]{:S(2)}) collective-permute-start(bf16[256,1024]{1,0:T(8,128)(2,1)} %refs_0_.1), channel_id=1, source_target_pairs={{0,2},{1,3},{2,0},{3,1},{4,6},{5,7},{6,4},{7,5},{8,10},{9,11},{10,... | collective-permute-start | bytes 1572872 | tf_op jit(solution)/shard_map/weight_first/ppermute | solution.py:292
  3.8 1.0 %constant_dynamic-slice_fusion = bf16[128,1024]{1,0:T(8,128)(2,1)S(1)} fusion(bf16[256,1024]{1,0:T(8,128)(2,1)} %refs_0_.1, s32[]{:T(128)S(6)} %select_n.3), kind=kLoop, calls=%fused_computation.8 | loop fusion | bytes 524292 | tf_op jit(solution)/shard_map/weight_first/dynamic_slice | solution.py:305
  4.8 1.6 %collective-permute-start.5 = (bf16[128,1024]{1,0:T(8,128)(2,1)S(1)}, bf16[128,1024]{1,0:T(8,128)(2,1)S(1)}, u32[]{:S(2)}, u32[]{:S(2)}) collective-permute-start(bf16[128,1024]{1,0:T(8,128)(2,1)S(1)} %constant_dynamic-slice_fusion), channel_id=1, source_target_pairs={{0,4},{1,5},{2,6},{3,7},{4,0},{5,1},{6,2},{7,3},{8,12},{9,13},{10,... | collective-permute-start | bytes 786440 | tf_op jit(solution)/shard_map/weight_first/ppermute | solution.py:292
  6.4 2.6 %collective-permute-start.3 = (bf16[128,1024]{1,0:T(8,128)(2,1)S(1)}, bf16[128,1024]{1,0:T(8,128)(2,1)S(1)}, u32[]{:S(2)}, u32[]{:S(2)}) collective-permute-start(bf16[128,1024]{1,0:T(8,128)(2,1)S(1)} %constant_dynamic-slice_fusion), channel_id=1, source_target_pairs={{0,8},{1,9},{2,10},{3,11},{4,12},{5,13},{6,14},{7,15},{8,0},{9,1},... | collective-permute-start | bytes 786440 | tf_op jit(solution)/shard_map/weight_first/ppermute | solution.py:292
  9.2 7.9 %query_gradient.1 = (bf16[512,1024]{1,0:T(8,128)(2,1)}, bf16[1,256,128]{2,1,0:T(8,128)(2,1)}) custom-call(s32[1,512]{1,0:T(1,128)} %ids.3, bf16[8,64,128]{2,1,0:T(8,128)(2,1)} %bitcast.7, f32[8,64,64]{2,1,0:T(8,128)} %a_inv.1, f32[8,64,64]{2,1,0:T(8,128)} %b_inv.1, bf16[512,1024]{1,0:T(8,128)(2,1)} %up_hbm.1, bf16[512,4096]{1,0:T(8,128)(2,1)} %hid_hbm.1, ...), custom_call_target="tpu_custom_call" | custom-call | flops 1 | bytes 1 | tf_op jit(solution)/shard_map/query_gradient/pallas_call | solution.py:89
  17.1 1.1 %collective-permute-done.5.refs_2_ = bf16[128,1024]{1,0:T(8,128)(2,1)S(1)} collective-permute-done((bf16[128,1024]{1,0:T(8,128)(2,1)S(1)}, bf16[128,1024]{1,0:T(8,128)(2,1)S(1)}, u32[]{:S(2)}, u32[]{:S(2)}) %collective-permute-start.5) | collective-permute-done | bytes 262176 | tf_op jit(solution)/shard_map/weight_first/ppermute | solution.py:292
  18.2 1.5 %collective-permute-start.7 = (bf16[128,1024]{1,0:T(8,128)(2,1)S(1)}, bf16[128,1024]{1,0:T(8,128)(2,1)S(1)}, u32[]{:S(2)}, u32[]{:S(2)}) collective-permute-start(bf16[128,1024]{1,0:T(8,128)(2,1)S(1)} %collective-permute-done.5.refs_2_), channel_id=1, source_target_pairs={{0,16},{16,0},{1,17},{17,1},{2,18},{18,2},{3,19},{19,3},{4,20},{20... | collective-permute-start | bytes 786440 | tf_op jit(solution)/shard_map/weight_second/ppermute | solution.py:292
  20.2 1.5 %collective-permute-start.1 = (bf16[1,256,128]{2,1,0:T(8,128)(2,1)}, bf16[1,256,128]{2,1,0:T(8,128)(2,1)S(1)}, u32[]{:S(2)}, u32[]{:S(2)}) collective-permute-start(bf16[1,256,128]{2,1,0:T(8,128)(2,1)} %get-tuple-element.41.first), channel_id=1, source_target_pairs={{0,2},{1,3},{2,0},{3,1},{4,6},{5,7},{6,4},{7,5},{8,10},{9,11},{10,... | collective-permute-start | bytes 196616 | tf_op jit(solution)/shard_map/query_exchange/ppermute | solution.py:292
  21.8 6.6 %collective-permute-done.1.second = bf16[1,256,128]{2,1,0:T(8,128)(2,1)S(1)} collective-permute-done((bf16[1,256,128]{2,1,0:T(8,128)(2,1)}, bf16[1,256,128]{2,1,0:T(8,128)(2,1)S(1)}, u32[]{:S(2)}, u32[]{:S(2)}) %collective-permute-start.1) | collective-permute-done | bytes 65568 | tf_op jit(solution)/shard_map/query_exchange/ppermute | solution.py:292
  29.7 4.6 %collective-permute-done.2.second = bf16[2,256,128]{2,1,0:T(8,128)(2,1)S(1)} collective-permute-done((bf16[2,256,128]{2,1,0:T(8,128)(2,1)S(1)}, bf16[2,256,128]{2,1,0:T(8,128)(2,1)S(1)}, u32[]{:S(2)}, u32[]{:S(2)}) %collective-permute-start.2) | collective-permute-done | bytes 131104 | tf_op jit(solution)/shard_map/query_exchange/ppermute | solution.py:292
  34.3 1.6 %collective-permute-start.10 = (bf16[4,256,128]{2,1,0:T(8,128)(2,1)S(1)}, bf16[4,256,128]{2,1,0:T(8,128)(2,1)S(1)}, u32[]{:S(2)}, u32[]{:S(2)}) collective-permute-start(bf16[4,256,128]{2,1,0:T(8,128)(2,1)S(1)} %join.4.refs_0_), channel_id=1, source_target_pairs={{0,8},{1,9},{2,10},{3,11},{4,12},{5,13},{6,14},{7,15},{8,0},{9,1},... | collective-permute-start | bytes 786440 | tf_op jit(solution)/shard_map/query_exchange/ppermute | solution.py:292
  36.4 1.5 %collective-permute-start.12 = (bf16[128,1024]{1,0:T(8,128)(2,1)S(1)}, bf16[128,1024]{1,0:T(8,128)(2,1)S(1)}, u32[]{:S(2)}, u32[]{:S(2)}) collective-permute-start(bf16[128,1024]{1,0:T(8,128)(2,1)S(1)} %collective-permute-done.4.refs_2_), channel_id=1, source_target_pairs={{0,16},{16,0},{1,17},{17,1},{2,18},{18,2},{3,19},{19,3},{4,20},{20... | collective-permute-start | bytes 786440 | tf_op jit(solution)/shard_map/query_exchange/ppermute | solution.py:292
  37.9 1.5 %collective-permute-start.13 = (bf16[128,1024]{1,0:T(8,128)(2,1)S(1)}, bf16[128,1024]{1,0:T(8,128)(2,1)S(1)}, u32[]{:S(2)}, u32[]{:S(2)}) collective-permute-start(bf16[128,1024]{1,0:T(8,128)(2,1)S(1)} %collective-permute-done.3.refs_0_), channel_id=1, source_target_pairs={{0,2},{1,3},{2,0},{3,1},{4,6},{5,7},{6,4},{7,5},{8,10},{9,11},{10,... | collective-permute-start | bytes 786440 | tf_op jit(solution)/shard_map/query_exchange/ppermute | solution.py:292
  39.9 1.2 %copy-done = bf16[512,1024]{1,0:T(8,128)(2,1)S(1)} copy-done((bf16[512,1024]{1,0:T(8,128)(2,1)S(1)}, bf16[512,1024]{1,0:T(8,128)(2,1)}, u32[]{:S(2)}) %copy-start) | copy-done | bytes 1048600
  41.1 2.6 %columns_0.1 = (bf16[512,4096]{1,0:T(8,128)(2,1)}, bf16[3,512,256]{2,1,0:T(8,128)(2,1)S(1)}) custom-call(bf16[512,1024]{1,0:T(8,128)(2,1)S(1)} %copy-done, bf16[512,1024]{1,0:T(8,128)(2,1)S(1)} %collective-permute-done.other, bf16[256,1024]{1,0:T(8,128)(2,1)S(1)} %copy-done.3, bf16[256,1024]{1,0:T(8,128)(2,1)S(1)} %collective-permute-done.6.refs_1_, ...), custom_call_target="tpu_custom_call" | custom-call | flops 1 | bytes 1 | tf_op jit(solution)/shard_map/query_exchange/input_grad/columns_0/pallas_call | solution.py:231
  43.7 2.4 %collective-permute-done.10.refs_1_ = bf16[4,256,128]{2,1,0:T(8,128)(2,1)S(1)} collective-permute-done((bf16[4,256,128]{2,1,0:T(8,128)(2,1)S(1)}, bf16[4,256,128]{2,1,0:T(8,128)(2,1)S(1)}, u32[]{:S(2)}, u32[]{:S(2)}) %collective-permute-start.10) | collective-permute-done | bytes 262176 | tf_op jit(solution)/shard_map/query_exchange/ppermute | solution.py:292
  46.1 0.9 %collective-permute-done.12.refs_3_ = bf16[128,1024]{1,0:T(8,128)(2,1)S(1)} collective-permute-done((bf16[128,1024]{1,0:T(8,128)(2,1)S(1)}, bf16[128,1024]{1,0:T(8,128)(2,1)S(1)}, u32[]{:S(2)}, u32[]{:S(2)}) %collective-permute-start.12) | collective-permute-done | bytes 262176 | tf_op jit(solution)/shard_map/query_exchange/ppermute | solution.py:292
  47.0 1.5 %collective-permute-done.14.refs_4_ = bf16[128,1024]{1,0:T(8,128)(2,1)S(1)} collective-permute-done((bf16[128,1024]{1,0:T(8,128)(2,1)S(1)}, bf16[128,1024]{1,0:T(8,128)(2,1)S(1)}, u32[]{:S(2)}, u32[]{:S(2)}) %collective-permute-start.14) | collective-permute-done | bytes 262176 | tf_op jit(solution)/shard_map/query_exchange/ppermute | solution.py:292
  48.5 1.2 %collective-permute-start.24 = (bf16[2,128,1024]{2,1,0:T(8,128)(2,1)S(1)}, bf16[2,128,1024]{2,1,0:T(8,128)(2,1)S(1)}, u32[]{:S(2)}, u32[]{:S(2)}) collective-permute-start(bf16[2,128,1024]{2,1,0:T(8,128)(2,1)S(1)} %join.5), channel_id=1, source_target_pairs={{0,16},{16,0},{1,17},{17,1},{2,18},{18,2},{3,19},{19,3},{4,20},{20... | collective-permute-start | bytes 1572872 | tf_op jit(solution)/shard_map/weight_third/ppermute | solution.py:292
  50.2 0.9 %collective-permute-start.23 = (bf16[128,1024]{1,0:T(8,128)(2,1)S(1)}, bf16[128,1024]{1,0:T(8,128)(2,1)S(1)}, u32[]{:S(2)}, u32[]{:S(2)}) collective-permute-start(bf16[128,1024]{1,0:T(8,128)(2,1)S(1)} %collective-permute-done.12.refs_3_), channel_id=1, source_target_pairs={{0,2},{1,3},{2,0},{3,1},{4,6},{5,7},{6,4},{7,5},{8,10},{9,11},{10,... | collective-permute-start | bytes 786440 | tf_op jit(solution)/shard_map/weight_third/ppermute | solution.py:292
  51.6 2.8 %raw_scores.1 = (f32[16,32]{1,0:T(8,128)S(1)}, f32[16,128]{1,0:T(8,128)S(1)}) custom-call(bf16[4,256,128]{2,1,0:T(8,128)(2,1)S(1)} %join.4.refs_0_, bf16[4,256,128]{2,1,0:T(8,128)(2,1)S(1)} %collective-permute-done.10.refs_1_, bf16[4,256,128]{2,1,0:T(8,128)(2,1)S(1)} %collective-permute-done.15.refs_2_, ...), custom_call_target="tpu_custom_call" | custom-call | flops 1 | bytes 1 | tf_op jit(solution)/shard_map/raw_scores/pallas_call | solution.py:166
  54.6 1.0 %collective-permute-done.18 = f32[16,128]{1,0:T(8,128)S(1)} collective-permute-done((f32[16,128]{1,0:T(8,128)S(1)}, f32[16,128]{1,0:T(8,128)S(1)}, u32[]{:S(2)}, u32[]{:S(2)}) %collective-permute-start.18) | collective-permute-done | bytes 8224 | tf_op jit(solution)/shard_map/power/ppermute | solution.py:292
  55.6 0.9 %collective-permute-start.19 = (f32[16,128]{1,0:T(8,128)S(1)}, f32[16,128]{1,0:T(8,128)S(1)}, u32[]{:S(2)}, u32[]{:S(2)}) collective-permute-start(f32[16,128]{1,0:T(8,128)S(1)} %add.22), channel_id=1, source_target_pairs={{0,2},{1,3},{2,0},{3,1},{4,6},{5,7},{6,4},{7,5},{8,10},{9,11},{10,... | collective-permute-start | bytes 24584 | tf_op jit(solution)/shard_map/power/ppermute | solution.py:292
  56.5 2.1 %columns_1.1 = (bf16[512,4096]{1,0:T(8,128)(2,1)}, bf16[2,512,256]{2,1,0:T(8,128)(2,1)S(1)}) custom-call(bf16[512,1024]{1,0:T(8,128)(2,1)S(1)} %copy-done.1, bf16[512,1024]{1,0:T(8,128)(2,1)S(1)} %collective-permute-done.other, bf16[128,1024]{1,0:T(8,128)(2,1)S(1)} %collective-permute-done.3.refs_0_, ...), custom_call_target="tpu_custom_call", output_to_operand_aliasing={{0}: (6, {})} | custom-call | flops 1 | bytes 1 | tf_op jit(solution)/shard_map/weight_third/input_grad/columns_1/pallas_call | solution.py:231
  59.2 0.9 %collective-permute-start.20 = (f32[16,128]{1,0:T(8,128)S(1)}, f32[16,128]{1,0:T(8,128)S(1)}, u32[]{:S(2)}, u32[]{:S(2)}) collective-permute-start(f32[16,128]{1,0:T(8,128)S(1)} %add.23), channel_id=1, source_target_pairs={{0,4},{1,5},{2,6},{3,7},{4,0},{5,1},{6,2},{7,3},{8,12},{9,13},{10,... | collective-permute-start | bytes 24584 | tf_op jit(solution)/shard_map/power/ppermute | solution.py:292
  60.1 1.0 %collective-permute-start.21 = (f32[16,128]{1,0:T(8,128)S(1)}, f32[16,128]{1,0:T(8,128)S(1)}, u32[]{:S(2)}, u32[]{:S(2)}) collective-permute-start(f32[16,128]{1,0:T(8,128)S(1)} %add.23), channel_id=1, source_target_pairs={{0,8},{1,9},{2,10},{3,11},{4,12},{5,13},{6,14},{7,15},{8,0},{9,1},... | collective-permute-start | bytes 24584 | tf_op jit(solution)/shard_map/power/ppermute | solution.py:292
  61.2 2.5 %collective-permute-start.22 = (f32[16,128]{1,0:T(8,128)S(1)}, f32[16,128]{1,0:T(8,128)S(1)}, u32[]{:S(2)}, u32[]{:S(2)}) collective-permute-start(f32[16,128]{1,0:T(8,128)S(1)} %add.23), channel_id=1, source_target_pairs={{0,12},{1,13},{2,14},{3,15},{4,8},{5,9},{6,10},{7,11},{8,4},{9,5},... | collective-permute-start | bytes 24584 | tf_op jit(solution)/shard_map/power/ppermute | solution.py:292
  63.7 1.0 %collective-permute-done.21 = f32[16,128]{1,0:T(8,128)S(1)} collective-permute-done((f32[16,128]{1,0:T(8,128)S(1)}, f32[16,128]{1,0:T(8,128)S(1)}, u32[]{:S(2)}, u32[]{:S(2)}) %collective-permute-start.21) | collective-permute-done | bytes 8224 | tf_op jit(solution)/shard_map/power/ppermute | solution.py:292
  64.7 1.9 %collective-permute-done.22 = f32[16,128]{1,0:T(8,128)S(1)} collective-permute-done((f32[16,128]{1,0:T(8,128)S(1)}, f32[16,128]{1,0:T(8,128)S(1)}, u32[]{:S(2)}, u32[]{:S(2)}) %collective-permute-start.22) | collective-permute-done | bytes 8224 | tf_op jit(solution)/shard_map/power/ppermute | solution.py:292
  66.6 2.6 %columns_2.1 = (bf16[512,4096]{1,0:T(8,128)(2,1)}, bf16[3,512,256]{2,1,0:T(8,128)(2,1)S(1)}) custom-call(bf16[512,1024]{1,0:T(8,128)(2,1)S(1)} %copy-done.1, bf16[512,1024]{1,0:T(8,128)(2,1)S(1)} %collective-permute-done.other, bf16[128,1024]{1,0:T(8,128)(2,1)S(1)} %collective-permute-done.8.refs_0_, ...), custom_call_target="tpu_custom_call", output_to_operand_aliasing={{0}: (8, {})} | custom-call | flops 1 | bytes 1 | tf_op jit(solution)/shard_map/input_grad/columns_2/pallas_call | solution.py:231
  70.6 1.7 %collective-permute-done.17.refs_1_ = bf16[2,512,256]{2,1,0:T(8,128)(2,1)S(1)} collective-permute-done((bf16[2,512,256]{2,1,0:T(8,128)(2,1)S(1)}, bf16[2,512,256]{2,1,0:T(8,128)(2,1)S(1)}, u32[]{:S(2)}, u32[]{:S(2)}) %collective-permute-start.17) | collective-permute-done | bytes 524320 | tf_op jit(solution)/shard_map/weight_third/input_grad/ppermute | solution.py:292
  72.4 1.6 %place_columns.1 = bf16[512,4096]{1,0:T(8,128)(2,1)} custom-call(s32[1,512]{1,0:T(1,128)S(1)} %copy-done.5, bf16[3,512,256]{2,1,0:T(8,128)(2,1)S(1)} %collective-permute-done.9.refs_0_, bf16[2,512,256]{2,1,0:T(8,128)(2,1)S(1)} %collective-permute-done.17.refs_1_, ...), custom_call_target="tpu_custom_call", output_to_operand_aliasing={{}: (4, {})} | custom-call | flops 1 | bytes 1 | tf_op jit(solution)/shard_map/place_columns/pallas_call | solution.py:275
  (46 shorter events, 7.0 us)
Async XLA Ops:
  0.6 39.3 %copy-start.3 = (bf16[256,1024]{1,0:T(8,128)(2,1)S(1)}, bf16[256,1024]{1,0:T(8,128)(2,1)}, u32[]{:S(2)}) copy-start(bf16[256,1024]{1,0:T(8,128)(2,1)} %refs_0_.1) | copy-start | bytes 1572868
  0.6 19.6 %collective-permute-start = (bf16[512,1024]{1,0:T(8,128)(2,1)}, bf16[512,1024]{1,0:T(8,128)(2,1)S(1)}, u32[]{:S(2)}, u32[]{:S(2)}) collective-permute-start(bf16[512,1024]{1,0:T(8,128)(2,1)} %up_hbm.1), channel_id=1, source_target_pairs={{0,1},{1,0},{2,3},{3,2},{4,5},{5,4},{6,7},{7,6},{8,9},{9,8},{10,11... | collective-permute-start | bytes 3145736 | tf_op jit(solution)/shard_map/weight_first/ppermute | solution.py:292
  1.2 17.1 %collective-permute-start.6 = (bf16[256,1024]{1,0:T(8,128)(2,1)}, bf16[256,1024]{1,0:T(8,128)(2,1)S(1)}, u32[]{:S(2)}, u32[]{:S(2)}) collective-permute-start(bf16[256,1024]{1,0:T(8,128)(2,1)} %refs_0_.1), channel_id=1, source_target_pairs={{0,2},{1,3},{2,0},{3,1},{4,6},{5,7},{6,4},{7,5},{8,10},{9,11},{10,... | collective-permute-start | bytes 1572872 | tf_op jit(solution)/shard_map/weight_first/ppermute | solution.py:292
  4.8 13.5 %collective-permute-start.5 = (bf16[128,1024]{1,0:T(8,128)(2,1)S(1)}, bf16[128,1024]{1,0:T(8,128)(2,1)S(1)}, u32[]{:S(2)}, u32[]{:S(2)}) collective-permute-start(bf16[128,1024]{1,0:T(8,128)(2,1)S(1)} %constant_dynamic-slice_fusion), channel_id=1, source_target_pairs={{0,4},{1,5},{2,6},{3,7},{4,0},{5,1},{6,2},{7,3},{8,12},{9,13},{10,... | collective-permute-start | bytes 786440 | tf_op jit(solution)/shard_map/weight_first/ppermute | solution.py:292
  6.4 23.3 %collective-permute-start.3 = (bf16[128,1024]{1,0:T(8,128)(2,1)S(1)}, bf16[128,1024]{1,0:T(8,128)(2,1)S(1)}, u32[]{:S(2)}, u32[]{:S(2)}) collective-permute-start(bf16[128,1024]{1,0:T(8,128)(2,1)S(1)} %constant_dynamic-slice_fusion), channel_id=1, source_target_pairs={{0,8},{1,9},{2,10},{3,11},{4,12},{5,13},{6,14},{7,15},{8,0},{9,1},... | collective-permute-start | bytes 786440 | tf_op jit(solution)/shard_map/weight_first/ppermute | solution.py:292
  9.0 20.7 %collective-permute-start.4 = (bf16[128,1024]{1,0:T(8,128)(2,1)S(1)}, bf16[128,1024]{1,0:T(8,128)(2,1)S(1)}, u32[]{:S(2)}, u32[]{:S(2)}) collective-permute-start(bf16[128,1024]{1,0:T(8,128)(2,1)S(1)} %constant_dynamic-slice_fusion), channel_id=1, source_target_pairs={{0,12},{1,13},{2,14},{3,15},{4,8},{5,9},{6,10},{7,11},{8,4},{9,5},... | collective-permute-start | bytes 786440 | tf_op jit(solution)/shard_map/weight_first/ppermute | solution.py:292
  9.2 42.3 %copy-start.2 = (bf16[32,32768]{1,0:T(8,128)(2,1)S(1)}, bf16[32,32768]{1,0:T(8,128)(2,1)}, u32[]{:S(2)}) copy-start(bf16[32,32768]{1,0:T(8,128)(2,1)} %refs_4_.1) | copy-start | bytes 6291460
  18.2 11.5 %collective-permute-start.7 = (bf16[128,1024]{1,0:T(8,128)(2,1)S(1)}, bf16[128,1024]{1,0:T(8,128)(2,1)S(1)}, u32[]{:S(2)}, u32[]{:S(2)}) collective-permute-start(bf16[128,1024]{1,0:T(8,128)(2,1)S(1)} %collective-permute-done.5.refs_2_), channel_id=1, source_target_pairs={{0,16},{16,0},{1,17},{17,1},{2,18},{18,2},{3,19},{19,3},{4,20},{20... | collective-permute-start | bytes 786440 | tf_op jit(solution)/shard_map/weight_second/ppermute | solution.py:292
  19.7 10.0 %collective-permute-start.8 = (bf16[128,1024]{1,0:T(8,128)(2,1)S(1)}, bf16[128,1024]{1,0:T(8,128)(2,1)S(1)}, u32[]{:S(2)}, u32[]{:S(2)}) collective-permute-start(bf16[128,1024]{1,0:T(8,128)(2,1)S(1)} %collective-permute-done.5.refs_2_), channel_id=1, source_target_pairs={{0,2},{1,3},{2,0},{3,1},{4,6},{5,7},{6,4},{7,5},{8,10},{9,11},{10,... | collective-permute-start | bytes 786440 | tf_op jit(solution)/shard_map/weight_second/ppermute | solution.py:292
  20.2 8.2 %collective-permute-start.1 = (bf16[1,256,128]{2,1,0:T(8,128)(2,1)}, bf16[1,256,128]{2,1,0:T(8,128)(2,1)S(1)}, u32[]{:S(2)}, u32[]{:S(2)}) collective-permute-start(bf16[1,256,128]{2,1,0:T(8,128)(2,1)} %get-tuple-element.41.first), channel_id=1, source_target_pairs={{0,2},{1,3},{2,0},{3,1},{4,6},{5,7},{6,4},{7,5},{8,10},{9,11},{10,... | collective-permute-start | bytes 196616 | tf_op jit(solution)/shard_map/query_exchange/ppermute | solution.py:292
  28.4 0.8 %copy-start.4 = (bf16[1,256,128]{2,1,0:T(8,128)(2,1)S(1)}, bf16[1,256,128]{2,1,0:T(8,128)(2,1)}, u32[]{:S(2)}) copy-start(bf16[1,256,128]{2,1,0:T(8,128)(2,1)} %get-tuple-element.41.first) | copy-start | bytes 196612
  29.3 5.0 %collective-permute-start.2 = (bf16[2,256,128]{2,1,0:T(8,128)(2,1)S(1)}, bf16[2,256,128]{2,1,0:T(8,128)(2,1)S(1)}, u32[]{:S(2)}, u32[]{:S(2)}) collective-permute-start(bf16[2,256,128]{2,1,0:T(8,128)(2,1)S(1)} %join.3.first), channel_id=1, source_target_pairs={{0,4},{1,5},{2,6},{3,7},{4,0},{5,1},{6,2},{7,3},{8,12},{9,13},{10,... | collective-permute-start | bytes 393224 | tf_op jit(solution)/shard_map/query_exchange/ppermute | solution.py:292
  34.3 11.8 %collective-permute-start.10 = (bf16[4,256,128]{2,1,0:T(8,128)(2,1)S(1)}, bf16[4,256,128]{2,1,0:T(8,128)(2,1)S(1)}, u32[]{:S(2)}, u32[]{:S(2)}) collective-permute-start(bf16[4,256,128]{2,1,0:T(8,128)(2,1)S(1)} %join.4.refs_0_), channel_id=1, source_target_pairs={{0,8},{1,9},{2,10},{3,11},{4,12},{5,13},{6,14},{7,15},{8,0},{9,1},... | collective-permute-start | bytes 786440 | tf_op jit(solution)/shard_map/query_exchange/ppermute | solution.py:292
  35.9 10.2 %collective-permute-start.11 = (bf16[128,1024]{1,0:T(8,128)(2,1)S(1)}, bf16[128,1024]{1,0:T(8,128)(2,1)S(1)}, u32[]{:S(2)}, u32[]{:S(2)}) collective-permute-start(bf16[128,1024]{1,0:T(8,128)(2,1)S(1)} %collective-permute-done.3.refs_0_), channel_id=1, source_target_pairs={{0,16},{16,0},{1,17},{17,1},{2,18},{18,2},{3,19},{19,3},{4,20},{20... | collective-permute-start | bytes 786440 | tf_op jit(solution)/shard_map/query_exchange/ppermute | solution.py:292
  36.4 10.6 %collective-permute-start.12 = (bf16[128,1024]{1,0:T(8,128)(2,1)S(1)}, bf16[128,1024]{1,0:T(8,128)(2,1)S(1)}, u32[]{:S(2)}, u32[]{:S(2)}) collective-permute-start(bf16[128,1024]{1,0:T(8,128)(2,1)S(1)} %collective-permute-done.4.refs_2_), channel_id=1, source_target_pairs={{0,16},{16,0},{1,17},{17,1},{2,18},{18,2},{3,19},{19,3},{4,20},{20... | collective-permute-start | bytes 786440 | tf_op jit(solution)/shard_map/query_exchange/ppermute | solution.py:292
  37.9 9.1 %collective-permute-start.13 = (bf16[128,1024]{1,0:T(8,128)(2,1)S(1)}, bf16[128,1024]{1,0:T(8,128)(2,1)S(1)}, u32[]{:S(2)}, u32[]{:S(2)}) collective-permute-start(bf16[128,1024]{1,0:T(8,128)(2,1)S(1)} %collective-permute-done.3.refs_0_), channel_id=1, source_target_pairs={{0,2},{1,3},{2,0},{3,1},{4,6},{5,7},{6,4},{7,5},{8,10},{9,11},{10,... | collective-permute-start | bytes 786440 | tf_op jit(solution)/shard_map/query_exchange/ppermute | solution.py:292
  39.4 9.0 %collective-permute-start.14 = (bf16[128,1024]{1,0:T(8,128)(2,1)S(1)}, bf16[128,1024]{1,0:T(8,128)(2,1)S(1)}, u32[]{:S(2)}, u32[]{:S(2)}) collective-permute-start(bf16[128,1024]{1,0:T(8,128)(2,1)S(1)} %collective-permute-done.4.refs_2_), channel_id=1, source_target_pairs={{0,2},{1,3},{2,0},{3,1},{4,6},{5,7},{6,4},{7,5},{8,10},{9,11},{10,... | collective-permute-start | bytes 786440 | tf_op jit(solution)/shard_map/query_exchange/ppermute | solution.py:292
  39.9 1.2 %copy-start = (bf16[512,1024]{1,0:T(8,128)(2,1)S(1)}, bf16[512,1024]{1,0:T(8,128)(2,1)}, u32[]{:S(2)}) copy-start(bf16[512,1024]{1,0:T(8,128)(2,1)} %get-tuple-element.39.mine) | copy-start | bytes 3145732
  41.1 15.4 %copy-start.1 = (bf16[512,1024]{1,0:T(8,128)(2,1)S(1)}, bf16[512,1024]{1,0:T(8,128)(2,1)}, u32[]{:S(2)}) copy-start(bf16[512,1024]{1,0:T(8,128)(2,1)} %get-tuple-element.39.mine) | copy-start | bytes 3145732
  48.5 18.1 %collective-permute-start.24 = (bf16[2,128,1024]{2,1,0:T(8,128)(2,1)S(1)}, bf16[2,128,1024]{2,1,0:T(8,128)(2,1)S(1)}, u32[]{:S(2)}, u32[]{:S(2)}) collective-permute-start(bf16[2,128,1024]{2,1,0:T(8,128)(2,1)S(1)} %join.5), channel_id=1, source_target_pairs={{0,16},{16,0},{1,17},{17,1},{2,18},{18,2},{3,19},{19,3},{4,20},{20... | collective-permute-start | bytes 1572872 | tf_op jit(solution)/shard_map/weight_third/ppermute | solution.py:292
  49.6 1.5 %collective-permute-start.15 = (bf16[4,256,128]{2,1,0:T(8,128)(2,1)S(1)}, bf16[4,256,128]{2,1,0:T(8,128)(2,1)S(1)}, u32[]{:S(2)}, u32[]{:S(2)}) collective-permute-start(bf16[4,256,128]{2,1,0:T(8,128)(2,1)S(1)} %join.4.refs_0_), channel_id=1, source_target_pairs={{0,1},{1,0},{2,3},{3,2},{4,5},{5,4},{6,7},{7,6},{8,9},{9,8},{10,11... | collective-permute-start | bytes 786440 | tf_op jit(solution)/shard_map/query_exchange/ppermute | solution.py:292
  49.6 1.9 %collective-permute-start.16 = (bf16[4,256,128]{2,1,0:T(8,128)(2,1)S(1)}, bf16[4,256,128]{2,1,0:T(8,128)(2,1)S(1)}, u32[]{:S(2)}, u32[]{:S(2)}) collective-permute-start(bf16[4,256,128]{2,1,0:T(8,128)(2,1)S(1)} %collective-permute-done.10.refs_1_), channel_id=1, source_target_pairs={{0,1},{1,0},{2,3},{3,2},{4,5},{5,4},{6,7},{7,6},{8,9},{9,8},{10,11... | collective-permute-start | bytes 786440 | tf_op jit(solution)/shard_map/query_exchange/ppermute | solution.py:292
  50.2 13.5 %collective-permute-start.23 = (bf16[128,1024]{1,0:T(8,128)(2,1)S(1)}, bf16[128,1024]{1,0:T(8,128)(2,1)S(1)}, u32[]{:S(2)}, u32[]{:S(2)}) collective-permute-start(bf16[128,1024]{1,0:T(8,128)(2,1)S(1)} %collective-permute-done.12.refs_3_), channel_id=1, source_target_pairs={{0,2},{1,3},{2,0},{3,1},{4,6},{5,7},{6,4},{7,5},{8,10},{9,11},{10,... | collective-permute-start | bytes 786440 | tf_op jit(solution)/shard_map/weight_third/ppermute | solution.py:292
  54.4 1.2 %collective-permute-start.18 = (f32[16,128]{1,0:T(8,128)S(1)}, f32[16,128]{1,0:T(8,128)S(1)}, u32[]{:S(2)}, u32[]{:S(2)}) collective-permute-start(f32[16,128]{1,0:T(8,128)S(1)} %get-tuple-element.56), channel_id=1, source_target_pairs={{0,1},{1,0},{2,3},{3,2},{4,5},{5,4},{6,7},{7,6},{8,9},{9,8},{10,11... | collective-permute-start | bytes 24584 | tf_op jit(solution)/shard_map/power/ppermute | solution.py:292
  55.6 3.7 %collective-permute-start.19 = (f32[16,128]{1,0:T(8,128)S(1)}, f32[16,128]{1,0:T(8,128)S(1)}, u32[]{:S(2)}, u32[]{:S(2)}) collective-permute-start(f32[16,128]{1,0:T(8,128)S(1)} %add.22), channel_id=1, source_target_pairs={{0,2},{1,3},{2,0},{3,1},{4,6},{5,7},{6,4},{7,5},{8,10},{9,11},{10,... | collective-permute-start | bytes 24584 | tf_op jit(solution)/shard_map/power/ppermute | solution.py:292
  59.2 4.4 %collective-permute-start.20 = (f32[16,128]{1,0:T(8,128)S(1)}, f32[16,128]{1,0:T(8,128)S(1)}, u32[]{:S(2)}, u32[]{:S(2)}) collective-permute-start(f32[16,128]{1,0:T(8,128)S(1)} %add.23), channel_id=1, source_target_pairs={{0,4},{1,5},{2,6},{3,7},{4,0},{5,1},{6,2},{7,3},{8,12},{9,13},{10,... | collective-permute-start | bytes 24584 | tf_op jit(solution)/shard_map/power/ppermute | solution.py:292
  60.1 4.5 %collective-permute-start.21 = (f32[16,128]{1,0:T(8,128)S(1)}, f32[16,128]{1,0:T(8,128)S(1)}, u32[]{:S(2)}, u32[]{:S(2)}) collective-permute-start(f32[16,128]{1,0:T(8,128)S(1)} %add.23), channel_id=1, source_target_pairs={{0,8},{1,9},{2,10},{3,11},{4,12},{5,13},{6,14},{7,15},{8,0},{9,1},... | collective-permute-start | bytes 24584 | tf_op jit(solution)/shard_map/power/ppermute | solution.py:292
  61.2 5.4 %collective-permute-start.22 = (f32[16,128]{1,0:T(8,128)S(1)}, f32[16,128]{1,0:T(8,128)S(1)}, u32[]{:S(2)}, u32[]{:S(2)}) collective-permute-start(f32[16,128]{1,0:T(8,128)S(1)} %add.23), channel_id=1, source_target_pairs={{0,12},{1,13},{2,14},{3,15},{4,8},{5,9},{6,10},{7,11},{8,4},{9,5},... | collective-permute-start | bytes 24584 | tf_op jit(solution)/shard_map/power/ppermute | solution.py:292
  63.6 8.7 %copy-start.5 = (s32[1,512]{1,0:T(1,128)S(1)}, s32[1,512]{1,0:T(1,128)}, u32[]{:S(2)}) copy-start(s32[1,512]{1,0:T(1,128)} %ids.3) | copy-start | bytes 6148
  63.6 7.0 %collective-permute-start.9 = (bf16[3,512,256]{2,1,0:T(8,128)(2,1)S(1)}, bf16[3,512,256]{2,1,0:T(8,128)(2,1)S(1)}, u32[]{:S(2)}, u32[]{:S(2)}) collective-permute-start(bf16[3,512,256]{2,1,0:T(8,128)(2,1)S(1)} %get-tuple-element.46), channel_id=1, source_target_pairs={{0,1},{1,0},{2,3},{3,2},{4,5},{5,4},{6,7},{7,6},{8,9},{9,8},{10,11... | collective-permute-start | bytes 2359304 | tf_op jit(solution)/shard_map/query_exchange/input_grad/ppermute | solution.py:292
  69.3 3.1 %collective-permute-start.25 = (bf16[3,512,256]{2,1,0:T(8,128)(2,1)S(1)}, bf16[3,512,256]{2,1,0:T(8,128)(2,1)S(1)}, u32[]{:S(2)}, u32[]{:S(2)}) collective-permute-start(bf16[3,512,256]{2,1,0:T(8,128)(2,1)S(1)} %get-tuple-element.69), channel_id=1, source_target_pairs={{0,1},{1,0},{2,3},{3,2},{4,5},{5,4},{6,7},{7,6},{8,9},{9,8},{10,11... | collective-permute-start | bytes 2359304 | tf_op jit(solution)/shard_map/input_grad/ppermute | solution.py:292
  69.3 3.0 %collective-permute-start.17 = (bf16[2,512,256]{2,1,0:T(8,128)(2,1)S(1)}, bf16[2,512,256]{2,1,0:T(8,128)(2,1)S(1)}, u32[]{:S(2)}, u32[]{:S(2)}) collective-permute-start(bf16[2,512,256]{2,1,0:T(8,128)(2,1)S(1)} %get-tuple-element.58), channel_id=1, source_target_pairs={{0,1},{1,0},{2,3},{3,2},{4,5},{5,4},{6,7},{7,6},{8,9},{9,8},{10,11... | collective-permute-start | bytes 1572872 | tf_op jit(solution)/shard_map/weight_third/input_grad/ppermute | solution.py:292

commit v5 on v4

--- a/solution.py
+++ b/solution.py
@@ -126,6 +126,26 @@
     )(first, second)
 
 
+def pair_kernel(spots, first, second, both):
+    for n, (at, ref) in enumerate(zip(spots, (first, second))):
+        both[n] = ref[...] if at is None else ref[at]
+
+
+def pair_up(first, second):
+    given = [p if isinstance(p, tuple) else (p, None) for p in (first, second)]
+    vmem = pl.BlockSpec(memory_space=VMEM)
+    shape = (2, *given[0][0].shape[-2:])
+    return pl.pallas_call(
+        functools.partial(pair_kernel, [at for _, at in given]),
+        in_specs=[vmem, vmem],
+        out_specs=vmem,
+        out_shape=jax.ShapeDtypeStruct(shape, given[0][0].dtype),
+        compiler_params=params(),
+        cost_estimate=SMALL,
+        name="pair_up",
+    )(*(array for array, _ in given))
+
+
 def score_kernel(bits, *refs):
     *held, store_hbm, scores, power, wide, store, sems = refs
     steps, _, chunk = store.shape
@@ -190,13 +210,24 @@
     return copy
 
 
-def column_kernel(bits, pieces, fresh, mine, other, *refs):
+def column_kernel(bits, pieces, todo, fresh, *refs):
+    own, others = todo
     me, grp = lax.axis_index("seq"), lax.axis_index("grp")
+    if own:
+        mine, *refs = refs
+    if others:
+        other, *refs = refs
     shard_refs = []
     for spots, _ in pieces:
         shard_refs.append([ref if at is None else ref.at[at] for at, ref in zip(spots, refs)])
         refs = refs[len(spots) :]
-    out, away, weight, tile, sems = refs[0 if fresh else 1 :]
+    if own:
+        out, *refs = refs[0 if fresh else 1 :]
+    if others:
+        away, *refs = refs
+    weight, *refs = refs
+    if own:
+        tile, sems = refs
     copies = []
     for k, (bit, parts) in enumerate(zip(bits, shard_refs)):
         if len(parts) == 1:
@@ -206,54 +237,51 @@
             rows = parts[0].shape[0]
             for part, half in zip(parts, (grp, 1 - grp) if pieces[k][1] else (0, 1)):
                 whole[pl.ds(pl.multiple_of(half * rows, rows), rows), :] = part[...]
-        tile[k] = lax.dot_general(mine[...], whole[...], LAST, preferred_element_type=F32).astype(BF16)
-        copies.append(put(tile.at[k], out, me ^ bit, sems.at[k]))
-        away[k] = lax.dot_general(
-            other[...], whole[...], LAST, preferred_element_type=F32
-        ).astype(BF16)
+        if own:
+            made = lax.dot_general(mine[...], whole[...], LAST, preferred_element_type=F32)
+            tile[k] = made.astype(BF16)
+            copies.append(put(tile.at[k], out, me ^ bit, sems.at[k]))
+        if others:
+            made = lax.dot_general(other[...], whole[...], LAST, preferred_element_type=F32)
+            away[k] = made.astype(BF16)
     for copy in copies:
         copy.wait()
 
 
-def columns(name, bits, tokens, shards, out, out_shape):
+def columns(name, bits, mine, other, shards, out, out_shape):
+    own, others = mine is not None, other is not None
     vmem, hbm = pl.BlockSpec(memory_space=VMEM), pl.BlockSpec(memory_space=pltpu.HBM)
     split_parts = [[p if isinstance(p, tuple) else (p, None) for p in shard[0]] for shard in shards]
     pieces = [([at for _, at in parts], shard[1]) for parts, shard in zip(split_parts, shards)]
+    tokens = [t for t in (mine, other) if t is not None]
     operands = [*tokens, *(array for parts in split_parts for array, _ in parts)]
     in_specs = [vmem] * len(operands)
-    aliases = {}
-    if out is not None:
-        aliases = {len(operands): 0}
-        operands.append(out)
-        in_specs.append(hbm)
     count, height = len(shards), out_shape[0]
     rows, depth = sum(array.shape[-2] for array, _ in split_parts[0]), tokens[0].shape[1]
-    return pl.pallas_call(
-        functools.partial(column_kernel, bits, pieces, out is None),
+    tall = (count, height, rows)
+    out_specs, shapes, scratch, aliases = [], [], [VMEM((count, rows, depth), BF16)], {}
+    if own:
+        out_specs.append(hbm)
+        shapes.append(jax.ShapeDtypeStruct(out_shape, BF16))
+        scratch += [VMEM(tall, BF16), pltpu.SemaphoreType.DMA((count,))]
+        if out is not None:
+            aliases = {len(operands): 0}
+            operands.append(out)
+            in_specs.append(hbm)
+    if others:
+        out_specs.append(vmem)
+        shapes.append(jax.ShapeDtypeStruct(tall, BF16))
+    return pl.pallas_call(
+        functools.partial(column_kernel, bits, pieces, (own, others), out is None),
         in_specs=in_specs,
-        out_specs=[hbm, vmem],
-        out_shape=[
-            jax.ShapeDtypeStruct(out_shape, BF16),
-            jax.ShapeDtypeStruct((count, height, rows), BF16),
-        ],
-        scratch_shapes=[
-            VMEM((count, rows, depth), BF16),
-            VMEM((count, height, rows), BF16),
-            pltpu.SemaphoreType.DMA((count,)),
-        ],
+        out_specs=out_specs,
+        out_shape=shapes,
+        scratch_shapes=scratch,
         input_output_aliases=aliases,
         compiler_params=params(),
         cost_estimate=SMALL,
         name=name,
     )(*operands)
-
-
-def put(source, out, spot, sem):
-    width = source.shape[1]
-    col = pl.multiple_of(spot * width, width)
-    copy = pltpu.make_async_copy(source, out.at[:, pl.ds(col, width)], sem)
-    copy.start()
-    return copy
 
 
 def place_kernel(bits, ids, *refs):
@@ -308,66 +336,75 @@
     with jax.named_scope("weight_first"):
         upstream_other = ring(core, upstream)
         near = own_half(w_value)
-        beside = ring(side, w_value)
-        got = [ring(b, near) for b in far]
+        beside, h4, h8 = ring(side, w_value), ring(4, near), ring(8, near)
     masked, grad = query_gradient(
         token_ids, upstream, hidden, proj_in, proj_out, in_inverse, out_inverse
     )
-    stages = [[0, side, far[0]], far[1:], [b ^ side for b in far]]
-
-    def stage_columns(n, out):
+    stages = [[0, side], [4, 8], [12, 4 ^ side, 8 ^ side], [12 ^ side]]
+    shards = {0: ((w_value,), False)}
+
+    def stage_columns(n, out, mine=True, other=True):
         with jax.named_scope("input_grad"):
-            tokens, each = [masked, upstream_other], [shards[b] for b in stages[n]]
-            out, away = columns(f"columns_{n}", stages[n], tokens, each, out, out_shape)
-            return out, ring(core, away)
+            made = columns(
+                f"columns_{n}",
+                stages[n],
+                masked if mine else None,
+                upstream_other if other else None,
+                [shards[b] for b in stages[n]],
+                out,
+                out_shape,
+            )
+            return [*made[:-1], ring(core, made[-1])] if other else made
 
     with jax.named_scope("weight_second"):
-        h1, beside = after((got[0], beside), grad)
-        x1, y1 = cross(h1), ring(side, h1)
+        h4, h8, beside = after((h4, h8, beside), grad)
+        both = pair_up(h4, h8)
+        x48, y48, h12 = cross(both), ring(side, both), ring(4, h8)
+
+    shards[side] = (beside,), False
+    out, back = stage_columns(0, None)
+    came_back = [back]
 
     with jax.named_scope("query_exchange"):
-        held, order, bit = after(grad, upstream_other), [0], side
-        while bit < size // 2:
+        held, order = after(grad, upstream_other), [0]
+        for bit in (8, side):
             came = ring(bit, held)
-            if bit == size // 4:
-                held, came, rest, x1, y1, beside = lax.optimization_barrier(
-                    (held, came, got[1:], x1, y1, beside)
+            if bit == side:
+                held, came, x48, y48, h12, out = lax.optimization_barrier(
+                    (held, came, x48, y48, h12, out)
                 )
             held, order = join(held, came), order + [b ^ bit for b in order]
-            bit *= 2
-        shards = {0: ((w_value,), False), side: ((beside,), False), far[0]: ((h1, x1), True)}
-        out, back = stage_columns(0, None)
-        came_back = [back]
-        came = ring(bit, held)
-        xs, ys = [cross(h) for h in rest], [ring(side, h) for h in rest]
-        came, xs, ys, out = lax.optimization_barrier((came, xs, ys, out))
-        groups = [held, came, ring(core, held), ring(core, came)]
-        order = [b ^ s for s in (0, bit, core, bit ^ core) for b in order]
+        shards.update({4: ((h4, (x48, 0)), True), 8: ((h8, (x48, 1)), True)})
+        came = ring(4, held)
+        cut = came.shape[0] // 2
+        groups = [held, came, ring(core, held), ring(core, came[:cut]), ring(core, came[cut:])]
+        order = [b ^ s for s in (0, 4, core, 4 ^ core) for b in order]
     raw, power = raw_score_call(order, groups, datastore)
 
     with jax.named_scope("weight_third"):
-        d3 = ring(side, xs[-1])
-        pair = cross(join(y1[None], ys[0][None]))
-        for b, h, x in zip(far[1:], rest, xs):
-            shards[b] = (h, x), True
-        out, back = stage_columns(1, after(out, power))
-        came_back.append(back)
-
+        x12, y12 = cross(pair_up(h12, (y48, 0))), ring(side, pair_up(h12, (x48, 1)))
+
+    out, back = stage_columns(1, after(out, power))
+    came_back.append(back)
     with jax.named_scope("power"):
-        for bits in ([core], [side], far):
-            parts = [ring(b, power) for b in bits]
-            if bits == [side]:
-                power, parts, out = lax.optimization_barrier((power, parts, out))
-            if bits is far:
-                power, parts, d3, pair, out = lax.optimization_barrier((power, parts, d3, pair, out))
-            power = power + functools.reduce(jnp.add, parts)
+        for bit in (core, side, 4, 8):
+            part = ring(bit, power)
+            if bit == side:
+                part, out, x12, y12 = lax.optimization_barrier((part, out, x12, y12))
+                shards[12] = (h12, (x12, 0)), True
+                shards[4 ^ side] = ((y48, 0), (x12, 1)), True
+                shards[8 ^ side] = ((y48, 1), (y12, 1)), True
+                d12 = cross(y12[0])
+                came_back += stage_columns(2, out, mine=False)
+                (out,) = stage_columns(2, out, other=False)
+            if bit == 8:
+                part, out, d12 = lax.optimization_barrier((part, out, d12))
+            power = power + part
         spread = jnp.sqrt(power[:, :1] / (datastore.shape[0] * size) + 1e-06)
 
-    shards[far[0] ^ side] = (y1, (pair, 0)), True
-    shards[far[1] ^ side] = (ys[0], (pair, 1)), True
-    shards[far[2] ^ side] = (ys[1], d3), True
-    out, back = stage_columns(2, out)
-    came_back.append(back)
+    shards[12 ^ side] = ((y12, 0), d12), True
+    came_back += stage_columns(3, out, mine=False)
+    (out,) = stage_columns(3, out, other=False)
     out = place_columns([core ^ b for stage in stages for b in stage], token_ids, came_back, out)
     return out, raw / spread
 

time: 74.2 us -> 67.9 us (0.915)
  waiting for transfers between devices: 23.9 us -> 15.4 us
  Pallas kernels: 19.6 us -> 21.4 us
    ppermute x26 -> x24, waiting for transfers between devices: 23.9 us -> 15.4 us  [swap(): return lax.ppermute(value, axis, [(i, i ^ bits) for i in range(size)])]
    pallas_call x3 -> x9, Pallas kernels: 7.25 us -> 9.15 us  [the longest x6 9.04 us: columns(): pl.pallas_call(functools.partial(column_kernel, bits, pieces, (own, other...]
    ppermute x26 -> x24, starting transfers between devices: 25.8 us -> 26 us  [swap(): return lax.ppermute(value, axis, [(i, i ^ bits) for i in range(size)])]
  transfers between devices with their start and end apart: 26 -> 24, of which waited for: 13 -> 11; matrix products, arithmetic and copies ran while one was open for 2% -> 3% of each run, Pallas kernels for 24% -> 28%
where the time goes in v5:
time: 67.9 us; the launch traced here: 67.6 us
  starting transfers between devices  26 us (38%)
  Pallas kernels  21.4 us (32%)
  waiting for transfers between devices  15.4 us (23%)
  local copies, waits for them, and re-layouts  3.12 us (5%)
  between operations  0.84 us (1%)
  other arithmetic  0.81 us (1%)
    ppermute x24, starting transfers between devices, swap(): return lax.ppermute(value, axis, [(i, i ^ bits) for i in range(size)])  26 us
    ppermute x24, waiting for transfers between devices, swap(): return lax.ppermute(value, axis, [(i, i ^ bits) for i in range(size)])  15.4 us
    pallas_call x6, Pallas kernels, columns(): pl.pallas_call(functools.partial(column_kernel, bits, pieces, (own, other...  9.04 us
    pallas_call x1, Pallas kernels, query_gradient(): pl.pallas_call(grad_kernel, in_specs=[whole] * 4 + [hbm] * 3, out_specs=[...  7.89 us
    pallas_call x1, Pallas kernels, raw_score_call(): pl.pallas_call(functools.partial(score_kernel, bits), in_specs=[vmem] * l...  2.79 us
    unnamed x12, local copies, waits for them, and re-layouts  2.08 us
    pallas_call x1, Pallas kernels, place_columns(): pl.pallas_call(functools.partial(place_kernel, bits), in_specs=[vmem] * (...  1.6 us
  transfers between devices with their start and end apart: 24, of which 11 were waited for; matrix products, arithmetic and copies ran while one was open for 3% of the time, Pallas kernels for 28%

profile of v5, /device:TPU:0, one launch (start us, length us, event | category | flops | bytes accessed | tf_op | source)
XLA Modules:
  0.0 67.6 jit_solution(12073206636677606848)
XLA Ops:
  1.2 2.6 %collective-permute-start.3 = (bf16[256,1024]{1,0:T(8,128)(2,1)}, bf16[256,1024]{1,0:T(8,128)(2,1)S(1)}, u32[]{:S(2)}, u32[]{:S(2)}) collective-permute-start(bf16[256,1024]{1,0:T(8,128)(2,1)} %refs_2_.1), channel_id=1, source_target_pairs={{0,2},{1,3},{2,0},{3,1},{4,6},{5,7},{6,4},{7,5},{8,10},{9,11},{10,... | collective-permute-start | bytes 1572872 | tf_op jit(solution)/shard_map/weight_first/ppermute | solution.py:320
  3.8 1.0 %constant_dynamic-slice_fusion = bf16[128,1024]{1,0:T(8,128)(2,1)S(1)} fusion(bf16[256,1024]{1,0:T(8,128)(2,1)} %refs_2_.1, s32[]{:T(128)S(6)} %select_n.3), kind=kLoop, calls=%fused_computation.7 | loop fusion | bytes 524292 | tf_op jit(solution)/shard_map/weight_first/dynamic_slice | solution.py:333
  4.8 1.6 %collective-permute-start.1 = (bf16[128,1024]{1,0:T(8,128)(2,1)S(1)}, bf16[128,1024]{1,0:T(8,128)(2,1)S(1)}, u32[]{:S(2)}, u32[]{:S(2)}) collective-permute-start(bf16[128,1024]{1,0:T(8,128)(2,1)S(1)} %constant_dynamic-slice_fusion), channel_id=1, source_target_pairs={{0,4},{1,5},{2,6},{3,7},{4,0},{5,1},{6,2},{7,3},{8,12},{9,13},{10,... | collective-permute-start | bytes 786440 | tf_op jit(solution)/shard_map/weight_first/ppermute | solution.py:320
  6.4 2.6 %collective-permute-start.2 = (bf16[128,1024]{1,0:T(8,128)(2,1)S(1)}, bf16[128,1024]{1,0:T(8,128)(2,1)S(1)}, u32[]{:S(2)}, u32[]{:S(2)}) collective-permute-start(bf16[128,1024]{1,0:T(8,128)(2,1)S(1)} %constant_dynamic-slice_fusion), channel_id=1, source_target_pairs={{0,8},{1,9},{2,10},{3,11},{4,12},{5,13},{6,14},{7,15},{8,0},{9,1},... | collective-permute-start | bytes 786440 | tf_op jit(solution)/shard_map/weight_first/ppermute | solution.py:320
  9.0 7.9 %query_gradient.1 = (bf16[512,1024]{1,0:T(8,128)(2,1)}, bf16[1,256,128]{2,1,0:T(8,128)(2,1)}) custom-call(s32[1,512]{1,0:T(1,128)} %ids.3, bf16[8,64,128]{2,1,0:T(8,128)(2,1)} %bitcast.5, f32[8,64,64]{2,1,0:T(8,128)} %a_inv.1, f32[8,64,64]{2,1,0:T(8,128)} %b_inv.1, bf16[512,1024]{1,0:T(8,128)(2,1)} %up_hbm.1, bf16[512,4096]{1,0:T(8,128)(2,1)} %hid_hbm.1, ...), custom_call_target="tpu_custom_call" | custom-call | flops 1 | bytes 1 | tf_op jit(solution)/shard_map/query_gradient/pallas_call | solution.py:89
  16.9 1.8 %collective-permute-done.1.first.refs_2_ = bf16[128,1024]{1,0:T(8,128)(2,1)S(1)} collective-permute-done((bf16[128,1024]{1,0:T(8,128)(2,1)S(1)}, bf16[128,1024]{1,0:T(8,128)(2,1)S(1)}, u32[]{:S(2)}, u32[]{:S(2)}) %collective-permute-start.1) | collective-permute-done | bytes 262176 | tf_op jit(solution)/shard_map/weight_first/ppermute | solution.py:320
  18.7 2.4 %collective-permute-done.2.second.refs_4_ = bf16[128,1024]{1,0:T(8,128)(2,1)S(1)} collective-permute-done((bf16[128,1024]{1,0:T(8,128)(2,1)S(1)}, bf16[128,1024]{1,0:T(8,128)(2,1)S(1)}, u32[]{:S(2)}, u32[]{:S(2)}) %collective-permute-start.2) | collective-permute-done | bytes 262176 | tf_op jit(solution)/shard_map/weight_first/ppermute | solution.py:320
  21.1 1.6 %collective-permute-start.7 = (bf16[2,128,1024]{2,1,0:T(8,128)(2,1)S(1)}, bf16[2,128,1024]{2,1,0:T(8,128)(2,1)S(1)}, u32[]{:S(2)}, u32[]{:S(2)}) collective-permute-start(bf16[2,128,1024]{2,1,0:T(8,128)(2,1)S(1)} %pair_up.3), channel_id=1, source_target_pairs={{0,16},{16,0},{1,17},{17,1},{2,18},{18,2},{3,19},{19,3},{4,20},{20... | collective-permute-start | bytes 1572872 | tf_op jit(solution)/shard_map/weight_second/ppermute | solution.py:320
  23.6 2.6 %collective-permute-start.5 = (bf16[1,256,128]{2,1,0:T(8,128)(2,1)}, bf16[1,256,128]{2,1,0:T(8,128)(2,1)S(1)}, u32[]{:S(2)}, u32[]{:S(2)}) collective-permute-start(bf16[1,256,128]{2,1,0:T(8,128)(2,1)} %get-tuple-element.33.first), channel_id=1, source_target_pairs={{0,8},{1,9},{2,10},{3,11},{4,12},{5,13},{6,14},{7,15},{8,0},{9,1},... | collective-permute-start | bytes 196616 | tf_op jit(solution)/shard_map/query_exchange/ppermute | solution.py:320
  26.2 3.4 %collective-permute-done.5.second = bf16[1,256,128]{2,1,0:T(8,128)(2,1)S(1)} collective-permute-done((bf16[1,256,128]{2,1,0:T(8,128)(2,1)}, bf16[1,256,128]{2,1,0:T(8,128)(2,1)S(1)}, u32[]{:S(2)}, u32[]{:S(2)}) %collective-permute-start.5) | collective-permute-done | bytes 65568 | tf_op jit(solution)/shard_map/query_exchange/ppermute | solution.py:320
  29.6 0.8 %copy-done.4 = bf16[1,256,128]{2,1,0:T(8,128)(2,1)S(1)} copy-done((bf16[1,256,128]{2,1,0:T(8,128)(2,1)S(1)}, bf16[1,256,128]{2,1,0:T(8,128)(2,1)}, u32[]{:S(2)}) %copy-start.4) | copy-done | bytes 65560
  30.5 1.6 %collective-permute-start.6 = (bf16[2,256,128]{2,1,0:T(8,128)(2,1)S(1)}, bf16[2,256,128]{2,1,0:T(8,128)(2,1)S(1)}, u32[]{:S(2)}, u32[]{:S(2)}) collective-permute-start(bf16[2,256,128]{2,1,0:T(8,128)(2,1)S(1)} %join.2.first), channel_id=1, source_target_pairs={{0,2},{1,3},{2,0},{3,1},{4,6},{5,7},{6,4},{7,5},{8,10},{9,11},{10,... | collective-permute-start | bytes 393224 | tf_op jit(solution)/shard_map/query_exchange/ppermute | solution.py:320
  32.1 1.2 %copy-done = bf16[512,1024]{1,0:T(8,128)(2,1)S(1)} copy-done((bf16[512,1024]{1,0:T(8,128)(2,1)S(1)}, bf16[512,1024]{1,0:T(8,128)(2,1)}, u32[]{:S(2)}) %copy-start) | copy-done | bytes 1048600
  33.3 2.0 %columns_0.1 = (bf16[512,4096]{1,0:T(8,128)(2,1)}, bf16[2,512,256]{2,1,0:T(8,128)(2,1)S(1)}) custom-call(bf16[512,1024]{1,0:T(8,128)(2,1)S(1)} %copy-done, bf16[512,1024]{1,0:T(8,128)(2,1)S(1)} %collective-permute-done.refs_1_.refs_0_, bf16[256,1024]{1,0:T(8,128)(2,1)S(1)} %copy-done.3, bf16[256,1024]{1,0:T(8,128)(2,1)S(1)} %collective-permute-done.3.refs_3_), custom_call_target="tpu_custom_call" | custom-call | flops 1 | bytes 1 | tf_op jit(solution)/shard_map/input_grad/columns_0/pallas_call | solution.py:274
  35.4 0.6 collective-permute-done.6.second
  36.0 2.8 %collective-permute-start.10 = (bf16[4,256,128]{2,1,0:T(8,128)(2,1)S(1)}, bf16[4,256,128]{2,1,0:T(8,128)(2,1)S(1)}, u32[]{:S(2)}, u32[]{:S(2)}) collective-permute-start(bf16[4,256,128]{2,1,0:T(8,128)(2,1)S(1)} %join.3.refs_0_), channel_id=1, source_target_pairs={{0,4},{1,5},{2,6},{3,7},{4,0},{5,1},{6,2},{7,3},{8,12},{9,13},{10,... | collective-permute-start | bytes 786440 | tf_op jit(solution)/shard_map/query_exchange/ppermute | solution.py:320
  38.9 0.6 collective-permute-start.17
  39.5 1.3 %collective-permute-start.18 = (bf16[2,128,1024]{2,1,0:T(8,128)(2,1)S(1)}, bf16[2,128,1024]{2,1,0:T(8,128)(2,1)S(1)}, u32[]{:S(2)}, u32[]{:S(2)}) collective-permute-start(bf16[2,128,1024]{2,1,0:T(8,128)(2,1)S(1)} %pair_up.5), channel_id=1, source_target_pairs={{0,2},{1,3},{2,0},{3,1},{4,6},{5,7},{6,4},{7,5},{8,10},{9,11},{10,... | collective-permute-start | bytes 1572872 | tf_op jit(solution)/shard_map/weight_third/ppermute | solution.py:320
  40.8 2.6 %collective-permute-done.10.refs_1_ = bf16[4,256,128]{2,1,0:T(8,128)(2,1)S(1)} collective-permute-done((bf16[4,256,128]{2,1,0:T(8,128)(2,1)S(1)}, bf16[4,256,128]{2,1,0:T(8,128)(2,1)S(1)}, u32[]{:S(2)}, u32[]{:S(2)}) %collective-permute-start.10) | collective-permute-done | bytes 262176 | tf_op jit(solution)/shard_map/query_exchange/ppermute | solution.py:320
  44.0 0.8 %collective-permute-done.12.refs_3_ = bf16[2,256,128]{2,1,0:T(8,128)(2,1)S(1)} collective-permute-done((bf16[2,256,128]{2,1,0:T(8,128)(2,1)S(1)}, bf16[2,256,128]{2,1,0:T(8,128)(2,1)S(1)}, u32[]{:S(2)}, u32[]{:S(2)}) %collective-permute-start.12) | collective-permute-done | bytes 131104 | tf_op jit(solution)/shard_map/query_exchange/ppermute | solution.py:320
  45.0 2.8 %raw_scores.1 = (f32[16,32]{1,0:T(8,128)S(1)}, f32[16,128]{1,0:T(8,128)S(1)}) custom-call(bf16[4,256,128]{2,1,0:T(8,128)(2,1)S(1)} %join.3.refs_0_, bf16[4,256,128]{2,1,0:T(8,128)(2,1)S(1)} %collective-permute-done.10.refs_1_, bf16[4,256,128]{2,1,0:T(8,128)(2,1)S(1)} %collective-permute-done.11.refs_2_, ...), custom_call_target="tpu_custom_call" | custom-call | flops 1 | bytes 1 | tf_op jit(solution)/shard_map/raw_scores/pallas_call | solution.py:186
  48.2 0.8 %collective-permute-done.15 = f32[16,128]{1,0:T(8,128)S(1)} collective-permute-done((f32[16,128]{1,0:T(8,128)S(1)}, f32[16,128]{1,0:T(8,128)S(1)}, u32[]{:S(2)}, u32[]{:S(2)}) %collective-permute-start.15) | collective-permute-done | bytes 8224 | tf_op jit(solution)/shard_map/power/ppermute | solution.py:320
  49.0 1.0 %collective-permute-start.16 = (f32[16,128]{1,0:T(8,128)S(1)}, f32[16,128]{1,0:T(8,128)S(1)}, u32[]{:S(2)}, u32[]{:S(2)}) collective-permute-start(f32[16,128]{1,0:T(8,128)S(1)} %add.19), channel_id=1, source_target_pairs={{0,2},{1,3},{2,0},{3,1},{4,6},{5,7},{6,4},{7,5},{8,10},{9,11},{10,... | collective-permute-start | bytes 24584 | tf_op jit(solution)/shard_map/power/ppermute | solution.py:320
  50.1 2.1 %columns_1.1 = (bf16[512,4096]{1,0:T(8,128)(2,1)}, bf16[2,512,256]{2,1,0:T(8,128)(2,1)S(1)}) custom-call(bf16[512,1024]{1,0:T(8,128)(2,1)S(1)} %copy-done.1, bf16[512,1024]{1,0:T(8,128)(2,1)S(1)} %collective-permute-done.refs_1_.refs_0_, bf16[128,1024]{1,0:T(8,128)(2,1)S(1)} %collective-permute-done.1.first.refs_2_, ...), custom_call_target="tpu_custom_call", output_to_operand_aliasing={{0}: (6, {})} | custom-call | flops 1 | bytes 1 | tf_op jit(solution)/shard_map/input_grad/columns_1/pallas_call | solution.py:274
  52.7 1.2 %columns_2.2 = bf16[3,512,256]{2,1,0:T(8,128)(2,1)S(1)} custom-call(bf16[512,1024]{1,0:T(8,128)(2,1)S(1)} %collective-permute-done.refs_1_.refs_0_, bf16[128,1024]{1,0:T(8,128)(2,1)S(1)} %collective-permute-done.9.first.refs_1_, bf16[2,128,1024]{2,1,0:T(8,128)(2,1)S(1)} %collective-permute-done.17.refs_2_.refs_4_, ...), custom_call_target="tpu_custom_call" | custom-call | flops 1 | bytes 1 | tf_op jit(solution)/shard_map/power/input_grad/columns_2/pallas_call | solution.py:274
  55.1 1.8 %collective-permute-start.20 = (f32[16,128]{1,0:T(8,128)S(1)}, f32[16,128]{1,0:T(8,128)S(1)}, u32[]{:S(2)}, u32[]{:S(2)}) collective-permute-start(f32[16,128]{1,0:T(8,128)S(1)} %add.20), channel_id=1, source_target_pairs={{0,4},{1,5},{2,6},{3,7},{4,0},{5,1},{6,2},{7,3},{8,12},{9,13},{10,... | collective-permute-start | bytes 24584 | tf_op jit(solution)/shard_map/power/ppermute | solution.py:320
  57.0 1.8 %collective-permute-done.20 = f32[16,128]{1,0:T(8,128)S(1)} collective-permute-done((f32[16,128]{1,0:T(8,128)S(1)}, f32[16,128]{1,0:T(8,128)S(1)}, u32[]{:S(2)}, u32[]{:S(2)}) %collective-permute-start.20) | collective-permute-done | bytes 8224 | tf_op jit(solution)/shard_map/power/ppermute | solution.py:320
  58.8 2.2 %collective-permute-start.21 = (f32[16,128]{1,0:T(8,128)S(1)}, f32[16,128]{1,0:T(8,128)S(1)}, u32[]{:S(2)}, u32[]{:S(2)}) collective-permute-start(f32[16,128]{1,0:T(8,128)S(1)} %add.21), channel_id=1, source_target_pairs={{0,8},{1,9},{2,10},{3,11},{4,12},{5,13},{6,14},{7,15},{8,0},{9,1},... | collective-permute-start | bytes 24584 | tf_op jit(solution)/shard_map/power/ppermute | solution.py:320
  61.0 2.0 %columns_2.3.refs_3_ = bf16[512,4096]{1,0:T(8,128)(2,1)} custom-call(bf16[512,1024]{1,0:T(8,128)(2,1)S(1)} %copy-done.1, bf16[128,1024]{1,0:T(8,128)(2,1)S(1)} %collective-permute-done.9.first.refs_1_, bf16[2,128,1024]{2,1,0:T(8,128)(2,1)S(1)} %collective-permute-done.17.refs_2_.refs_4_, ...), custom_call_target="tpu_custom_call", output_to_operand_aliasing={{}: (7, {})} | custom-call | flops 1 | bytes 1 | tf_op jit(solution)/shard_map/power/input_grad/columns_2/pallas_call | solution.py:274
  64.1 1.2 %columns_3.3.refs_4_ = bf16[512,4096]{1,0:T(8,128)(2,1)} custom-call(bf16[512,1024]{1,0:T(8,128)(2,1)S(1)} %copy-done.1, bf16[2,128,1024]{2,1,0:T(8,128)(2,1)S(1)} %collective-permute-done.18.refs_6_.refs_1_, bf16[128,1024]{1,0:T(8,128)(2,1)S(1)} %collective-permute-done.22.refs_2_, bf16[512,4096]{1,0:T(8,128)(2,1)} %columns_2.3.refs_3_), custom_call_target="tpu_custom_call", output_to_operand_aliasing={{}: (3, {})} | custom-call | flops 1 | bytes 1 | tf_op jit(solution)/shard_map/input_grad/columns_3/pallas_call | solution.py:274
  65.3 0.7 %broadcast_divide_fusion = f32[16,32]{1,0:T(8,128)} fusion(f32[16,32]{1,0:T(8,128)S(1)} %get-tuple-element.52, f32[16]{0:T(128)S(1)} %fusion.3), kind=kLoop, calls=%fused_computation.6 | loop fusion | flops 512 | bytes 4160 | tf_op jit(solution)/shard_map/div | solution.py:409
  66.0 1.6 %place_columns.1 = bf16[512,4096]{1,0:T(8,128)(2,1)} custom-call(s32[1,512]{1,0:T(1,128)S(1)} %copy-done.5, bf16[2,512,256]{2,1,0:T(8,128)(2,1)S(1)} %collective-permute-done.4.refs_0_, bf16[2,512,256]{2,1,0:T(8,128)(2,1)S(1)} %collective-permute-done.14.refs_1_, ...), custom_call_target="tpu_custom_call", output_to_operand_aliasing={{}: (5, {})} | custom-call | flops 1 | bytes 1 | tf_op jit(solution)/shard_map/place_columns/pallas_call | solution.py:303
  (50 shorter events, 5.6 us)
Async XLA Ops:
  0.6 31.4 %copy-start.3 = (bf16[256,1024]{1,0:T(8,128)(2,1)S(1)}, bf16[256,1024]{1,0:T(8,128)(2,1)}, u32[]{:S(2)}) copy-start(bf16[256,1024]{1,0:T(8,128)(2,1)} %refs_2_.1) | copy-start | bytes 1572868
  0.6 23.0 %collective-permute-start = (bf16[512,1024]{1,0:T(8,128)(2,1)}, bf16[512,1024]{1,0:T(8,128)(2,1)S(1)}, u32[]{:S(2)}, u32[]{:S(2)}) collective-permute-start(bf16[512,1024]{1,0:T(8,128)(2,1)} %up_hbm.1), channel_id=1, source_target_pairs={{0,1},{1,0},{2,3},{3,2},{4,5},{5,4},{6,7},{7,6},{8,9},{9,8},{10,11... | collective-permute-start | bytes 3145736 | tf_op jit(solution)/shard_map/weight_first/ppermute | solution.py:320
  1.2 19.9 %collective-permute-start.3 = (bf16[256,1024]{1,0:T(8,128)(2,1)}, bf16[256,1024]{1,0:T(8,128)(2,1)S(1)}, u32[]{:S(2)}, u32[]{:S(2)}) collective-permute-start(bf16[256,1024]{1,0:T(8,128)(2,1)} %refs_2_.1), channel_id=1, source_target_pairs={{0,2},{1,3},{2,0},{3,1},{4,6},{5,7},{6,4},{7,5},{8,10},{9,11},{10,... | collective-permute-start | bytes 1572872 | tf_op jit(solution)/shard_map/weight_first/ppermute | solution.py:320
  4.8 13.9 %collective-permute-start.1 = (bf16[128,1024]{1,0:T(8,128)(2,1)S(1)}, bf16[128,1024]{1,0:T(8,128)(2,1)S(1)}, u32[]{:S(2)}, u32[]{:S(2)}) collective-permute-start(bf16[128,1024]{1,0:T(8,128)(2,1)S(1)} %constant_dynamic-slice_fusion), channel_id=1, source_target_pairs={{0,4},{1,5},{2,6},{3,7},{4,0},{5,1},{6,2},{7,3},{8,12},{9,13},{10,... | collective-permute-start | bytes 786440 | tf_op jit(solution)/shard_map/weight_first/ppermute | solution.py:320
  6.4 14.7 %collective-permute-start.2 = (bf16[128,1024]{1,0:T(8,128)(2,1)S(1)}, bf16[128,1024]{1,0:T(8,128)(2,1)S(1)}, u32[]{:S(2)}, u32[]{:S(2)}) collective-permute-start(bf16[128,1024]{1,0:T(8,128)(2,1)S(1)} %constant_dynamic-slice_fusion), channel_id=1, source_target_pairs={{0,8},{1,9},{2,10},{3,11},{4,12},{5,13},{6,14},{7,15},{8,0},{9,1},... | collective-permute-start | bytes 786440 | tf_op jit(solution)/shard_map/weight_first/ppermute | solution.py:320
  9.0 36.0 %copy-start.2 = (bf16[32,32768]{1,0:T(8,128)(2,1)S(1)}, bf16[32,32768]{1,0:T(8,128)(2,1)}, u32[]{:S(2)}) copy-start(bf16[32,32768]{1,0:T(8,128)(2,1)} %refs_5_.1) | copy-start | bytes 6291460
  21.1 14.2 %collective-permute-start.7 = (bf16[2,128,1024]{2,1,0:T(8,128)(2,1)S(1)}, bf16[2,128,1024]{2,1,0:T(8,128)(2,1)S(1)}, u32[]{:S(2)}, u32[]{:S(2)}) collective-permute-start(bf16[2,128,1024]{2,1,0:T(8,128)(2,1)S(1)} %pair_up.3), channel_id=1, source_target_pairs={{0,16},{16,0},{1,17},{17,1},{2,18},{18,2},{3,19},{19,3},{4,20},{20... | collective-permute-start | bytes 1572872 | tf_op jit(solution)/shard_map/weight_second/ppermute | solution.py:320
  22.7 12.7 %collective-permute-start.8 = (bf16[2,128,1024]{2,1,0:T(8,128)(2,1)S(1)}, bf16[2,128,1024]{2,1,0:T(8,128)(2,1)S(1)}, u32[]{:S(2)}, u32[]{:S(2)}) collective-permute-start(bf16[2,128,1024]{2,1,0:T(8,128)(2,1)S(1)} %pair_up.3), channel_id=1, source_target_pairs={{0,2},{1,3},{2,0},{3,1},{4,6},{5,7},{6,4},{7,5},{8,10},{9,11},{10,... | collective-permute-start | bytes 1572872 | tf_op jit(solution)/shard_map/weight_second/ppermute | solution.py:320
  23.2 12.2 %collective-permute-start.9 = (bf16[128,1024]{1,0:T(8,128)(2,1)S(1)}, bf16[128,1024]{1,0:T(8,128)(2,1)S(1)}, u32[]{:S(2)}, u32[]{:S(2)}) collective-permute-start(bf16[128,1024]{1,0:T(8,128)(2,1)S(1)} %collective-permute-done.2.second.refs_4_), channel_id=1, source_target_pairs={{0,4},{1,5},{2,6},{3,7},{4,0},{5,1},{6,2},{7,3},{8,12},{9,13},{10,... | collective-permute-start | bytes 786440 | tf_op jit(solution)/shard_map/weight_second/ppermute | solution.py:320
  23.6 6.0 %collective-permute-start.5 = (bf16[1,256,128]{2,1,0:T(8,128)(2,1)}, bf16[1,256,128]{2,1,0:T(8,128)(2,1)S(1)}, u32[]{:S(2)}, u32[]{:S(2)}) collective-permute-start(bf16[1,256,128]{2,1,0:T(8,128)(2,1)} %get-tuple-element.33.first), channel_id=1, source_target_pairs={{0,8},{1,9},{2,10},{3,11},{4,12},{5,13},{6,14},{7,15},{8,0},{9,1},... | collective-permute-start | bytes 196616 | tf_op jit(solution)/shard_map/query_exchange/ppermute | solution.py:320
  29.6 0.8 %copy-start.4 = (bf16[1,256,128]{2,1,0:T(8,128)(2,1)S(1)}, bf16[1,256,128]{2,1,0:T(8,128)(2,1)}, u32[]{:S(2)}) copy-start(bf16[1,256,128]{2,1,0:T(8,128)(2,1)} %get-tuple-element.33.first) | copy-start | bytes 196612
  30.5 5.5 %collective-permute-start.6 = (bf16[2,256,128]{2,1,0:T(8,128)(2,1)S(1)}, bf16[2,256,128]{2,1,0:T(8,128)(2,1)S(1)}, u32[]{:S(2)}, u32[]{:S(2)}) collective-permute-start(bf16[2,256,128]{2,1,0:T(8,128)(2,1)S(1)} %join.2.first), channel_id=1, source_target_pairs={{0,2},{1,3},{2,0},{3,1},{4,6},{5,7},{6,4},{7,5},{8,10},{9,11},{10,... | collective-permute-start | bytes 393224 | tf_op jit(solution)/shard_map/query_exchange/ppermute | solution.py:320
  32.1 1.2 %copy-start = (bf16[512,1024]{1,0:T(8,128)(2,1)S(1)}, bf16[512,1024]{1,0:T(8,128)(2,1)}, u32[]{:S(2)}) copy-start(bf16[512,1024]{1,0:T(8,128)(2,1)} %get-tuple-element.28.refs_0_) | copy-start | bytes 3145732
  35.3 14.8 %copy-start.1 = (bf16[512,1024]{1,0:T(8,128)(2,1)S(1)}, bf16[512,1024]{1,0:T(8,128)(2,1)}, u32[]{:S(2)}) copy-start(bf16[512,1024]{1,0:T(8,128)(2,1)} %get-tuple-element.28.refs_0_) | copy-start | bytes 3145732
  36.0 7.4 %collective-permute-start.10 = (bf16[4,256,128]{2,1,0:T(8,128)(2,1)S(1)}, bf16[4,256,128]{2,1,0:T(8,128)(2,1)S(1)}, u32[]{:S(2)}, u32[]{:S(2)}) collective-permute-start(bf16[4,256,128]{2,1,0:T(8,128)(2,1)S(1)} %join.3.refs_0_), channel_id=1, source_target_pairs={{0,4},{1,5},{2,6},{3,7},{4,0},{5,1},{6,2},{7,3},{8,12},{9,13},{10,... | collective-permute-start | bytes 786440 | tf_op jit(solution)/shard_map/query_exchange/ppermute | solution.py:320
  38.9 13.8 %collective-permute-start.17 = (bf16[2,128,1024]{2,1,0:T(8,128)(2,1)S(1)}, bf16[2,128,1024]{2,1,0:T(8,128)(2,1)S(1)}, u32[]{:S(2)}, u32[]{:S(2)}) collective-permute-start(bf16[2,128,1024]{2,1,0:T(8,128)(2,1)S(1)} %pair_up.4), channel_id=1, source_target_pairs={{0,16},{16,0},{1,17},{17,1},{2,18},{18,2},{3,19},{19,3},{4,20},{20... | collective-permute-start | bytes 1572872 | tf_op jit(solution)/shard_map/weight_third/ppermute | solution.py:320
  39.5 13.2 %collective-permute-start.18 = (bf16[2,128,1024]{2,1,0:T(8,128)(2,1)S(1)}, bf16[2,128,1024]{2,1,0:T(8,128)(2,1)S(1)}, u32[]{:S(2)}, u32[]{:S(2)}) collective-permute-start(bf16[2,128,1024]{2,1,0:T(8,128)(2,1)S(1)} %pair_up.5), channel_id=1, source_target_pairs={{0,2},{1,3},{2,0},{3,1},{4,6},{5,7},{6,4},{7,5},{8,10},{9,11},{10,... | collective-permute-start | bytes 1572872 | tf_op jit(solution)/shard_map/weight_third/ppermute | solution.py:320
  40.8 3.2 %collective-permute-start.11 = (bf16[4,256,128]{2,1,0:T(8,128)(2,1)S(1)}, bf16[4,256,128]{2,1,0:T(8,128)(2,1)S(1)}, u32[]{:S(2)}, u32[]{:S(2)}) collective-permute-start(bf16[4,256,128]{2,1,0:T(8,128)(2,1)S(1)} %join.3.refs_0_), channel_id=1, source_target_pairs={{0,1},{1,0},{2,3},{3,2},{4,5},{5,4},{6,7},{7,6},{8,9},{9,8},{10,11... | collective-permute-start | bytes 786440 | tf_op jit(solution)/shard_map/query_exchange/ppermute | solution.py:320
  43.4 1.4 %collective-permute-start.12 = (bf16[2,256,128]{2,1,0:T(8,128)(2,1)S(1)}, bf16[2,256,128]{2,1,0:T(8,128)(2,1)S(1)}, u32[]{:S(2)}, u32[]{:S(2)}) collective-permute-start(bf16[2,256,128]{2,1,0:T(8,128)(2,1)S(1)} %get-tuple-element.55), channel_id=1, source_target_pairs={{0,1},{1,0},{2,3},{3,2},{4,5},{5,4},{6,7},{7,6},{8,9},{9,8},{10,11... | collective-permute-start | bytes 393224 | tf_op jit(solution)/shard_map/query_exchange/ppermute | solution.py:320
  43.5 1.5 %collective-permute-start.13 = (bf16[2,256,128]{2,1,0:T(8,128)(2,1)S(1)}, bf16[2,256,128]{2,1,0:T(8,128)(2,1)S(1)}, u32[]{:S(2)}, u32[]{:S(2)}) collective-permute-start(bf16[2,256,128]{2,1,0:T(8,128)(2,1)S(1)} %get-tuple-element.54), channel_id=1, source_target_pairs={{0,1},{1,0},{2,3},{3,2},{4,5},{5,4},{6,7},{7,6},{8,9},{9,8},{10,11... | collective-permute-start | bytes 393224 | tf_op jit(solution)/shard_map/query_exchange/ppermute | solution.py:320
  47.8 1.2 %collective-permute-start.15 = (f32[16,128]{1,0:T(8,128)S(1)}, f32[16,128]{1,0:T(8,128)S(1)}, u32[]{:S(2)}, u32[]{:S(2)}) collective-permute-start(f32[16,128]{1,0:T(8,128)S(1)} %get-tuple-element.40), channel_id=1, source_target_pairs={{0,1},{1,0},{2,3},{3,2},{4,5},{5,4},{6,7},{7,6},{8,9},{9,8},{10,11... | collective-permute-start | bytes 24584 | tf_op jit(solution)/shard_map/power/ppermute | solution.py:320
  49.0 3.7 %collective-permute-start.16 = (f32[16,128]{1,0:T(8,128)S(1)}, f32[16,128]{1,0:T(8,128)S(1)}, u32[]{:S(2)}, u32[]{:S(2)}) collective-permute-start(f32[16,128]{1,0:T(8,128)S(1)} %add.19), channel_id=1, source_target_pairs={{0,2},{1,3},{2,0},{3,1},{4,6},{5,7},{6,4},{7,5},{8,10},{9,11},{10,... | collective-permute-start | bytes 24584 | tf_op jit(solution)/shard_map/power/ppermute | solution.py:320
  53.9 12.1 %collective-permute-start.19 = (bf16[3,512,256]{2,1,0:T(8,128)(2,1)S(1)}, bf16[3,512,256]{2,1,0:T(8,128)(2,1)S(1)}, u32[]{:S(2)}, u32[]{:S(2)}) collective-permute-start(bf16[3,512,256]{2,1,0:T(8,128)(2,1)S(1)} %columns_2.2), channel_id=1, source_target_pairs={{0,1},{1,0},{2,3},{3,2},{4,5},{5,4},{6,7},{7,6},{8,9},{9,8},{10,11... | collective-permute-start | bytes 2359304 | tf_op jit(solution)/shard_map/power/input_grad/ppermute | solution.py:320
  54.0 9.3 %collective-permute-start.22 = (bf16[128,1024]{1,0:T(8,128)(2,1)S(1)}, bf16[128,1024]{1,0:T(8,128)(2,1)S(1)}, u32[]{:S(2)}, u32[]{:S(2)}) collective-permute-start(bf16[128,1024]{1,0:T(8,128)(2,1)S(1)} %slice_bitcast_fusion), channel_id=1, source_target_pairs={{0,16},{16,0},{1,17},{17,1},{2,18},{18,2},{3,19},{19,3},{4,20},{20... | collective-permute-start | bytes 786440 | tf_op jit(solution)/shard_map/power/ppermute | solution.py:320
  54.6 11.4 %collective-permute-start.4 = (bf16[2,512,256]{2,1,0:T(8,128)(2,1)S(1)}, bf16[2,512,256]{2,1,0:T(8,128)(2,1)S(1)}, u32[]{:S(2)}, u32[]{:S(2)}) collective-permute-start(bf16[2,512,256]{2,1,0:T(8,128)(2,1)S(1)} %get-tuple-element.31), channel_id=1, source_target_pairs={{0,1},{1,0},{2,3},{3,2},{4,5},{5,4},{6,7},{7,6},{8,9},{9,8},{10,11... | collective-permute-start | bytes 1572872 | tf_op jit(solution)/shard_map/input_grad/ppermute | solution.py:320
  54.8 11.2 %collective-permute-start.14 = (bf16[2,512,256]{2,1,0:T(8,128)(2,1)S(1)}, bf16[2,512,256]{2,1,0:T(8,128)(2,1)S(1)}, u32[]{:S(2)}, u32[]{:S(2)}) collective-permute-start(bf16[2,512,256]{2,1,0:T(8,128)(2,1)S(1)} %get-tuple-element.42), channel_id=1, source_target_pairs={{0,1},{1,0},{2,3},{3,2},{4,5},{5,4},{6,7},{7,6},{8,9},{9,8},{10,11... | collective-permute-start | bytes 1572872 | tf_op jit(solution)/shard_map/input_grad/ppermute | solution.py:320
  55.1 3.7 %collective-permute-start.20 = (f32[16,128]{1,0:T(8,128)S(1)}, f32[16,128]{1,0:T(8,128)S(1)}, u32[]{:S(2)}, u32[]{:S(2)}) collective-permute-start(f32[16,128]{1,0:T(8,128)S(1)} %add.20), channel_id=1, source_target_pairs={{0,4},{1,5},{2,6},{3,7},{4,0},{5,1},{6,2},{7,3},{8,12},{9,13},{10,... | collective-permute-start | bytes 24584 | tf_op jit(solution)/shard_map/power/ppermute | solution.py:320
  58.8 4.5 %collective-permute-start.21 = (f32[16,128]{1,0:T(8,128)S(1)}, f32[16,128]{1,0:T(8,128)S(1)}, u32[]{:S(2)}, u32[]{:S(2)}) collective-permute-start(f32[16,128]{1,0:T(8,128)S(1)} %add.21), channel_id=1, source_target_pairs={{0,8},{1,9},{2,10},{3,11},{4,12},{5,13},{6,14},{7,15},{8,0},{9,1},... | collective-permute-start | bytes 24584 | tf_op jit(solution)/shard_map/power/ppermute | solution.py:320
  63.9 2.1 %collective-permute-start.23 = (bf16[1,512,256]{2,1,0:T(8,128)(2,1)S(1)}, bf16[1,512,256]{2,1,0:T(8,128)(2,1)S(1)}, u32[]{:S(2)}, u32[]{:S(2)}) collective-permute-start(bf16[1,512,256]{2,1,0:T(8,128)(2,1)S(1)} %columns_3.2), channel_id=1, source_target_pairs={{0,1},{1,0},{2,3},{3,2},{4,5},{5,4},{6,7},{7,6},{8,9},{9,8},{10,11... | collective-permute-start | bytes 786440 | tf_op jit(solution)/shard_map/input_grad/ppermute | solution.py:320
  64.1 1.9 %copy-start.5 = (s32[1,512]{1,0:T(1,128)S(1)}, s32[1,512]{1,0:T(1,128)}, u32[]{:S(2)}) copy-start(s32[1,512]{1,0:T(1,128)} %ids.3) | copy-start | bytes 6148

commit v6 on v5

--- a/solution.py
+++ b/solution.py
@@ -284,8 +284,13 @@
     )(*operands)
 
 
-def place_kernel(bits, ids, *refs):
-    (*came, _, out, tiles, sems) = refs
+def place_kernel(bits, rows_in_all, ids, *refs):
+    if rows_in_all:
+        raw, power, *refs = refs
+        *refs, out, scores, tiles, sems = refs
+    else:
+        *refs, out, tiles, sems = refs
+    came = refs[:-1]
     me = lax.axis_index("seq")
     live = jnp.sum((ids[...] != 0).astype(jnp.int32))
     row = lax.broadcasted_iota(jnp.int32, tiles.shape[1:], 0)
@@ -294,26 +299,32 @@
     for n, (bit, ref) in enumerate(zip(bits, given)):
         tiles[n] = jnp.where(row < live, ref[...].astype(F32), 0.0).astype(BF16)
         copies.append(put(tiles.at[n], out, me ^ bit, sems.at[n]))
+    if rows_in_all:
+        scores[...] = raw[...] / jnp.sqrt(power[:, : raw.shape[1]] / rows_in_all + 1e-06)
     for copy in copies:
         copy.wait()
 
 
-def place_columns(bits, token_ids, came, out):
+def place_columns(bits, token_ids, came, out, raw=None, power=None, rows_in_all=0):
     vmem, hbm = pl.BlockSpec(memory_space=VMEM), pl.BlockSpec(memory_space=pltpu.HBM)
-    return pl.pallas_call(
-        functools.partial(place_kernel, bits),
-        in_specs=[vmem] * (1 + len(came)) + [hbm],
-        out_specs=hbm,
-        out_shape=jax.ShapeDtypeStruct(out.shape, BF16),
+    extra = [raw, power] if rows_in_all else []
+    shapes = [jax.ShapeDtypeStruct(out.shape, BF16)]
+    if rows_in_all:
+        shapes.append(jax.ShapeDtypeStruct(raw.shape, F32))
+    return pl.pallas_call(
+        functools.partial(place_kernel, bits, rows_in_all),
+        in_specs=[vmem] * (1 + len(extra) + len(came)) + [hbm],
+        out_specs=[hbm] + [vmem] * (len(shapes) - 1),
+        out_shape=shapes,
         scratch_shapes=[
             VMEM((len(bits), *came[0].shape[1:]), BF16),
             pltpu.SemaphoreType.DMA((len(bits),)),
         ],
-        input_output_aliases={1 + len(came): 0},
+        input_output_aliases={1 + len(extra) + len(came): 0},
         compiler_params=params(),
         cost_estimate=SMALL,
         name="place_columns",
-    )(token_ids, *came, out)
+    )(token_ids, *extra, *came, out)
 
 
 def swap(value, axis, size, bits):
@@ -357,7 +368,7 @@
             return [*made[:-1], ring(core, made[-1])] if other else made
 
     with jax.named_scope("weight_second"):
-        h4, h8, beside = after((h4, h8, beside), grad)
+        h4, h8 = after((h4, h8), grad)
         both = pair_up(h4, h8)
         x48, y48, h12 = cross(both), ring(side, both), ring(4, h8)
 
@@ -400,13 +411,13 @@
             if bit == 8:
                 part, out, d12 = lax.optimization_barrier((part, out, d12))
             power = power + part
-        spread = jnp.sqrt(power[:, :1] / (datastore.shape[0] * size) + 1e-06)
 
     shards[12 ^ side] = ((y12, 0), d12), True
     came_back += stage_columns(3, out, mine=False)
     (out,) = stage_columns(3, out, other=False)
-    out = place_columns([core ^ b for stage in stages for b in stage], token_ids, came_back, out)
-    return out, raw / spread
+    order = [core ^ b for stage in stages for b in stage]
+    rows_in_all = datastore.shape[0] * size
+    return place_columns(order, token_ids, came_back, out, raw, power, rows_in_all)
 
 
 def by_gather(
@@ -452,6 +463,7 @@
             and size == 16
             and token_ids.shape[0] == 1
             and w_value.shape[0] % 256 == 0
+            and args[8].shape[0] <= 2 * args[4].shape[1]
         )
         return (by_exchange if fits else by_gather)(size, *args)
 

time: 67.9 us -> 67.5 us (level)
  other arithmetic: 0.81 us -> 0.01 us
  waiting for transfers between devices: 15.4 us -> 14.7 us
    ppermute x24, waiting for transfers between devices: 15.4 us -> 14.7 us  [swap(): return lax.ppermute(value, axis, [(i, i ^ bits) for i in range(size)])]
  transfers between devices with their start and end apart: 24 -> 24, of which waited for: 11 -> 12; matrix products, arithmetic and copies ran while one was open for 3% -> 2% of each run, Pallas kernels for 28% -> 28%
where the time goes in v6:
time: 67.5 us; the launch traced here: 67.2 us
  starting transfers between devices  26.5 us (39%)
  Pallas kernels  22 us (33%)
  waiting for transfers between devices  14.7 us (22%)
  local copies, waits for them, and re-layouts  3.09 us (5%)
  between operations  0.84 us (1%)
    ppermute x24, starting transfers between devices, swap(): return lax.ppermute(value, axis, [(i, i ^ bits) for i in range(size)])  26.5 us
    ppermute x24, waiting for transfers between devices, swap(): return lax.ppermute(value, axis, [(i, i ^ bits) for i in range(size)])  14.7 us
    pallas_call x6, Pallas kernels, columns(): pl.pallas_call(functools.partial(column_kernel, bits, pieces, (own, other...  9.03 us
    pallas_call x1, Pallas kernels, query_gradient(): pl.pallas_call(grad_kernel, in_specs=[whole] * 4 + [hbm] * 3, out_specs=[...  7.89 us
    pallas_call x1, Pallas kernels, raw_score_call(): pl.pallas_call(functools.partial(score_kernel, bits), in_specs=[vmem] * l...  2.79 us
    pallas_call x1, Pallas kernels, place_columns(): pl.pallas_call(functools.partial(place_kernel, bits, rows_in_all), in_spe...  2.19 us
    unnamed x12, local copies, waits for them, and re-layouts  2.09 us
  transfers between devices with their start and end apart: 24, of which 12 were waited for; matrix products, arithmetic and copies ran while one was open for 2% of the time, Pallas kernels for 28%

profile of v6, /device:TPU:0, one launch (start us, length us, event | category | flops | bytes accessed | tf_op | source)
XLA Modules:
  0.0 67.2 jit_solution(10788063173220407509)
XLA Ops:
  1.2 1.0 %constant_dynamic-slice_fusion = bf16[128,1024]{1,0:T(8,128)(2,1)S(1)} fusion(bf16[256,1024]{1,0:T(8,128)(2,1)} %refs_2_.1, s32[]{:T(128)S(6)} %select_n.3), kind=kLoop, calls=%fused_computation.1 | loop fusion | bytes 524292 | tf_op jit(solution)/shard_map/weight_first/dynamic_slice | solution.py:344
  2.1 2.7 %collective-permute-start.3 = (bf16[128,1024]{1,0:T(8,128)(2,1)S(1)}, bf16[128,1024]{1,0:T(8,128)(2,1)S(1)}, u32[]{:S(2)}, u32[]{:S(2)}) collective-permute-start(bf16[128,1024]{1,0:T(8,128)(2,1)S(1)} %constant_dynamic-slice_fusion), channel_id=1, source_target_pairs={{0,4},{1,5},{2,6},{3,7},{4,0},{5,1},{6,2},{7,3},{8,12},{9,13},{10,... | collective-permute-start | bytes 786440 | tf_op jit(solution)/shard_map/weight_first/ppermute | solution.py:331
  4.8 2.6 %collective-permute-start.4 = (bf16[128,1024]{1,0:T(8,128)(2,1)S(1)}, bf16[128,1024]{1,0:T(8,128)(2,1)S(1)}, u32[]{:S(2)}, u32[]{:S(2)}) collective-permute-start(bf16[128,1024]{1,0:T(8,128)(2,1)S(1)} %constant_dynamic-slice_fusion), channel_id=1, source_target_pairs={{0,8},{1,9},{2,10},{3,11},{4,12},{5,13},{6,14},{7,15},{8,0},{9,1},... | collective-permute-start | bytes 786440 | tf_op jit(solution)/shard_map/weight_first/ppermute | solution.py:331
  7.4 1.5 %collective-permute-start.8 = (bf16[256,1024]{1,0:T(8,128)(2,1)}, bf16[256,1024]{1,0:T(8,128)(2,1)S(1)}, u32[]{:S(2)}, u32[]{:S(2)}) collective-permute-start(bf16[256,1024]{1,0:T(8,128)(2,1)} %refs_2_.1), channel_id=1, source_target_pairs={{0,2},{1,3},{2,0},{3,1},{4,6},{5,7},{6,4},{7,5},{8,10},{9,11},{10,... | collective-permute-start | bytes 1572872 | tf_op jit(solution)/shard_map/weight_first/ppermute | solution.py:331
  9.0 7.9 %query_gradient.1 = (bf16[512,1024]{1,0:T(8,128)(2,1)}, bf16[1,256,128]{2,1,0:T(8,128)(2,1)}) custom-call(s32[1,512]{1,0:T(1,128)} %ids.3, bf16[8,64,128]{2,1,0:T(8,128)(2,1)} %bitcast.5, f32[8,64,64]{2,1,0:T(8,128)} %a_inv.1, f32[8,64,64]{2,1,0:T(8,128)} %b_inv.1, bf16[512,1024]{1,0:T(8,128)(2,1)} %up_hbm.1, bf16[512,4096]{1,0:T(8,128)(2,1)} %hid_hbm.1, ...), custom_call_target="tpu_custom_call" | custom-call | flops 1 | bytes 1 | tf_op jit(solution)/shard_map/query_gradient/pallas_call | solution.py:89
  17.2 2.5 %collective-permute-done.4.second.refs_4_ = bf16[128,1024]{1,0:T(8,128)(2,1)S(1)} collective-permute-done((bf16[128,1024]{1,0:T(8,128)(2,1)S(1)}, bf16[128,1024]{1,0:T(8,128)(2,1)S(1)}, u32[]{:S(2)}, u32[]{:S(2)}) %collective-permute-start.4) | collective-permute-done | bytes 262176 | tf_op jit(solution)/shard_map/weight_first/ppermute | solution.py:331
  19.8 1.6 %collective-permute-start.5 = (bf16[2,128,1024]{2,1,0:T(8,128)(2,1)S(1)}, bf16[2,128,1024]{2,1,0:T(8,128)(2,1)S(1)}, u32[]{:S(2)}, u32[]{:S(2)}) collective-permute-start(bf16[2,128,1024]{2,1,0:T(8,128)(2,1)S(1)} %pair_up.3), channel_id=1, source_target_pairs={{0,16},{16,0},{1,17},{17,1},{2,18},{18,2},{3,19},{19,3},{4,20},{20... | collective-permute-start | bytes 1572872 | tf_op jit(solution)/shard_map/weight_second/ppermute | solution.py:331
  21.4 1.5 %collective-permute-start.6 = (bf16[2,128,1024]{2,1,0:T(8,128)(2,1)S(1)}, bf16[2,128,1024]{2,1,0:T(8,128)(2,1)S(1)}, u32[]{:S(2)}, u32[]{:S(2)}) collective-permute-start(bf16[2,128,1024]{2,1,0:T(8,128)(2,1)S(1)} %pair_up.3), channel_id=1, source_target_pairs={{0,2},{1,3},{2,0},{3,1},{4,6},{5,7},{6,4},{7,5},{8,10},{9,11},{10,... | collective-permute-start | bytes 1572872 | tf_op jit(solution)/shard_map/weight_second/ppermute | solution.py:331
  23.4 2.6 %collective-permute-start.1 = (bf16[1,256,128]{2,1,0:T(8,128)(2,1)}, bf16[1,256,128]{2,1,0:T(8,128)(2,1)S(1)}, u32[]{:S(2)}, u32[]{:S(2)}) collective-permute-start(bf16[1,256,128]{2,1,0:T(8,128)(2,1)} %get-tuple-element.28.first), channel_id=1, source_target_pairs={{0,8},{1,9},{2,10},{3,11},{4,12},{5,13},{6,14},{7,15},{8,0},{9,1},... | collective-permute-start | bytes 196616 | tf_op jit(solution)/shard_map/query_exchange/ppermute | solution.py:331
  25.9 3.7 %collective-permute-done.1.second = bf16[1,256,128]{2,1,0:T(8,128)(2,1)S(1)} collective-permute-done((bf16[1,256,128]{2,1,0:T(8,128)(2,1)}, bf16[1,256,128]{2,1,0:T(8,128)(2,1)S(1)}, u32[]{:S(2)}, u32[]{:S(2)}) %collective-permute-start.1) | collective-permute-done | bytes 65568 | tf_op jit(solution)/shard_map/query_exchange/ppermute | solution.py:331
  29.6 0.8 %copy-done.4 = bf16[1,256,128]{2,1,0:T(8,128)(2,1)S(1)} copy-done((bf16[1,256,128]{2,1,0:T(8,128)(2,1)S(1)}, bf16[1,256,128]{2,1,0:T(8,128)(2,1)}, u32[]{:S(2)}) %copy-start.4) | copy-done | bytes 65560
  30.5 0.6 collective-permute-start.2
  31.1 1.2 %copy-done = bf16[512,1024]{1,0:T(8,128)(2,1)S(1)} copy-done((bf16[512,1024]{1,0:T(8,128)(2,1)S(1)}, bf16[512,1024]{1,0:T(8,128)(2,1)}, u32[]{:S(2)}) %copy-start) | copy-done | bytes 1048600
  32.3 2.0 %columns_0.1 = (bf16[512,4096]{1,0:T(8,128)(2,1)}, bf16[2,512,256]{2,1,0:T(8,128)(2,1)S(1)}) custom-call(bf16[512,1024]{1,0:T(8,128)(2,1)S(1)} %copy-done, bf16[512,1024]{1,0:T(8,128)(2,1)S(1)} %collective-permute-done.refs_1_.refs_0_, bf16[256,1024]{1,0:T(8,128)(2,1)S(1)} %copy-done.3, bf16[256,1024]{1,0:T(8,128)(2,1)S(1)} %collective-permute-done.8.refs_3_), custom_call_target="tpu_custom_call" | custom-call | flops 1 | bytes 1 | tf_op jit(solution)/shard_map/input_grad/columns_0/pallas_call | solution.py:274
  34.3 1.2 %collective-permute-done.2.second = bf16[2,256,128]{2,1,0:T(8,128)(2,1)S(1)} collective-permute-done((bf16[2,256,128]{2,1,0:T(8,128)(2,1)S(1)}, bf16[2,256,128]{2,1,0:T(8,128)(2,1)S(1)}, u32[]{:S(2)}, u32[]{:S(2)}) %collective-permute-start.2) | collective-permute-done | bytes 131104 | tf_op jit(solution)/shard_map/query_exchange/ppermute | solution.py:331
  35.5 3.0 %collective-permute-start.9 = (bf16[4,256,128]{2,1,0:T(8,128)(2,1)S(1)}, bf16[4,256,128]{2,1,0:T(8,128)(2,1)S(1)}, u32[]{:S(2)}, u32[]{:S(2)}) collective-permute-start(bf16[4,256,128]{2,1,0:T(8,128)(2,1)S(1)} %join.3.refs_0_), channel_id=1, source_target_pairs={{0,4},{1,5},{2,6},{3,7},{4,0},{5,1},{6,2},{7,3},{8,12},{9,13},{10,... | collective-permute-start | bytes 786440 | tf_op jit(solution)/shard_map/query_exchange/ppermute | solution.py:331
  38.6 0.6 collective-permute-start.15
  39.2 0.9 %collective-permute-start.16 = (bf16[2,128,1024]{2,1,0:T(8,128)(2,1)S(1)}, bf16[2,128,1024]{2,1,0:T(8,128)(2,1)S(1)}, u32[]{:S(2)}, u32[]{:S(2)}) collective-permute-start(bf16[2,128,1024]{2,1,0:T(8,128)(2,1)S(1)} %pair_up.5), channel_id=1, source_target_pairs={{0,2},{1,3},{2,0},{3,1},{4,6},{5,7},{6,4},{7,5},{8,10},{9,11},{10,... | collective-permute-start | bytes 1572872 | tf_op jit(solution)/shard_map/weight_third/ppermute | solution.py:331
  40.1 2.8 %collective-permute-done.9.refs_1_ = bf16[4,256,128]{2,1,0:T(8,128)(2,1)S(1)} collective-permute-done((bf16[4,256,128]{2,1,0:T(8,128)(2,1)S(1)}, bf16[4,256,128]{2,1,0:T(8,128)(2,1)S(1)}, u32[]{:S(2)}, u32[]{:S(2)}) %collective-permute-start.9) | collective-permute-done | bytes 262176 | tf_op jit(solution)/shard_map/query_exchange/ppermute | solution.py:331
  43.5 0.8 %collective-permute-done.11.refs_3_ = bf16[2,256,128]{2,1,0:T(8,128)(2,1)S(1)} collective-permute-done((bf16[2,256,128]{2,1,0:T(8,128)(2,1)S(1)}, bf16[2,256,128]{2,1,0:T(8,128)(2,1)S(1)}, u32[]{:S(2)}, u32[]{:S(2)}) %collective-permute-start.11) | collective-permute-done | bytes 131104 | tf_op jit(solution)/shard_map/query_exchange/ppermute | solution.py:331
  44.5 2.8 %raw_scores.1 = (f32[16,32]{1,0:T(8,128)S(1)}, f32[16,128]{1,0:T(8,128)S(1)}) custom-call(bf16[4,256,128]{2,1,0:T(8,128)(2,1)S(1)} %join.3.refs_0_, bf16[4,256,128]{2,1,0:T(8,128)(2,1)S(1)} %collective-permute-done.9.refs_1_, bf16[4,256,128]{2,1,0:T(8,128)(2,1)S(1)} %collective-permute-done.10.refs_2_, ...), custom_call_target="tpu_custom_call" | custom-call | flops 1 | bytes 1 | tf_op jit(solution)/shard_map/raw_scores/pallas_call | solution.py:186
  47.7 0.8 %collective-permute-done.13 = f32[16,128]{1,0:T(8,128)S(1)} collective-permute-done((f32[16,128]{1,0:T(8,128)S(1)}, f32[16,128]{1,0:T(8,128)S(1)}, u32[]{:S(2)}, u32[]{:S(2)}) %collective-permute-start.13) | collective-permute-done | bytes 8224 | tf_op jit(solution)/shard_map/power/ppermute | solution.py:331
  48.6 1.4 %collective-permute-start.14 = (f32[16,128]{1,0:T(8,128)S(1)}, f32[16,128]{1,0:T(8,128)S(1)}, u32[]{:S(2)}, u32[]{:S(2)}) collective-permute-start(f32[16,128]{1,0:T(8,128)S(1)} %add.16), channel_id=1, source_target_pairs={{0,2},{1,3},{2,0},{3,1},{4,6},{5,7},{6,4},{7,5},{8,10},{9,11},{10,... | collective-permute-start | bytes 24584 | tf_op jit(solution)/shard_map/power/ppermute | solution.py:331
  49.9 2.1 %columns_1.1 = (bf16[512,4096]{1,0:T(8,128)(2,1)}, bf16[2,512,256]{2,1,0:T(8,128)(2,1)S(1)}) custom-call(bf16[512,1024]{1,0:T(8,128)(2,1)S(1)} %copy-done.1, bf16[512,1024]{1,0:T(8,128)(2,1)S(1)} %collective-permute-done.refs_1_.refs_0_, bf16[128,1024]{1,0:T(8,128)(2,1)S(1)} %collective-permute-done.3.first.refs_2_, ...), custom_call_target="tpu_custom_call", output_to_operand_aliasing={{0}: (6, {})} | custom-call | flops 1 | bytes 1 | tf_op jit(solution)/shard_map/input_grad/columns_1/pallas_call | solution.py:274
  52.2 1.2 %columns_2.3 = bf16[3,512,256]{2,1,0:T(8,128)(2,1)S(1)} custom-call(bf16[512,1024]{1,0:T(8,128)(2,1)S(1)} %collective-permute-done.refs_1_.refs_0_, bf16[128,1024]{1,0:T(8,128)(2,1)S(1)} %collective-permute-done.7.first.refs_1_, bf16[2,128,1024]{2,1,0:T(8,128)(2,1)S(1)} %collective-permute-done.15.refs_2_.refs_4_, ...), custom_call_target="tpu_custom_call" | custom-call | flops 1 | bytes 1 | tf_op jit(solution)/shard_map/power/input_grad/columns_2/pallas_call | solution.py:274
  53.5 0.6 collective-permute-start.19
  54.7 2.0 %collective-permute-start.17 = (f32[16,128]{1,0:T(8,128)S(1)}, f32[16,128]{1,0:T(8,128)S(1)}, u32[]{:S(2)}, u32[]{:S(2)}) collective-permute-start(f32[16,128]{1,0:T(8,128)S(1)} %add.17), channel_id=1, source_target_pairs={{0,4},{1,5},{2,6},{3,7},{4,0},{5,1},{6,2},{7,3},{8,12},{9,13},{10,... | collective-permute-start | bytes 24584 | tf_op jit(solution)/shard_map/power/ppermute | solution.py:331
  56.7 1.6 %collective-permute-done.17 = f32[16,128]{1,0:T(8,128)S(1)} collective-permute-done((f32[16,128]{1,0:T(8,128)S(1)}, f32[16,128]{1,0:T(8,128)S(1)}, u32[]{:S(2)}, u32[]{:S(2)}) %collective-permute-start.17) | collective-permute-done | bytes 8224 | tf_op jit(solution)/shard_map/power/ppermute | solution.py:331
  58.3 2.3 %collective-permute-start.18 = (f32[16,128]{1,0:T(8,128)S(1)}, f32[16,128]{1,0:T(8,128)S(1)}, u32[]{:S(2)}, u32[]{:S(2)}) collective-permute-start(f32[16,128]{1,0:T(8,128)S(1)} %add.18), channel_id=1, source_target_pairs={{0,8},{1,9},{2,10},{3,11},{4,12},{5,13},{6,14},{7,15},{8,0},{9,1},... | collective-permute-start | bytes 24584 | tf_op jit(solution)/shard_map/power/ppermute | solution.py:331
  60.7 2.0 %columns_2.2.refs_3_ = bf16[512,4096]{1,0:T(8,128)(2,1)} custom-call(bf16[512,1024]{1,0:T(8,128)(2,1)S(1)} %copy-done.1, bf16[128,1024]{1,0:T(8,128)(2,1)S(1)} %collective-permute-done.7.first.refs_1_, bf16[2,128,1024]{2,1,0:T(8,128)(2,1)S(1)} %collective-permute-done.15.refs_2_.refs_4_, ...), custom_call_target="tpu_custom_call", output_to_operand_aliasing={{}: (7, {})} | custom-call | flops 1 | bytes 1 | tf_op jit(solution)/shard_map/power/input_grad/columns_2/pallas_call | solution.py:274
  63.5 1.2 %columns_3.3.refs_6_ = bf16[512,4096]{1,0:T(8,128)(2,1)} custom-call(bf16[512,1024]{1,0:T(8,128)(2,1)S(1)} %copy-done.1, bf16[2,128,1024]{2,1,0:T(8,128)(2,1)S(1)} %collective-permute-done.16.refs_6_.refs_1_, bf16[128,1024]{1,0:T(8,128)(2,1)S(1)} %collective-permute-done.19.refs_2_, bf16[512,4096]{1,0:T(8,128)(2,1)} %columns_2.2.refs_3_), custom_call_target="tpu_custom_call", output_to_operand_aliasing={{}: (3, {})} | custom-call | flops 1 | bytes 1 | tf_op jit(solution)/shard_map/input_grad/columns_3/pallas_call | solution.py:274
  65.0 2.2 %place_columns.1 = (bf16[512,4096]{1,0:T(8,128)(2,1)}, f32[16,32]{1,0:T(8,128)}) custom-call(s32[1,512]{1,0:T(1,128)S(1)} %copy-done.5, f32[16,32]{1,0:T(8,128)S(1)} %get-tuple-element.35.refs_0_, f32[16,128]{1,0:T(8,128)S(1)} %add.19.refs_1_, bf16[2,512,256]{2,1,0:T(8,128)(2,1)S(1)} %collective-permute-done.20.refs_2_, ...), custom_call_target="tpu_custom_call", output_to_operand_aliasing={{0}: (7, {})} | custom-call | flops 1 | bytes 1 | tf_op jit(solution)/shard_map/place_columns/pallas_call | solution.py:314
  (49 shorter events, 4.6 us)
Async XLA Ops:
  0.6 30.4 %copy-start.3 = (bf16[256,1024]{1,0:T(8,128)(2,1)S(1)}, bf16[256,1024]{1,0:T(8,128)(2,1)}, u32[]{:S(2)}) copy-start(bf16[256,1024]{1,0:T(8,128)(2,1)} %refs_2_.1) | copy-start | bytes 1572868
  0.6 22.7 %collective-permute-start = (bf16[512,1024]{1,0:T(8,128)(2,1)}, bf16[512,1024]{1,0:T(8,128)(2,1)S(1)}, u32[]{:S(2)}, u32[]{:S(2)}) collective-permute-start(bf16[512,1024]{1,0:T(8,128)(2,1)} %up_hbm.1), channel_id=1, source_target_pairs={{0,1},{1,0},{2,3},{3,2},{4,5},{5,4},{6,7},{7,6},{8,9},{9,8},{10,11... | collective-permute-start | bytes 3145736 | tf_op jit(solution)/shard_map/weight_first/ppermute | solution.py:331
  2.1 15.1 %collective-permute-start.3 = (bf16[128,1024]{1,0:T(8,128)(2,1)S(1)}, bf16[128,1024]{1,0:T(8,128)(2,1)S(1)}, u32[]{:S(2)}, u32[]{:S(2)}) collective-permute-start(bf16[128,1024]{1,0:T(8,128)(2,1)S(1)} %constant_dynamic-slice_fusion), channel_id=1, source_target_pairs={{0,4},{1,5},{2,6},{3,7},{4,0},{5,1},{6,2},{7,3},{8,12},{9,13},{10,... | collective-permute-start | bytes 786440 | tf_op jit(solution)/shard_map/weight_first/ppermute | solution.py:331
  4.8 14.9 %collective-permute-start.4 = (bf16[128,1024]{1,0:T(8,128)(2,1)S(1)}, bf16[128,1024]{1,0:T(8,128)(2,1)S(1)}, u32[]{:S(2)}, u32[]{:S(2)}) collective-permute-start(bf16[128,1024]{1,0:T(8,128)(2,1)S(1)} %constant_dynamic-slice_fusion), channel_id=1, source_target_pairs={{0,8},{1,9},{2,10},{3,11},{4,12},{5,13},{6,14},{7,15},{8,0},{9,1},... | collective-permute-start | bytes 786440 | tf_op jit(solution)/shard_map/weight_first/ppermute | solution.py:331
  7.4 23.6 %collective-permute-start.8 = (bf16[256,1024]{1,0:T(8,128)(2,1)}, bf16[256,1024]{1,0:T(8,128)(2,1)S(1)}, u32[]{:S(2)}, u32[]{:S(2)}) collective-permute-start(bf16[256,1024]{1,0:T(8,128)(2,1)} %refs_2_.1), channel_id=1, source_target_pairs={{0,2},{1,3},{2,0},{3,1},{4,6},{5,7},{6,4},{7,5},{8,10},{9,11},{10,... | collective-permute-start | bytes 1572872 | tf_op jit(solution)/shard_map/weight_first/ppermute | solution.py:331
  9.0 35.6 %copy-start.2 = (bf16[32,32768]{1,0:T(8,128)(2,1)S(1)}, bf16[32,32768]{1,0:T(8,128)(2,1)}, u32[]{:S(2)}) copy-start(bf16[32,32768]{1,0:T(8,128)(2,1)} %refs_5_.1) | copy-start | bytes 6291460
  19.8 14.5 %collective-permute-start.5 = (bf16[2,128,1024]{2,1,0:T(8,128)(2,1)S(1)}, bf16[2,128,1024]{2,1,0:T(8,128)(2,1)S(1)}, u32[]{:S(2)}, u32[]{:S(2)}) collective-permute-start(bf16[2,128,1024]{2,1,0:T(8,128)(2,1)S(1)} %pair_up.3), channel_id=1, source_target_pairs={{0,16},{16,0},{1,17},{17,1},{2,18},{18,2},{3,19},{19,3},{4,20},{20... | collective-permute-start | bytes 1572872 | tf_op jit(solution)/shard_map/weight_second/ppermute | solution.py:331
  21.4 13.0 %collective-permute-start.6 = (bf16[2,128,1024]{2,1,0:T(8,128)(2,1)S(1)}, bf16[2,128,1024]{2,1,0:T(8,128)(2,1)S(1)}, u32[]{:S(2)}, u32[]{:S(2)}) collective-permute-start(bf16[2,128,1024]{2,1,0:T(8,128)(2,1)S(1)} %pair_up.3), channel_id=1, source_target_pairs={{0,2},{1,3},{2,0},{3,1},{4,6},{5,7},{6,4},{7,5},{8,10},{9,11},{10,... | collective-permute-start | bytes 1572872 | tf_op jit(solution)/shard_map/weight_second/ppermute | solution.py:331
  22.9 11.4 %collective-permute-start.7 = (bf16[128,1024]{1,0:T(8,128)(2,1)S(1)}, bf16[128,1024]{1,0:T(8,128)(2,1)S(1)}, u32[]{:S(2)}, u32[]{:S(2)}) collective-permute-start(bf16[128,1024]{1,0:T(8,128)(2,1)S(1)} %collective-permute-done.4.second.refs_4_), channel_id=1, source_target_pairs={{0,4},{1,5},{2,6},{3,7},{4,0},{5,1},{6,2},{7,3},{8,12},{9,13},{10,... | collective-permute-start | bytes 786440 | tf_op jit(solution)/shard_map/weight_second/ppermute | solution.py:331
  23.4 6.3 %collective-permute-start.1 = (bf16[1,256,128]{2,1,0:T(8,128)(2,1)}, bf16[1,256,128]{2,1,0:T(8,128)(2,1)S(1)}, u32[]{:S(2)}, u32[]{:S(2)}) collective-permute-start(bf16[1,256,128]{2,1,0:T(8,128)(2,1)} %get-tuple-element.28.first), channel_id=1, source_target_pairs={{0,8},{1,9},{2,10},{3,11},{4,12},{5,13},{6,14},{7,15},{8,0},{9,1},... | collective-permute-start | bytes 196616 | tf_op jit(solution)/shard_map/query_exchange/ppermute | solution.py:331
  29.6 0.8 %copy-start.4 = (bf16[1,256,128]{2,1,0:T(8,128)(2,1)S(1)}, bf16[1,256,128]{2,1,0:T(8,128)(2,1)}, u32[]{:S(2)}) copy-start(bf16[1,256,128]{2,1,0:T(8,128)(2,1)} %get-tuple-element.28.first) | copy-start | bytes 196612
  30.5 5.0 %collective-permute-start.2 = (bf16[2,256,128]{2,1,0:T(8,128)(2,1)S(1)}, bf16[2,256,128]{2,1,0:T(8,128)(2,1)S(1)}, u32[]{:S(2)}, u32[]{:S(2)}) collective-permute-start(bf16[2,256,128]{2,1,0:T(8,128)(2,1)S(1)} %join.2.first), channel_id=1, source_target_pairs={{0,2},{1,3},{2,0},{3,1},{4,6},{5,7},{6,4},{7,5},{8,10},{9,11},{10,... | collective-permute-start | bytes 393224 | tf_op jit(solution)/shard_map/query_exchange/ppermute | solution.py:331
  31.1 1.2 %copy-start = (bf16[512,1024]{1,0:T(8,128)(2,1)S(1)}, bf16[512,1024]{1,0:T(8,128)(2,1)}, u32[]{:S(2)}) copy-start(bf16[512,1024]{1,0:T(8,128)(2,1)} %get-tuple-element.31.refs_0_) | copy-start | bytes 3145732
  34.3 15.6 %copy-start.1 = (bf16[512,1024]{1,0:T(8,128)(2,1)S(1)}, bf16[512,1024]{1,0:T(8,128)(2,1)}, u32[]{:S(2)}) copy-start(bf16[512,1024]{1,0:T(8,128)(2,1)} %get-tuple-element.31.refs_0_) | copy-start | bytes 3145732
  35.5 7.4 %collective-permute-start.9 = (bf16[4,256,128]{2,1,0:T(8,128)(2,1)S(1)}, bf16[4,256,128]{2,1,0:T(8,128)(2,1)S(1)}, u32[]{:S(2)}, u32[]{:S(2)}) collective-permute-start(bf16[4,256,128]{2,1,0:T(8,128)(2,1)S(1)} %join.3.refs_0_), channel_id=1, source_target_pairs={{0,4},{1,5},{2,6},{3,7},{4,0},{5,1},{6,2},{7,3},{8,12},{9,13},{10,... | collective-permute-start | bytes 786440 | tf_op jit(solution)/shard_map/query_exchange/ppermute | solution.py:331
  38.6 13.6 %collective-permute-start.15 = (bf16[2,128,1024]{2,1,0:T(8,128)(2,1)S(1)}, bf16[2,128,1024]{2,1,0:T(8,128)(2,1)S(1)}, u32[]{:S(2)}, u32[]{:S(2)}) collective-permute-start(bf16[2,128,1024]{2,1,0:T(8,128)(2,1)S(1)} %pair_up.4), channel_id=1, source_target_pairs={{0,16},{16,0},{1,17},{17,1},{2,18},{18,2},{3,19},{19,3},{4,20},{20... | collective-permute-start | bytes 1572872 | tf_op jit(solution)/shard_map/weight_third/ppermute | solution.py:331
  39.2 13.0 %collective-permute-start.16 = (bf16[2,128,1024]{2,1,0:T(8,128)(2,1)S(1)}, bf16[2,128,1024]{2,1,0:T(8,128)(2,1)S(1)}, u32[]{:S(2)}, u32[]{:S(2)}) collective-permute-start(bf16[2,128,1024]{2,1,0:T(8,128)(2,1)S(1)} %pair_up.5), channel_id=1, source_target_pairs={{0,2},{1,3},{2,0},{3,1},{4,6},{5,7},{6,4},{7,5},{8,10},{9,11},{10,... | collective-permute-start | bytes 1572872 | tf_op jit(solution)/shard_map/weight_third/ppermute | solution.py:331
  40.1 3.4 %collective-permute-start.10 = (bf16[4,256,128]{2,1,0:T(8,128)(2,1)S(1)}, bf16[4,256,128]{2,1,0:T(8,128)(2,1)S(1)}, u32[]{:S(2)}, u32[]{:S(2)}) collective-permute-start(bf16[4,256,128]{2,1,0:T(8,128)(2,1)S(1)} %join.3.refs_0_), channel_id=1, source_target_pairs={{0,1},{1,0},{2,3},{3,2},{4,5},{5,4},{6,7},{7,6},{8,9},{9,8},{10,11... | collective-permute-start | bytes 786440 | tf_op jit(solution)/shard_map/query_exchange/ppermute | solution.py:331
  42.9 1.4 %collective-permute-start.11 = (bf16[2,256,128]{2,1,0:T(8,128)(2,1)S(1)}, bf16[2,256,128]{2,1,0:T(8,128)(2,1)S(1)}, u32[]{:S(2)}, u32[]{:S(2)}) collective-permute-start(bf16[2,256,128]{2,1,0:T(8,128)(2,1)S(1)} %get-tuple-element.53), channel_id=1, source_target_pairs={{0,1},{1,0},{2,3},{3,2},{4,5},{5,4},{6,7},{7,6},{8,9},{9,8},{10,11... | collective-permute-start | bytes 393224 | tf_op jit(solution)/shard_map/query_exchange/ppermute | solution.py:331
  43.0 1.5 %collective-permute-start.12 = (bf16[2,256,128]{2,1,0:T(8,128)(2,1)S(1)}, bf16[2,256,128]{2,1,0:T(8,128)(2,1)S(1)}, u32[]{:S(2)}, u32[]{:S(2)}) collective-permute-start(bf16[2,256,128]{2,1,0:T(8,128)(2,1)S(1)} %get-tuple-element.52), channel_id=1, source_target_pairs={{0,1},{1,0},{2,3},{3,2},{4,5},{5,4},{6,7},{7,6},{8,9},{9,8},{10,11... | collective-permute-start | bytes 393224 | tf_op jit(solution)/shard_map/query_exchange/ppermute | solution.py:331
  47.3 1.2 %collective-permute-start.13 = (f32[16,128]{1,0:T(8,128)S(1)}, f32[16,128]{1,0:T(8,128)S(1)}, u32[]{:S(2)}, u32[]{:S(2)}) collective-permute-start(f32[16,128]{1,0:T(8,128)S(1)} %get-tuple-element.36), channel_id=1, source_target_pairs={{0,1},{1,0},{2,3},{3,2},{4,5},{5,4},{6,7},{7,6},{8,9},{9,8},{10,11... | collective-permute-start | bytes 24584 | tf_op jit(solution)/shard_map/power/ppermute | solution.py:331
  48.6 3.7 %collective-permute-start.14 = (f32[16,128]{1,0:T(8,128)S(1)}, f32[16,128]{1,0:T(8,128)S(1)}, u32[]{:S(2)}, u32[]{:S(2)}) collective-permute-start(f32[16,128]{1,0:T(8,128)S(1)} %add.16), channel_id=1, source_target_pairs={{0,2},{1,3},{2,0},{3,1},{4,6},{5,7},{6,4},{7,5},{8,10},{9,11},{10,... | collective-permute-start | bytes 24584 | tf_op jit(solution)/shard_map/power/ppermute | solution.py:331
  53.4 11.6 %collective-permute-start.22 = (bf16[3,512,256]{2,1,0:T(8,128)(2,1)S(1)}, bf16[3,512,256]{2,1,0:T(8,128)(2,1)S(1)}, u32[]{:S(2)}, u32[]{:S(2)}) collective-permute-start(bf16[3,512,256]{2,1,0:T(8,128)(2,1)S(1)} %columns_2.3), channel_id=1, source_target_pairs={{0,1},{1,0},{2,3},{3,2},{4,5},{5,4},{6,7},{7,6},{8,9},{9,8},{10,11... | collective-permute-start | bytes 2359304 | tf_op jit(solution)/shard_map/power/input_grad/ppermute | solution.py:331
  53.5 9.3 %collective-permute-start.19 = (bf16[128,1024]{1,0:T(8,128)(2,1)S(1)}, bf16[128,1024]{1,0:T(8,128)(2,1)S(1)}, u32[]{:S(2)}, u32[]{:S(2)}) collective-permute-start(bf16[128,1024]{1,0:T(8,128)(2,1)S(1)} %slice_bitcast_fusion), channel_id=1, source_target_pairs={{0,16},{16,0},{1,17},{17,1},{2,18},{18,2},{3,19},{19,3},{4,20},{20... | collective-permute-start | bytes 786440 | tf_op jit(solution)/shard_map/power/ppermute | solution.py:331
  54.1 10.6 %collective-permute-start.20 = (bf16[2,512,256]{2,1,0:T(8,128)(2,1)S(1)}, bf16[2,512,256]{2,1,0:T(8,128)(2,1)S(1)}, u32[]{:S(2)}, u32[]{:S(2)}) collective-permute-start(bf16[2,512,256]{2,1,0:T(8,128)(2,1)S(1)} %get-tuple-element.48), channel_id=1, source_target_pairs={{0,1},{1,0},{2,3},{3,2},{4,5},{5,4},{6,7},{7,6},{8,9},{9,8},{10,11... | collective-permute-start | bytes 1572872 | tf_op jit(solution)/shard_map/input_grad/ppermute | solution.py:331
  54.4 10.4 %collective-permute-start.21 = (bf16[2,512,256]{2,1,0:T(8,128)(2,1)S(1)}, bf16[2,512,256]{2,1,0:T(8,128)(2,1)S(1)}, u32[]{:S(2)}, u32[]{:S(2)}) collective-permute-start(bf16[2,512,256]{2,1,0:T(8,128)(2,1)S(1)} %get-tuple-element.49), channel_id=1, source_target_pairs={{0,1},{1,0},{2,3},{3,2},{4,5},{5,4},{6,7},{7,6},{8,9},{9,8},{10,11... | collective-permute-start | bytes 1572872 | tf_op jit(solution)/shard_map/input_grad/ppermute | solution.py:331
  54.7 3.7 %collective-permute-start.17 = (f32[16,128]{1,0:T(8,128)S(1)}, f32[16,128]{1,0:T(8,128)S(1)}, u32[]{:S(2)}, u32[]{:S(2)}) collective-permute-start(f32[16,128]{1,0:T(8,128)S(1)} %add.17), channel_id=1, source_target_pairs={{0,4},{1,5},{2,6},{3,7},{4,0},{5,1},{6,2},{7,3},{8,12},{9,13},{10,... | collective-permute-start | bytes 24584 | tf_op jit(solution)/shard_map/power/ppermute | solution.py:331
  58.3 4.5 %collective-permute-start.18 = (f32[16,128]{1,0:T(8,128)S(1)}, f32[16,128]{1,0:T(8,128)S(1)}, u32[]{:S(2)}, u32[]{:S(2)}) collective-permute-start(f32[16,128]{1,0:T(8,128)S(1)} %add.18), channel_id=1, source_target_pairs={{0,8},{1,9},{2,10},{3,11},{4,12},{5,13},{6,14},{7,15},{8,0},{9,1},... | collective-permute-start | bytes 24584 | tf_op jit(solution)/shard_map/power/ppermute | solution.py:331
  63.4 1.6 %copy-start.5 = (s32[1,512]{1,0:T(1,128)S(1)}, s32[1,512]{1,0:T(1,128)}, u32[]{:S(2)}) copy-start(s32[1,512]{1,0:T(1,128)} %ids.3) | copy-start | bytes 6148
  63.4 1.6 %collective-permute-start.23 = (bf16[1,512,256]{2,1,0:T(8,128)(2,1)S(1)}, bf16[1,512,256]{2,1,0:T(8,128)(2,1)S(1)}, u32[]{:S(2)}, u32[]{:S(2)}) collective-permute-start(bf16[1,512,256]{2,1,0:T(8,128)(2,1)S(1)} %columns_3.2), channel_id=1, source_target_pairs={{0,1},{1,0},{2,3},{3,2},{4,5},{5,4},{6,7},{7,6},{8,9},{9,8},{10,11... | collective-permute-start | bytes 786440 | tf_op jit(solution)/shard_map/input_grad/ppermute | solution.py:331

commit v7 on v6

--- a/solution.py
+++ b/solution.py
@@ -112,6 +112,23 @@
     both[count:] = second[...]
 
 
+def near_copy_kernel(value, copied):
+    copied[...] = value[...]
+
+
+def near_copy(value):
+    vmem = pl.BlockSpec(memory_space=VMEM)
+    return pl.pallas_call(
+        near_copy_kernel,
+        in_specs=[vmem],
+        out_specs=vmem,
+        out_shape=jax.ShapeDtypeStruct(value.shape, value.dtype),
+        compiler_params=params(),
+        cost_estimate=SMALL,
+        name="near_copy",
+    )(value)
+
+
 def join(first, second):
     vmem = pl.BlockSpec(memory_space=VMEM)
     shape = (first.shape[0] + second.shape[0], *first.shape[1:])
@@ -347,7 +364,7 @@
     with jax.named_scope("weight_first"):
         upstream_other = ring(core, upstream)
         near = own_half(w_value)
-        beside, h4, h8 = ring(side, w_value), ring(4, near), ring(8, near)
+        h8, h4, beside = ring(8, near), ring(4, near), ring(side, w_value)
     masked, grad = query_gradient(
         token_ids, upstream, hidden, proj_in, proj_out, in_inverse, out_inverse
     )
@@ -368,9 +385,9 @@
             return [*made[:-1], ring(core, made[-1])] if other else made
 
     with jax.named_scope("weight_second"):
-        h4, h8 = after((h4, h8), grad)
-        both = pair_up(h4, h8)
-        x48, y48, h12 = cross(both), ring(side, both), ring(4, h8)
+        h8, h4 = after((h8, h4), grad)
+        both = pair_up(h8, h4)
+        x84, y84, h12 = cross(both), ring(side, both), ring(4, h8)
 
     shards[side] = (beside,), False
     out, back = stage_columns(0, None)
@@ -380,12 +397,14 @@
         held, order = after(grad, upstream_other), [0]
         for bit in (8, side):
             came = ring(bit, held)
+            if bit == 8:
+                held = near_copy(held)
             if bit == side:
-                held, came, x48, y48, h12, out = lax.optimization_barrier(
-                    (held, came, x48, y48, h12, out)
+                held, came, x84, y84, h12, out = lax.optimization_barrier(
+                    (held, came, x84, y84, h12, out)
                 )
             held, order = join(held, came), order + [b ^ bit for b in order]
-        shards.update({4: ((h4, (x48, 0)), True), 8: ((h8, (x48, 1)), True)})
+        shards.update({4: ((h4, (x84, 1)), True), 8: ((h8, (x84, 0)), True)})
         came = ring(4, held)
         cut = came.shape[0] // 2
         groups = [held, came, ring(core, held), ring(core, came[:cut]), ring(core, came[cut:])]
@@ -393,7 +412,7 @@
     raw, power = raw_score_call(order, groups, datastore)
 
     with jax.named_scope("weight_third"):
-        x12, y12 = cross(pair_up(h12, (y48, 0))), ring(side, pair_up(h12, (x48, 1)))
+        x12, y12 = cross(pair_up(h12, (y84, 1))), ring(side, pair_up(h12, (x84, 0)))
 
     out, back = stage_columns(1, after(out, power))
     came_back.append(back)
@@ -403,8 +422,8 @@
             if bit == side:
                 part, out, x12, y12 = lax.optimization_barrier((part, out, x12, y12))
                 shards[12] = (h12, (x12, 0)), True
-                shards[4 ^ side] = ((y48, 0), (x12, 1)), True
-                shards[8 ^ side] = ((y48, 1), (y12, 1)), True
+                shards[4 ^ side] = ((y84, 1), (x12, 1)), True
+                shards[8 ^ side] = ((y84, 0), (y12, 1)), True
                 d12 = cross(y12[0])
                 came_back += stage_columns(2, out, mine=False)
                 (out,) = stage_columns(2, out, other=False)

time: 67.5 us -> 68.1 us (level)
  transfers between devices with their start and end apart: 24 -> 24, of which waited for: 12 -> 11; matrix products, arithmetic and copies ran while one was open for 2% -> 2% of each run, Pallas kernels for 28% -> 27%
where the time goes in v7:
time: 68.1 us; the launch traced here: 67.8 us
  starting transfers between devices  27.1 us (40%)
  Pallas kernels  22 us (32%)
  waiting for transfers between devices  14.6 us (21%)
  local copies, waits for them, and re-layouts  3.19 us (5%)
  between operations  0.85 us (1%)
    ppermute x24, starting transfers between devices, swap(): return lax.ppermute(value, axis, [(i, i ^ bits) for i in range(size)])  27.1 us
    ppermute x24, waiting for transfers between devices, swap(): return lax.ppermute(value, axis, [(i, i ^ bits) for i in range(size)])  14.6 us
    pallas_call x6, Pallas kernels, columns(): pl.pallas_call(functools.partial(column_kernel, bits, pieces, (own, other...  9.03 us
    pallas_call x1, Pallas kernels, query_gradient(): pl.pallas_call(grad_kernel, in_specs=[whole] * 4 + [hbm] * 3, out_specs=[...  7.89 us
    pallas_call x1, Pallas kernels, raw_score_call(): pl.pallas_call(functools.partial(score_kernel, bits), in_specs=[vmem] * l...  2.79 us
    pallas_call x1, Pallas kernels, place_columns(): pl.pallas_call(functools.partial(place_kernel, bits, rows_in_all), in_spe...  2.19 us
    unnamed x12, local copies, waits for them, and re-layouts  2.12 us
  transfers between devices with their start and end apart: 24, of which 11 were waited for; matrix products, arithmetic and copies ran while one was open for 2% of the time, Pallas kernels for 27%

profile of v7, /device:TPU:0, one launch (start us, length us, event | category | flops | bytes accessed | tf_op | source)
XLA Modules:
  0.0 67.8 jit_solution(9584065672499026138)
XLA Ops:
  1.1 1.0 %constant_dynamic-slice_fusion = bf16[128,1024]{1,0:T(8,128)(2,1)S(1)} fusion(bf16[256,1024]{1,0:T(8,128)(2,1)} %refs_2_.1, s32[]{:T(128)S(6)} %select_n.3), kind=kLoop, calls=%fused_computation.1 | loop fusion | bytes 524292 | tf_op jit(solution)/shard_map/weight_first/dynamic_slice | solution.py:361
  2.2 3.7 %collective-permute-start.3 = (bf16[128,1024]{1,0:T(8,128)(2,1)S(1)}, bf16[128,1024]{1,0:T(8,128)(2,1)S(1)}, u32[]{:S(2)}, u32[]{:S(2)}) collective-permute-start(bf16[128,1024]{1,0:T(8,128)(2,1)S(1)} %constant_dynamic-slice_fusion), channel_id=1, source_target_pairs={{0,8},{1,9},{2,10},{3,11},{4,12},{5,13},{6,14},{7,15},{8,0},{9,1},... | collective-permute-start | bytes 786440 | tf_op jit(solution)/shard_map/weight_first/ppermute | solution.py:348
  5.9 1.6 %collective-permute-start.4 = (bf16[128,1024]{1,0:T(8,128)(2,1)S(1)}, bf16[128,1024]{1,0:T(8,128)(2,1)S(1)}, u32[]{:S(2)}, u32[]{:S(2)}) collective-permute-start(bf16[128,1024]{1,0:T(8,128)(2,1)S(1)} %constant_dynamic-slice_fusion), channel_id=1, source_target_pairs={{0,4},{1,5},{2,6},{3,7},{4,0},{5,1},{6,2},{7,3},{8,12},{9,13},{10,... | collective-permute-start | bytes 786440 | tf_op jit(solution)/shard_map/weight_first/ppermute | solution.py:348
  7.4 1.5 %collective-permute-start.8 = (bf16[256,1024]{1,0:T(8,128)(2,1)}, bf16[256,1024]{1,0:T(8,128)(2,1)S(1)}, u32[]{:S(2)}, u32[]{:S(2)}) collective-permute-start(bf16[256,1024]{1,0:T(8,128)(2,1)} %refs_2_.1), channel_id=1, source_target_pairs={{0,2},{1,3},{2,0},{3,1},{4,6},{5,7},{6,4},{7,5},{8,10},{9,11},{10,... | collective-permute-start | bytes 1572872 | tf_op jit(solution)/shard_map/weight_first/ppermute | solution.py:348
  9.0 7.9 %query_gradient.1 = (bf16[512,1024]{1,0:T(8,128)(2,1)}, bf16[1,256,128]{2,1,0:T(8,128)(2,1)}) custom-call(s32[1,512]{1,0:T(1,128)} %ids.3, bf16[8,64,128]{2,1,0:T(8,128)(2,1)} %bitcast.5, f32[8,64,64]{2,1,0:T(8,128)} %a_inv.1, f32[8,64,64]{2,1,0:T(8,128)} %b_inv.1, bf16[512,1024]{1,0:T(8,128)(2,1)} %up_hbm.1, bf16[512,4096]{1,0:T(8,128)(2,1)} %hid_hbm.1, ...), custom_call_target="tpu_custom_call" | custom-call | flops 1 | bytes 1 | tf_op jit(solution)/shard_map/query_gradient/pallas_call | solution.py:89
  16.9 1.7 %collective-permute-done.3.first.refs_4_ = bf16[128,1024]{1,0:T(8,128)(2,1)S(1)} collective-permute-done((bf16[128,1024]{1,0:T(8,128)(2,1)S(1)}, bf16[128,1024]{1,0:T(8,128)(2,1)S(1)}, u32[]{:S(2)}, u32[]{:S(2)}) %collective-permute-start.3) | collective-permute-done | bytes 262176 | tf_op jit(solution)/shard_map/weight_first/ppermute | solution.py:348
  18.8 1.6 %collective-permute-start.5 = (bf16[2,128,1024]{2,1,0:T(8,128)(2,1)S(1)}, bf16[2,128,1024]{2,1,0:T(8,128)(2,1)S(1)}, u32[]{:S(2)}, u32[]{:S(2)}) collective-permute-start(bf16[2,128,1024]{2,1,0:T(8,128)(2,1)S(1)} %pair_up.3), channel_id=1, source_target_pairs={{0,16},{16,0},{1,17},{17,1},{2,18},{18,2},{3,19},{19,3},{4,20},{20... | collective-permute-start | bytes 1572872 | tf_op jit(solution)/shard_map/weight_second/ppermute | solution.py:348
  20.4 1.5 %collective-permute-start.6 = (bf16[2,128,1024]{2,1,0:T(8,128)(2,1)S(1)}, bf16[2,128,1024]{2,1,0:T(8,128)(2,1)S(1)}, u32[]{:S(2)}, u32[]{:S(2)}) collective-permute-start(bf16[2,128,1024]{2,1,0:T(8,128)(2,1)S(1)} %pair_up.3), channel_id=1, source_target_pairs={{0,2},{1,3},{2,0},{3,1},{4,6},{5,7},{6,4},{7,5},{8,10},{9,11},{10,... | collective-permute-start | bytes 1572872 | tf_op jit(solution)/shard_map/weight_second/ppermute | solution.py:348
  21.9 1.4 %collective-permute-start.7 = (bf16[128,1024]{1,0:T(8,128)(2,1)S(1)}, bf16[128,1024]{1,0:T(8,128)(2,1)S(1)}, u32[]{:S(2)}, u32[]{:S(2)}) collective-permute-start(bf16[128,1024]{1,0:T(8,128)(2,1)S(1)} %collective-permute-done.3.first.refs_4_), channel_id=1, source_target_pairs={{0,4},{1,5},{2,6},{3,7},{4,0},{5,1},{6,2},{7,3},{8,12},{9,13},{10,... | collective-permute-start | bytes 786440 | tf_op jit(solution)/shard_map/weight_second/ppermute | solution.py:348
  23.3 2.3 %collective-permute-start.1 = (bf16[1,256,128]{2,1,0:T(8,128)(2,1)}, bf16[1,256,128]{2,1,0:T(8,128)(2,1)S(1)}, u32[]{:S(2)}, u32[]{:S(2)}) collective-permute-start(bf16[1,256,128]{2,1,0:T(8,128)(2,1)} %get-tuple-element.28.value), channel_id=1, source_target_pairs={{0,8},{1,9},{2,10},{3,11},{4,12},{5,13},{6,14},{7,15},{8,0},{9,1},... | collective-permute-start | bytes 196616 | tf_op jit(solution)/shard_map/query_exchange/ppermute | solution.py:348
  25.7 0.9 %copy-done.4 = bf16[1,256,128]{2,1,0:T(8,128)(2,1)S(1)} copy-done((bf16[1,256,128]{2,1,0:T(8,128)(2,1)S(1)}, bf16[1,256,128]{2,1,0:T(8,128)(2,1)}, u32[]{:S(2)}) %copy-start.4) | copy-done | bytes 65560
  26.5 3.2 %collective-permute-done.1.second = bf16[1,256,128]{2,1,0:T(8,128)(2,1)S(1)} collective-permute-done((bf16[1,256,128]{2,1,0:T(8,128)(2,1)}, bf16[1,256,128]{2,1,0:T(8,128)(2,1)S(1)}, u32[]{:S(2)}, u32[]{:S(2)}) %collective-permute-start.1) | collective-permute-done | bytes 65568 | tf_op jit(solution)/shard_map/query_exchange/ppermute | solution.py:348
  30.3 1.2 %copy-done = bf16[512,1024]{1,0:T(8,128)(2,1)S(1)} copy-done((bf16[512,1024]{1,0:T(8,128)(2,1)S(1)}, bf16[512,1024]{1,0:T(8,128)(2,1)}, u32[]{:S(2)}) %copy-start) | copy-done | bytes 1048600
  31.5 2.0 %columns_0.1 = (bf16[512,4096]{1,0:T(8,128)(2,1)}, bf16[2,512,256]{2,1,0:T(8,128)(2,1)S(1)}) custom-call(bf16[512,1024]{1,0:T(8,128)(2,1)S(1)} %copy-done, bf16[512,1024]{1,0:T(8,128)(2,1)S(1)} %collective-permute-done.refs_1_.refs_0_, bf16[256,1024]{1,0:T(8,128)(2,1)S(1)} %copy-done.3, bf16[256,1024]{1,0:T(8,128)(2,1)S(1)} %collective-permute-done.8.refs_3_), custom_call_target="tpu_custom_call" | custom-call | flops 1 | bytes 1 | tf_op jit(solution)/shard_map/input_grad/columns_0/pallas_call | solution.py:291
  33.6 1.2 %collective-permute-done.6.second.refs_3_.refs_5_ = bf16[2,128,1024]{2,1,0:T(8,128)(2,1)S(1)} collective-permute-done((bf16[2,128,1024]{2,1,0:T(8,128)(2,1)S(1)}, bf16[2,128,1024]{2,1,0:T(8,128)(2,1)S(1)}, u32[]{:S(2)}, u32[]{:S(2)}) %collective-permute-start.6) | collective-permute-done | bytes 524320 | tf_op jit(solution)/shard_map/weight_second/ppermute | solution.py:348
  34.8 1.4 %collective-permute-done.2.second = bf16[2,256,128]{2,1,0:T(8,128)(2,1)S(1)} collective-permute-done((bf16[2,256,128]{2,1,0:T(8,128)(2,1)S(1)}, bf16[2,256,128]{2,1,0:T(8,128)(2,1)S(1)}, u32[]{:S(2)}, u32[]{:S(2)}) %collective-permute-start.2) | collective-permute-done | bytes 131104 | tf_op jit(solution)/shard_map/query_exchange/ppermute | solution.py:348
  36.2 2.0 %collective-permute-start.9 = (bf16[4,256,128]{2,1,0:T(8,128)(2,1)S(1)}, bf16[4,256,128]{2,1,0:T(8,128)(2,1)S(1)}, u32[]{:S(2)}, u32[]{:S(2)}) collective-permute-start(bf16[4,256,128]{2,1,0:T(8,128)(2,1)S(1)} %join.3.refs_0_), channel_id=1, source_target_pairs={{0,4},{1,5},{2,6},{3,7},{4,0},{5,1},{6,2},{7,3},{8,12},{9,13},{10,... | collective-permute-start | bytes 786440 | tf_op jit(solution)/shard_map/query_exchange/ppermute | solution.py:348
  38.9 1.4 %collective-permute-start.16 = (bf16[2,128,1024]{2,1,0:T(8,128)(2,1)S(1)}, bf16[2,128,1024]{2,1,0:T(8,128)(2,1)S(1)}, u32[]{:S(2)}, u32[]{:S(2)}) collective-permute-start(bf16[2,128,1024]{2,1,0:T(8,128)(2,1)S(1)} %pair_up.5), channel_id=1, source_target_pairs={{0,2},{1,3},{2,0},{3,1},{4,6},{5,7},{6,4},{7,5},{8,10},{9,11},{10,... | collective-permute-start | bytes 1572872 | tf_op jit(solution)/shard_map/weight_third/ppermute | solution.py:348
  40.2 2.6 %collective-permute-done.9.refs_1_ = bf16[4,256,128]{2,1,0:T(8,128)(2,1)S(1)} collective-permute-done((bf16[4,256,128]{2,1,0:T(8,128)(2,1)S(1)}, bf16[4,256,128]{2,1,0:T(8,128)(2,1)S(1)}, u32[]{:S(2)}, u32[]{:S(2)}) %collective-permute-start.9) | collective-permute-done | bytes 262176 | tf_op jit(solution)/shard_map/query_exchange/ppermute | solution.py:348
  43.5 0.8 %collective-permute-done.11.refs_3_ = bf16[2,256,128]{2,1,0:T(8,128)(2,1)S(1)} collective-permute-done((bf16[2,256,128]{2,1,0:T(8,128)(2,1)S(1)}, bf16[2,256,128]{2,1,0:T(8,128)(2,1)S(1)}, u32[]{:S(2)}, u32[]{:S(2)}) %collective-permute-start.11) | collective-permute-done | bytes 131104 | tf_op jit(solution)/shard_map/query_exchange/ppermute | solution.py:348
  44.5 2.8 %raw_scores.1 = (f32[16,32]{1,0:T(8,128)S(1)}, f32[16,128]{1,0:T(8,128)S(1)}) custom-call(bf16[4,256,128]{2,1,0:T(8,128)(2,1)S(1)} %join.3.refs_0_, bf16[4,256,128]{2,1,0:T(8,128)(2,1)S(1)} %collective-permute-done.9.refs_1_, bf16[4,256,128]{2,1,0:T(8,128)(2,1)S(1)} %collective-permute-done.10.refs_2_, ...), custom_call_target="tpu_custom_call" | custom-call | flops 1 | bytes 1 | tf_op jit(solution)/shard_map/raw_scores/pallas_call | solution.py:203
  47.7 0.8 %collective-permute-done.13 = f32[16,128]{1,0:T(8,128)S(1)} collective-permute-done((f32[16,128]{1,0:T(8,128)S(1)}, f32[16,128]{1,0:T(8,128)S(1)}, u32[]{:S(2)}, u32[]{:S(2)}) %collective-permute-start.13) | collective-permute-done | bytes 8224 | tf_op jit(solution)/shard_map/power/ppermute | solution.py:348
  48.5 1.6 %collective-permute-start.14 = (f32[16,128]{1,0:T(8,128)S(1)}, f32[16,128]{1,0:T(8,128)S(1)}, u32[]{:S(2)}, u32[]{:S(2)}) collective-permute-start(f32[16,128]{1,0:T(8,128)S(1)} %add.16), channel_id=1, source_target_pairs={{0,2},{1,3},{2,0},{3,1},{4,6},{5,7},{6,4},{7,5},{8,10},{9,11},{10,... | collective-permute-start | bytes 24584 | tf_op jit(solution)/shard_map/power/ppermute | solution.py:348
  50.1 2.1 %columns_1.1 = (bf16[512,4096]{1,0:T(8,128)(2,1)}, bf16[2,512,256]{2,1,0:T(8,128)(2,1)S(1)}) custom-call(bf16[512,1024]{1,0:T(8,128)(2,1)S(1)} %copy-done.1, bf16[512,1024]{1,0:T(8,128)(2,1)S(1)} %collective-permute-done.refs_1_.refs_0_, bf16[128,1024]{1,0:T(8,128)(2,1)S(1)} %collective-permute-done.4.second.refs_2_, ...), custom_call_target="tpu_custom_call", output_to_operand_aliasing={{0}: (6, {})} | custom-call | flops 1 | bytes 1 | tf_op jit(solution)/shard_map/input_grad/columns_1/pallas_call | solution.py:291
  52.2 1.2 %columns_2.3 = bf16[3,512,256]{2,1,0:T(8,128)(2,1)S(1)} custom-call(bf16[512,1024]{1,0:T(8,128)(2,1)S(1)} %collective-permute-done.refs_1_.refs_0_, bf16[128,1024]{1,0:T(8,128)(2,1)S(1)} %collective-permute-done.7.first.refs_1_, bf16[2,128,1024]{2,1,0:T(8,128)(2,1)S(1)} %collective-permute-done.15.refs_2_.refs_4_, ...), custom_call_target="tpu_custom_call" | custom-call | flops 1 | bytes 1 | tf_op jit(solution)/shard_map/power/input_grad/columns_2/pallas_call | solution.py:291
  53.6 0.9 %collective-permute-start.19 = (bf16[128,1024]{1,0:T(8,128)(2,1)S(1)}, bf16[128,1024]{1,0:T(8,128)(2,1)S(1)}, u32[]{:S(2)}, u32[]{:S(2)}) collective-permute-start(bf16[128,1024]{1,0:T(8,128)(2,1)S(1)} %slice_bitcast_fusion), channel_id=1, source_target_pairs={{0,16},{16,0},{1,17},{17,1},{2,18},{18,2},{3,19},{19,3},{4,20},{20... | collective-permute-start | bytes 786440 | tf_op jit(solution)/shard_map/power/ppermute | solution.py:348
  55.0 1.5 %collective-permute-start.17 = (f32[16,128]{1,0:T(8,128)S(1)}, f32[16,128]{1,0:T(8,128)S(1)}, u32[]{:S(2)}, u32[]{:S(2)}) collective-permute-start(f32[16,128]{1,0:T(8,128)S(1)} %add.17), channel_id=1, source_target_pairs={{0,4},{1,5},{2,6},{3,7},{4,0},{5,1},{6,2},{7,3},{8,12},{9,13},{10,... | collective-permute-start | bytes 24584 | tf_op jit(solution)/shard_map/power/ppermute | solution.py:348
  56.4 2.2 %collective-permute-done.17 = f32[16,128]{1,0:T(8,128)S(1)} collective-permute-done((f32[16,128]{1,0:T(8,128)S(1)}, f32[16,128]{1,0:T(8,128)S(1)}, u32[]{:S(2)}, u32[]{:S(2)}) %collective-permute-start.17) | collective-permute-done | bytes 8224 | tf_op jit(solution)/shard_map/power/ppermute | solution.py:348
  58.6 2.8 %collective-permute-start.18 = (f32[16,128]{1,0:T(8,128)S(1)}, f32[16,128]{1,0:T(8,128)S(1)}, u32[]{:S(2)}, u32[]{:S(2)}) collective-permute-start(f32[16,128]{1,0:T(8,128)S(1)} %add.18), channel_id=1, source_target_pairs={{0,8},{1,9},{2,10},{3,11},{4,12},{5,13},{6,14},{7,15},{8,0},{9,1},... | collective-permute-start | bytes 24584 | tf_op jit(solution)/shard_map/power/ppermute | solution.py:348
  61.5 2.0 %columns_2.2.refs_3_ = bf16[512,4096]{1,0:T(8,128)(2,1)} custom-call(bf16[512,1024]{1,0:T(8,128)(2,1)S(1)} %copy-done.1, bf16[128,1024]{1,0:T(8,128)(2,1)S(1)} %collective-permute-done.7.first.refs_1_, bf16[2,128,1024]{2,1,0:T(8,128)(2,1)S(1)} %collective-permute-done.15.refs_2_.refs_4_, ...), custom_call_target="tpu_custom_call", output_to_operand_aliasing={{}: (7, {})} | custom-call | flops 1 | bytes 1 | tf_op jit(solution)/shard_map/power/input_grad/columns_2/pallas_call | solution.py:291
  64.1 1.2 %columns_3.3.refs_6_ = bf16[512,4096]{1,0:T(8,128)(2,1)} custom-call(bf16[512,1024]{1,0:T(8,128)(2,1)S(1)} %copy-done.1, bf16[2,128,1024]{2,1,0:T(8,128)(2,1)S(1)} %collective-permute-done.16.refs_6_.refs_1_, bf16[128,1024]{1,0:T(8,128)(2,1)S(1)} %collective-permute-done.19.refs_2_, bf16[512,4096]{1,0:T(8,128)(2,1)} %columns_2.2.refs_3_), custom_call_target="tpu_custom_call", output_to_operand_aliasing={{}: (3, {})} | custom-call | flops 1 | bytes 1 | tf_op jit(solution)/shard_map/input_grad/columns_3/pallas_call | solution.py:291
  65.6 2.2 %place_columns.1 = (bf16[512,4096]{1,0:T(8,128)(2,1)}, f32[16,32]{1,0:T(8,128)}) custom-call(s32[1,512]{1,0:T(1,128)S(1)} %copy-done.5, f32[16,32]{1,0:T(8,128)S(1)} %get-tuple-element.35.refs_0_, f32[16,128]{1,0:T(8,128)S(1)} %add.19.refs_1_, bf16[2,512,256]{2,1,0:T(8,128)(2,1)S(1)} %collective-permute-done.20.refs_2_, ...), custom_call_target="tpu_custom_call", output_to_operand_aliasing={{0}: (7, {})} | custom-call | flops 1 | bytes 1 | tf_op jit(solution)/shard_map/place_columns/pallas_call | solution.py:331
  (50 shorter events, 4.7 us)
Async XLA Ops:
  0.6 22.7 %collective-permute-start = (bf16[512,1024]{1,0:T(8,128)(2,1)}, bf16[512,1024]{1,0:T(8,128)(2,1)S(1)}, u32[]{:S(2)}, u32[]{:S(2)}) collective-permute-start(bf16[512,1024]{1,0:T(8,128)(2,1)} %up_hbm.1), channel_id=1, source_target_pairs={{0,1},{1,0},{2,3},{3,2},{4,5},{5,4},{6,7},{7,6},{8,9},{9,8},{10,11... | collective-permute-start | bytes 3145736 | tf_op jit(solution)/shard_map/weight_first/ppermute | solution.py:348
  1.1 29.2 %copy-start.3 = (bf16[256,1024]{1,0:T(8,128)(2,1)S(1)}, bf16[256,1024]{1,0:T(8,128)(2,1)}, u32[]{:S(2)}) copy-start(bf16[256,1024]{1,0:T(8,128)(2,1)} %refs_2_.1) | copy-start | bytes 1572868
  2.2 16.4 %collective-permute-start.3 = (bf16[128,1024]{1,0:T(8,128)(2,1)S(1)}, bf16[128,1024]{1,0:T(8,128)(2,1)S(1)}, u32[]{:S(2)}, u32[]{:S(2)}) collective-permute-start(bf16[128,1024]{1,0:T(8,128)(2,1)S(1)} %constant_dynamic-slice_fusion), channel_id=1, source_target_pairs={{0,8},{1,9},{2,10},{3,11},{4,12},{5,13},{6,14},{7,15},{8,0},{9,1},... | collective-permute-start | bytes 786440 | tf_op jit(solution)/shard_map/weight_first/ppermute | solution.py:348
  5.9 12.9 %collective-permute-start.4 = (bf16[128,1024]{1,0:T(8,128)(2,1)S(1)}, bf16[128,1024]{1,0:T(8,128)(2,1)S(1)}, u32[]{:S(2)}, u32[]{:S(2)}) collective-permute-start(bf16[128,1024]{1,0:T(8,128)(2,1)S(1)} %constant_dynamic-slice_fusion), channel_id=1, source_target_pairs={{0,4},{1,5},{2,6},{3,7},{4,0},{5,1},{6,2},{7,3},{8,12},{9,13},{10,... | collective-permute-start | bytes 786440 | tf_op jit(solution)/shard_map/weight_first/ppermute | solution.py:348
  7.4 22.9 %collective-permute-start.8 = (bf16[256,1024]{1,0:T(8,128)(2,1)}, bf16[256,1024]{1,0:T(8,128)(2,1)S(1)}, u32[]{:S(2)}, u32[]{:S(2)}) collective-permute-start(bf16[256,1024]{1,0:T(8,128)(2,1)} %refs_2_.1), channel_id=1, source_target_pairs={{0,2},{1,3},{2,0},{3,1},{4,6},{5,7},{6,4},{7,5},{8,10},{9,11},{10,... | collective-permute-start | bytes 1572872 | tf_op jit(solution)/shard_map/weight_first/ppermute | solution.py:348
  9.0 35.5 %copy-start.2 = (bf16[32,32768]{1,0:T(8,128)(2,1)S(1)}, bf16[32,32768]{1,0:T(8,128)(2,1)}, u32[]{:S(2)}) copy-start(bf16[32,32768]{1,0:T(8,128)(2,1)} %refs_5_.1) | copy-start | bytes 6291460
  18.8 14.8 %collective-permute-start.5 = (bf16[2,128,1024]{2,1,0:T(8,128)(2,1)S(1)}, bf16[2,128,1024]{2,1,0:T(8,128)(2,1)S(1)}, u32[]{:S(2)}, u32[]{:S(2)}) collective-permute-start(bf16[2,128,1024]{2,1,0:T(8,128)(2,1)S(1)} %pair_up.3), channel_id=1, source_target_pairs={{0,16},{16,0},{1,17},{17,1},{2,18},{18,2},{3,19},{19,3},{4,20},{20... | collective-permute-start | bytes 1572872 | tf_op jit(solution)/shard_map/weight_second/ppermute | solution.py:348
  20.4 14.4 %collective-permute-start.6 = (bf16[2,128,1024]{2,1,0:T(8,128)(2,1)S(1)}, bf16[2,128,1024]{2,1,0:T(8,128)(2,1)S(1)}, u32[]{:S(2)}, u32[]{:S(2)}) collective-permute-start(bf16[2,128,1024]{2,1,0:T(8,128)(2,1)S(1)} %pair_up.3), channel_id=1, source_target_pairs={{0,2},{1,3},{2,0},{3,1},{4,6},{5,7},{6,4},{7,5},{8,10},{9,11},{10,... | collective-permute-start | bytes 1572872 | tf_op jit(solution)/shard_map/weight_second/ppermute | solution.py:348
  21.9 11.7 %collective-permute-start.7 = (bf16[128,1024]{1,0:T(8,128)(2,1)S(1)}, bf16[128,1024]{1,0:T(8,128)(2,1)S(1)}, u32[]{:S(2)}, u32[]{:S(2)}) collective-permute-start(bf16[128,1024]{1,0:T(8,128)(2,1)S(1)} %collective-permute-done.3.first.refs_4_), channel_id=1, source_target_pairs={{0,4},{1,5},{2,6},{3,7},{4,0},{5,1},{6,2},{7,3},{8,12},{9,13},{10,... | collective-permute-start | bytes 786440 | tf_op jit(solution)/shard_map/weight_second/ppermute | solution.py:348
  23.3 6.4 %collective-permute-start.1 = (bf16[1,256,128]{2,1,0:T(8,128)(2,1)}, bf16[1,256,128]{2,1,0:T(8,128)(2,1)S(1)}, u32[]{:S(2)}, u32[]{:S(2)}) collective-permute-start(bf16[1,256,128]{2,1,0:T(8,128)(2,1)} %get-tuple-element.28.value), channel_id=1, source_target_pairs={{0,8},{1,9},{2,10},{3,11},{4,12},{5,13},{6,14},{7,15},{8,0},{9,1},... | collective-permute-start | bytes 196616 | tf_op jit(solution)/shard_map/query_exchange/ppermute | solution.py:348
  25.7 0.9 %copy-start.4 = (bf16[1,256,128]{2,1,0:T(8,128)(2,1)S(1)}, bf16[1,256,128]{2,1,0:T(8,128)(2,1)}, u32[]{:S(2)}) copy-start(bf16[1,256,128]{2,1,0:T(8,128)(2,1)} %get-tuple-element.28.value) | copy-start | bytes 196612
  29.7 6.5 %collective-permute-start.2 = (bf16[2,256,128]{2,1,0:T(8,128)(2,1)S(1)}, bf16[2,256,128]{2,1,0:T(8,128)(2,1)S(1)}, u32[]{:S(2)}, u32[]{:S(2)}) collective-permute-start(bf16[2,256,128]{2,1,0:T(8,128)(2,1)S(1)} %join.2.first), channel_id=1, source_target_pairs={{0,2},{1,3},{2,0},{3,1},{4,6},{5,7},{6,4},{7,5},{8,10},{9,11},{10,... | collective-permute-start | bytes 393224 | tf_op jit(solution)/shard_map/query_exchange/ppermute | solution.py:348
  30.3 1.2 %copy-start = (bf16[512,1024]{1,0:T(8,128)(2,1)S(1)}, bf16[512,1024]{1,0:T(8,128)(2,1)}, u32[]{:S(2)}) copy-start(bf16[512,1024]{1,0:T(8,128)(2,1)} %get-tuple-element.31.refs_0_) | copy-start | bytes 3145732
  33.6 16.6 %copy-start.1 = (bf16[512,1024]{1,0:T(8,128)(2,1)S(1)}, bf16[512,1024]{1,0:T(8,128)(2,1)}, u32[]{:S(2)}) copy-start(bf16[512,1024]{1,0:T(8,128)(2,1)} %get-tuple-element.31.refs_0_) | copy-start | bytes 3145732
  36.2 6.6 %collective-permute-start.9 = (bf16[4,256,128]{2,1,0:T(8,128)(2,1)S(1)}, bf16[4,256,128]{2,1,0:T(8,128)(2,1)S(1)}, u32[]{:S(2)}, u32[]{:S(2)}) collective-permute-start(bf16[4,256,128]{2,1,0:T(8,128)(2,1)S(1)} %join.3.refs_0_), channel_id=1, source_target_pairs={{0,4},{1,5},{2,6},{3,7},{4,0},{5,1},{6,2},{7,3},{8,12},{9,13},{10,... | collective-permute-start | bytes 786440 | tf_op jit(solution)/shard_map/query_exchange/ppermute | solution.py:348
  38.2 14.0 %collective-permute-start.15 = (bf16[2,128,1024]{2,1,0:T(8,128)(2,1)S(1)}, bf16[2,128,1024]{2,1,0:T(8,128)(2,1)S(1)}, u32[]{:S(2)}, u32[]{:S(2)}) collective-permute-start(bf16[2,128,1024]{2,1,0:T(8,128)(2,1)S(1)} %pair_up.4), channel_id=1, source_target_pairs={{0,16},{16,0},{1,17},{17,1},{2,18},{18,2},{3,19},{19,3},{4,20},{20... | collective-permute-start | bytes 1572872 | tf_op jit(solution)/shard_map/weight_third/ppermute | solution.py:348
  38.9 13.4 %collective-permute-start.16 = (bf16[2,128,1024]{2,1,0:T(8,128)(2,1)S(1)}, bf16[2,128,1024]{2,1,0:T(8,128)(2,1)S(1)}, u32[]{:S(2)}, u32[]{:S(2)}) collective-permute-start(bf16[2,128,1024]{2,1,0:T(8,128)(2,1)S(1)} %pair_up.5), channel_id=1, source_target_pairs={{0,2},{1,3},{2,0},{3,1},{4,6},{5,7},{6,4},{7,5},{8,10},{9,11},{10,... | collective-permute-start | bytes 1572872 | tf_op jit(solution)/shard_map/weight_third/ppermute | solution.py:348
  40.2 3.2 %collective-permute-start.10 = (bf16[4,256,128]{2,1,0:T(8,128)(2,1)S(1)}, bf16[4,256,128]{2,1,0:T(8,128)(2,1)S(1)}, u32[]{:S(2)}, u32[]{:S(2)}) collective-permute-start(bf16[4,256,128]{2,1,0:T(8,128)(2,1)S(1)} %join.3.refs_0_), channel_id=1, source_target_pairs={{0,1},{1,0},{2,3},{3,2},{4,5},{5,4},{6,7},{7,6},{8,9},{9,8},{10,11... | collective-permute-start | bytes 786440 | tf_op jit(solution)/shard_map/query_exchange/ppermute | solution.py:348
  42.9 1.4 %collective-permute-start.11 = (bf16[2,256,128]{2,1,0:T(8,128)(2,1)S(1)}, bf16[2,256,128]{2,1,0:T(8,128)(2,1)S(1)}, u32[]{:S(2)}, u32[]{:S(2)}) collective-permute-start(bf16[2,256,128]{2,1,0:T(8,128)(2,1)S(1)} %get-tuple-element.53), channel_id=1, source_target_pairs={{0,1},{1,0},{2,3},{3,2},{4,5},{5,4},{6,7},{7,6},{8,9},{9,8},{10,11... | collective-permute-start | bytes 393224 | tf_op jit(solution)/shard_map/query_exchange/ppermute | solution.py:348
  43.0 1.5 %collective-permute-start.12 = (bf16[2,256,128]{2,1,0:T(8,128)(2,1)S(1)}, bf16[2,256,128]{2,1,0:T(8,128)(2,1)S(1)}, u32[]{:S(2)}, u32[]{:S(2)}) collective-permute-start(bf16[2,256,128]{2,1,0:T(8,128)(2,1)S(1)} %get-tuple-element.52), channel_id=1, source_target_pairs={{0,1},{1,0},{2,3},{3,2},{4,5},{5,4},{6,7},{7,6},{8,9},{9,8},{10,11... | collective-permute-start | bytes 393224 | tf_op jit(solution)/shard_map/query_exchange/ppermute | solution.py:348
  47.3 1.2 %collective-permute-start.13 = (f32[16,128]{1,0:T(8,128)S(1)}, f32[16,128]{1,0:T(8,128)S(1)}, u32[]{:S(2)}, u32[]{:S(2)}) collective-permute-start(f32[16,128]{1,0:T(8,128)S(1)} %get-tuple-element.36), channel_id=1, source_target_pairs={{0,1},{1,0},{2,3},{3,2},{4,5},{5,4},{6,7},{7,6},{8,9},{9,8},{10,11... | collective-permute-start | bytes 24584 | tf_op jit(solution)/shard_map/power/ppermute | solution.py:348
  48.5 3.7 %collective-permute-start.14 = (f32[16,128]{1,0:T(8,128)S(1)}, f32[16,128]{1,0:T(8,128)S(1)}, u32[]{:S(2)}, u32[]{:S(2)}) collective-permute-start(f32[16,128]{1,0:T(8,128)S(1)} %add.16), channel_id=1, source_target_pairs={{0,2},{1,3},{2,0},{3,1},{4,6},{5,7},{6,4},{7,5},{8,10},{9,11},{10,... | collective-permute-start | bytes 24584 | tf_op jit(solution)/shard_map/power/ppermute | solution.py:348
  53.4 12.2 %collective-permute-start.22 = (bf16[3,512,256]{2,1,0:T(8,128)(2,1)S(1)}, bf16[3,512,256]{2,1,0:T(8,128)(2,1)S(1)}, u32[]{:S(2)}, u32[]{:S(2)}) collective-permute-start(bf16[3,512,256]{2,1,0:T(8,128)(2,1)S(1)} %columns_2.3), channel_id=1, source_target_pairs={{0,1},{1,0},{2,3},{3,2},{4,5},{5,4},{6,7},{7,6},{8,9},{9,8},{10,11... | collective-permute-start | bytes 2359304 | tf_op jit(solution)/shard_map/power/input_grad/ppermute | solution.py:348
  53.6 9.9 %collective-permute-start.19 = (bf16[128,1024]{1,0:T(8,128)(2,1)S(1)}, bf16[128,1024]{1,0:T(8,128)(2,1)S(1)}, u32[]{:S(2)}, u32[]{:S(2)}) collective-permute-start(bf16[128,1024]{1,0:T(8,128)(2,1)S(1)} %slice_bitcast_fusion), channel_id=1, source_target_pairs={{0,16},{16,0},{1,17},{17,1},{2,18},{18,2},{3,19},{19,3},{4,20},{20... | collective-permute-start | bytes 786440 | tf_op jit(solution)/shard_map/power/ppermute | solution.py:348
  54.5 10.9 %collective-permute-start.20 = (bf16[2,512,256]{2,1,0:T(8,128)(2,1)S(1)}, bf16[2,512,256]{2,1,0:T(8,128)(2,1)S(1)}, u32[]{:S(2)}, u32[]{:S(2)}) collective-permute-start(bf16[2,512,256]{2,1,0:T(8,128)(2,1)S(1)} %get-tuple-element.48), channel_id=1, source_target_pairs={{0,1},{1,0},{2,3},{3,2},{4,5},{5,4},{6,7},{7,6},{8,9},{9,8},{10,11... | collective-permute-start | bytes 1572872 | tf_op jit(solution)/shard_map/input_grad/ppermute | solution.py:348
  54.7 10.7 %collective-permute-start.21 = (bf16[2,512,256]{2,1,0:T(8,128)(2,1)S(1)}, bf16[2,512,256]{2,1,0:T(8,128)(2,1)S(1)}, u32[]{:S(2)}, u32[]{:S(2)}) collective-permute-start(bf16[2,512,256]{2,1,0:T(8,128)(2,1)S(1)} %get-tuple-element.49), channel_id=1, source_target_pairs={{0,1},{1,0},{2,3},{3,2},{4,5},{5,4},{6,7},{7,6},{8,9},{9,8},{10,11... | collective-permute-start | bytes 1572872 | tf_op jit(solution)/shard_map/input_grad/ppermute | solution.py:348
  55.0 3.7 %collective-permute-start.17 = (f32[16,128]{1,0:T(8,128)S(1)}, f32[16,128]{1,0:T(8,128)S(1)}, u32[]{:S(2)}, u32[]{:S(2)}) collective-permute-start(f32[16,128]{1,0:T(8,128)S(1)} %add.17), channel_id=1, source_target_pairs={{0,4},{1,5},{2,6},{3,7},{4,0},{5,1},{6,2},{7,3},{8,12},{9,13},{10,... | collective-permute-start | bytes 24584 | tf_op jit(solution)/shard_map/power/ppermute | solution.py:348
  58.6 4.8 %collective-permute-start.18 = (f32[16,128]{1,0:T(8,128)S(1)}, f32[16,128]{1,0:T(8,128)S(1)}, u32[]{:S(2)}, u32[]{:S(2)}) collective-permute-start(f32[16,128]{1,0:T(8,128)S(1)} %add.18), channel_id=1, source_target_pairs={{0,8},{1,9},{2,10},{3,11},{4,12},{5,13},{6,14},{7,15},{8,0},{9,1},... | collective-permute-start | bytes 24584 | tf_op jit(solution)/shard_map/power/ppermute | solution.py:348
  64.0 1.6 %copy-start.5 = (s32[1,512]{1,0:T(1,128)S(1)}, s32[1,512]{1,0:T(1,128)}, u32[]{:S(2)}) copy-start(s32[1,512]{1,0:T(1,128)} %ids.3) | copy-start | bytes 6148
  64.0 1.6 %collective-permute-start.23 = (bf16[1,512,256]{2,1,0:T(8,128)(2,1)S(1)}, bf16[1,512,256]{2,1,0:T(8,128)(2,1)S(1)}, u32[]{:S(2)}, u32[]{:S(2)}) collective-permute-start(bf16[1,512,256]{2,1,0:T(8,128)(2,1)S(1)} %columns_3.2), channel_id=1, source_target_pairs={{0,1},{1,0},{2,3},{3,2},{4,5},{5,4},{6,7},{7,6},{8,9},{9,8},{10,11... | collective-permute-start | bytes 786440 | tf_op jit(solution)/shard_map/input_grad/ppermute | solution.py:348
